TPU v7x, 32 devices: a whole 2x2x4 slice. The times are simulated.
32 devices in a mesh: blk: 8 (over z, x), hist: 4 (over y, core).
Axes of the slice: x: 2, y: 2, z: 4, core: 2. Of those that a mesh axis runs over, the one named last changes fastest.
Arguments:
- hidden: bfloat16 [8192, 512], P(('blk', 'hist')), may hold values from -6 to 6
- initial: bfloat16 [8192, 512], P(('blk', 'hist')), may hold values from -6 to 6
- own_adj: bfloat16 [8192, 256], P(('blk', 'hist')), may hold values from -0.21875 to 0.21875
- tiles: bfloat16 [128, 64, 64], P(('blk', 'hist')), may hold values from -0.21875 to 0.21875
- tile_src: int32 [32, 4], P(('blk', 'hist')), may hold values from 0 to 31, as said below
- tile_dst: int32 [32, 4], P(('blk', 'hist')), may hold values from 0 to 3
- history: bfloat16 [32768, 512], P(('blk', 'hist')), may hold values from -6 to 6
- pull_rows: int32 [32, 4, 128], P(('blk', 'hist')), may hold values from 0 to 1023
- pull_count: int32 [32, 4], P(('blk', 'hist')), may hold values from 1 to 128, 256 in all within a row
- pull_adj: bfloat16 [8192, 512], P(('blk', 'hist')), may hold values from -0.21875 to 0.21875
- weight: bfloat16 [512, 512], replicated, may hold values from -0.25 to 0.25
- push_rows: int32 [8192], P(('blk', 'hist')), may hold values from 0 to 1023, as said below
Outputs:
- refreshed: bfloat16 [8192, 512], P(('blk', 'hist'))
- new_history: bfloat16 [32768, 512], P(('blk', 'hist'))
Inputs may be any that keep to these rules, and one draw needn't show every extreme that they name: `tile_src`: the 4 tiles of one device take their sources from 4 different other blk indices, one block each. `pull_count`: each device's counts sum to 256; slots past the count hold arbitrary rows. `push_rows`: within one blk group the rows written to each owner are all different.
All inputs are finite; a program needn't handle non-finite values.
Results may differ from a plain program's by a relative error of at most 0.005.
Values may be sent and summed in bfloat16 or wider, within the bound.
No kernel may reach another device: no remote copies, remote signals or barrier semaphores. Data moves between devices by JAX's collectives and lax.ppermute only.
A program may use at most 64 MiB of HBM per device.

v0:
```python
import jax
import jax.numpy as jnp
from jax import lax
from jax.sharding import PartitionSpec as P

alpha_init = 0.1
beta_map = 0.4


def local(
    hidden,
    initial,
    own_adj,
    tiles,
    tile_src,
    tile_dst,
    history,
    pull_rows,
    pull_count,
    pull_adj,
    weight,
    push_rows,
):
    rows_dev, feature = hidden.shape
    block_rows = tiles.shape[1]
    per_dev = rows_dev // block_rows
    n_blk = lax.axis_size("blk")
    n_hist = lax.axis_size("hist")
    sources = tile_src[0]
    targets = tile_dst[0]
    dst_onehot = (targets[:, None] == jnp.arange(per_dev, dtype=jnp.int32)[None, :]).astype(
        jnp.float32
    )
    tiles_f = tiles.astype(jnp.float32)
    requested = lax.all_to_all(pull_rows[0], "hist", split_axis=0, concat_axis=0, tiled=True)
    fetched = jnp.take(history, requested.reshape(-1), axis=0).reshape(requested.shape + (feature,))
    arrived = lax.all_to_all(fetched, "hist", split_axis=0, concat_axis=0, tiled=True)
    slots = arrived.shape[1]
    filled = jnp.arange(slots, dtype=jnp.int32)[None, :] < pull_count[0][:, None]
    arrived = jnp.where(filled[:, :, None], arrived, jnp.zeros_like(arrived)).reshape(
        n_hist * slots, feature
    )
    outside = jnp.dot(pull_adj, arrived, preferred_element_type=jnp.float32)
    inside = jnp.dot(own_adj, hidden, preferred_element_type=jnp.float32)
    peers = sources // per_dev
    local_block = sources % per_dev
    peer_match = peers[:, None] == jnp.arange(n_blk, dtype=jnp.int32)[None, :]
    wanted = jnp.sum(jnp.where(peer_match, local_block[:, None], 0), axis=0)
    own_blocks = hidden.reshape(per_dev, block_rows, feature)
    requested = lax.all_to_all(wanted[:, None], "blk", split_axis=0, concat_axis=0, tiled=True)
    picked = jnp.take(own_blocks, requested.reshape(-1), axis=0).reshape(
        requested.shape + (block_rows, feature)
    )
    received = lax.all_to_all(picked, "blk", split_axis=0, concat_axis=0, tiled=True)
    received = received.reshape(n_blk * block_rows, feature)
    placed = jnp.einsum("kd,kp,kqr->dqpr", dst_onehot, peer_match.astype(jnp.float32), tiles_f)
    placed = placed.astype(jnp.bfloat16).reshape(rows_dev, n_blk * block_rows)
    remote = jnp.dot(placed, received, preferred_element_type=jnp.float32)
    aggregate = inside + remote + outside
    support = ((1.0 - alpha_init) * aggregate + alpha_init * initial.astype(jnp.float32)).astype(
        jnp.bfloat16
    )
    projected = jnp.dot(support, weight, preferred_element_type=jnp.float32)
    refreshed = jax.nn.relu(
        (1.0 - beta_map) * support.astype(jnp.float32) + beta_map * projected
    ).astype(jnp.bfloat16)
    per_owner = rows_dev // n_hist
    pushed_rows, pushed_index = (
        lax.all_to_all(
            refreshed.reshape(n_hist, per_owner, feature),
            "hist",
            split_axis=0,
            concat_axis=0,
            tiled=True,
        ),
        lax.all_to_all(
            push_rows.reshape(n_hist, per_owner), "hist", split_axis=0, concat_axis=0, tiled=True
        ),
    )
    new_history = history.at[pushed_index.reshape(-1)].set(pushed_rows.reshape(-1, feature))
    return (refreshed, new_history)


def solution(mesh):
    return jax.shard_map(
        local,
        mesh=mesh,
        in_specs=(
            P(("blk", "hist"), None),
            P(("blk", "hist"), None),
            P(("blk", "hist"), None),
            P(("blk", "hist"), None, None),
            P(("blk", "hist"), None),
            P(("blk", "hist"), None),
            P(("blk", "hist"), None),
            P(("blk", "hist"), None, None),
            P(("blk", "hist"), None),
            P(("blk", "hist"), None),
            P(),
            P(("blk", "hist")),
        ),
        out_specs=(P(("blk", "hist"), None), P(("blk", "hist"), None)),
        check_vma=False,
    )
```

profile of v0, /device:TPU:0, one launch (start us, length us, event | category | flops | bytes accessed | tf_op | source)
XLA Modules:
  0.0 75.2 jit_solution(5832639511634923161)
XLA Ops:
  0.6 0.0 copy-start
  0.6 0.0 copy-start.10
  0.7 0.0 copy-start.2
  0.7 1.3 %copy.26 = bf16[1024,512]{1,0:T(8,128)(2,1)S(1)} copy(bf16[1024,512]{1,0:T(8,128)(2,1)} %param.18) | data formatting | bytes 2097152
  2.0 0.0 copy-done.10
  2.0 0.1 select_reduce_fusion
  2.1 0.7 copy.18
  2.7 7.3 %all-to-all-start = ((s32[8,1,1]{2,1,0:T(1,128)}), s32[8,1,1]{2,1,0:T(1,128)S(1)}, u32[]{:S(2)}, u32[]{:S(2)}) async-start(s32[8,1,1]{2,1,0:T(1,128)} %copy.18), calls=%async_computation | async-start | bytes 8192 | tf_op jit(solution)/shard_map/all_to_all | solution.py:50
  10.0 0.1 fusion.14
  10.1 0.0 copy-start.9
  10.1 0.7 copy-done.9
  10.7 0.0 copy-start.8
  10.7 0.7 copy-done.8
  11.4 0.7 all_to_all.39
  12.1 4.3 %all-to-all-done = s32[8,1,1]{2,1,0:T(1,128)S(1)} async-done(((s32[8,1,1]{2,1,0:T(1,128)}), s32[8,1,1]{2,1,0:T(1,128)S(1)}, u32[]{:S(2)}, u32[]{:S(2)}) %all-to-all-start) | async-done | bytes 64 | tf_op jit(solution)/shard_map/all_to_all | solution.py:50
  16.4 3.2 %all-to-all-start.2 = ((s32[4,1,128]{2,1,0:T(1,128)}), s32[4,1,128]{2,1,0:T(1,128)S(1)}, u32[]{:S(2)}, u32[]{:S(2)}) async-start(s32[4,1,128]{2,1,0:T(1,128)} %bitcast.12), calls=%async_computation.2 | async-start | bytes 4096 | tf_op jit(solution)/shard_map/all_to_all | solution.py:35
  19.6 0.2 reduce
  19.9 0.0 copy-done.2
  19.9 0.6 gather_fusion
  20.5 2.8 %all-to-all-done.2 = s32[4,1,128]{2,1,0:T(1,128)S(1)} async-done(((s32[4,1,128]{2,1,0:T(1,128)}), s32[4,1,128]{2,1,0:T(1,128)S(1)}, u32[]{:S(2)}, u32[]{:S(2)}) %all-to-all-start.2) | async-done | bytes 2080 | tf_op jit(solution)/shard_map/all_to_all | solution.py:35
  23.3 3.2 %all-to-all-start.4 = ((s32[4,1,64]{2,1,0:T(1,128)}), s32[4,1,64]{2,1,0:T(1,128)S(1)}, u32[]{:S(2)}, u32[]{:S(2)}) async-start(s32[4,1,64]{2,1,0:T(1,128)} %all_to_all.39), calls=%async_computation.4 | async-start | bytes 4096 | tf_op jit(solution)/shard_map/all_to_all | solution.py:76
  26.5 2.0 %gather_fusion.1 = bf16[512,512]{1,0:T(8,128)(2,1)S(1)} fusion(bf16[1024,512]{1,0:T(8,128)(2,1)S(1)} %copy.26, s32[1024]{0:T(1024)S(1)} %pad_clamp_fusion), kind=kCustom, calls=%fused_computation.1 | custom fusion | bytes 1050624 | tf_op jit(solution)/shard_map/jit(_take)/gather | solution.py:36
  28.5 0.9 %broadcast_select_fusion = bf16[4,128,512]{2,1,0:T(8,128)(2,1)} fusion(bf16[4,128,512]{2,1,0:T(8,128)(2,1)S(1)} %bitcast.59, pred[4,128]{1,0:T(4,128)(4,1)S(1)} %compare_and_fusion), kind=kLoop, calls=%fused_computation.16 | loop fusion | flops 262144 | bytes 1049088 | tf_op jit(solution)/shard_map/jit(_take)/select_n | solution.py:36
  29.4 0.8 %all-to-all-done.4 = s32[4,1,64]{2,1,0:T(1,128)S(1)} async-done(((s32[4,1,64]{2,1,0:T(1,128)}), s32[4,1,64]{2,1,0:T(1,128)S(1)}, u32[]{:S(2)}, u32[]{:S(2)}) %all-to-all-start.4) | async-done | bytes 1056 | tf_op jit(solution)/shard_map/all_to_all | solution.py:76
  30.2 3.5 %all-to-all-start.3 = ((bf16[4,128,512]{2,1,0:T(8,128)(2,1)}), bf16[4,128,512]{2,1,0:T(8,128)(2,1)S(1)}, u32[]{:S(2)}, u32[]{:S(2)}) async-start(bf16[4,128,512]{2,1,0:T(8,128)(2,1)} %broadcast_select_fusion), calls=%async_computation.3 | async-start | bytes 1048576 | tf_op jit(solution)/shard_map/all_to_all | solution.py:37
  33.7 0.9 %bitcast_select_fusion = bf16[8,1,64,512]{3,2,1,0:T(8,128)(2,1)} fusion(bf16[8,64,512]{2,1,0:T(8,128)(2,1)S(1)} %gather_fusion, pred[8]{0:T(512)(128)(4,1)S(1)} %compare_and_fusion.1), kind=kLoop, calls=%fused_computation.15 | loop fusion | flops 262144 | bytes 1048584 | tf_op jit(solution)/shard_map/jit(_take)/select_n | solution.py:51
  34.6 0.0 copy-start.7
  34.6 7.9 %all-to-all-done.3 = bf16[4,128,512]{2,1,0:T(8,128)(2,1)S(1)} async-done(((bf16[4,128,512]{2,1,0:T(8,128)(2,1)}), bf16[4,128,512]{2,1,0:T(8,128)(2,1)S(1)}, u32[]{:S(2)}, u32[]{:S(2)}) %all-to-all-start.3) | async-done | bytes 524320 | tf_op jit(solution)/shard_map/all_to_all | solution.py:37
  42.5 3.5 %all-to-all-start.1 = ((bf16[8,1,64,512]{3,2,1,0:T(8,128)(2,1)}), bf16[8,1,64,512]{3,2,1,0:T(8,128)(2,1)S(1)}, u32[]{:S(2)}, u32[]{:S(2)}) async-start(bf16[8,1,64,512]{3,2,1,0:T(8,128)(2,1)} %bitcast_select_fusion), calls=%async_computation.1 | async-start | bytes 1048576 | tf_op jit(solution)/shard_map/all_to_all | solution.py:54
  46.0 0.0 copy-done.7
  46.0 0.4 fusion
  46.4 1.0 %reshape.227 = bf16[256,512]{1,0:T(8,128)(2,1)} reshape(bf16[4,64,8,64]{3,2,1,0:T(8,128)(2,1)S(1)} %fusion) | data formatting | bytes 524288 | tf_op jit(solution)/shard_map/reshape | solution.py:57
  47.4 0.0 copy-start.11
  47.4 0.7 copy-done.11
  48.1 0.1 iota_compare_fusion
  48.2 0.5 broadcast.191
  48.7 0.7 reduce.5
  49.3 0.1 reshape.233
  49.4 0.0 copy-start.4
  49.4 0.1 broadcast_select_fusion.1
  49.6 0.8 %copy-done.4 = bf16[256,512]{1,0:T(8,128)(2,1)S(1)} copy-done((bf16[256,512]{1,0:T(8,128)(2,1)S(1)}, bf16[256,512]{1,0:T(8,128)(2,1)}, u32[]{:S(2)}) %copy-start.4) | copy-done | bytes 262168
  50.4 0.0 copy-start.3
  50.4 0.3 convolution_bitcast_fusion
  50.7 9.8 %all-to-all-done.1 = bf16[8,1,64,512]{3,2,1,0:T(8,128)(2,1)S(1)} async-done(((bf16[8,1,64,512]{3,2,1,0:T(8,128)(2,1)}), bf16[8,1,64,512]{3,2,1,0:T(8,128)(2,1)S(1)}, u32[]{:S(2)}, u32[]{:S(2)}) %all-to-all-start.1) | async-done | bytes 524320 | tf_op jit(solution)/shard_map/all_to_all | solution.py:54
  60.5 0.0 copy-done.3
  60.5 0.0 copy-start.5
  60.5 0.0 copy-start.6
  60.5 0.3 fusion.17
  60.8 0.6 copy-done.5
  61.4 0.0 copy-done.6
  61.5 0.3 fusion.7
  61.7 0.0 copy-done
  61.7 1.0 %fusion.6 = bf16[256,512]{1,0:T(8,128)(2,1)} fusion(bf16[256,512]{1,0:T(8,128)(2,1)S(1)} %fusion.7, bf16[512,512]{1,0:T(8,128)(2,1)S(1)} %copy-done), kind=kOutput, calls=%fused_computation.13 | convolution fusion | flops 135004160 | bytes 1048576 | tf_op jit(solution)/shard_map/dot_general | solution.py:63
  62.7 3.4 %all-to-all-start.5 = ((bf16[4,64,512]{2,1,0:T(8,128)(2,1)}), bf16[4,64,512]{2,1,0:T(8,128)(2,1)S(1)}, u32[]{:S(2)}, u32[]{:S(2)}) async-start(bf16[4,64,512]{2,1,0:T(8,128)(2,1)} %bitcast.20), calls=%async_computation.5 | async-start | bytes 524288 | tf_op jit(solution)/shard_map/all_to_all | solution.py:69
  66.2 6.0 %all-to-all-done.5 = bf16[4,64,512]{2,1,0:T(8,128)(2,1)S(1)} async-done(((bf16[4,64,512]{2,1,0:T(8,128)(2,1)}), bf16[4,64,512]{2,1,0:T(8,128)(2,1)S(1)}, u32[]{:S(2)}, u32[]{:S(2)}) %all-to-all-start.5) | async-done | bytes 262176 | tf_op jit(solution)/shard_map/all_to_all | solution.py:69
  72.2 2.1 %scatter_fusion = bf16[1024,512]{1,0:T(8,128)(2,1)S(1)} fusion(bf16[1024,512]{1,0:T(8,128)(2,1)S(1)} %copy.26, s32[256]{0:T(256)S(1)} %bitcast.65, bf16[256,512]{1,0:T(8,128)(2,1)S(1)} %bitcast.62), kind=kCustom, calls=%fused_computation.2 | custom fusion | bytes 787456 | tf_op jit(solution)/shard_map/scatter | solution.py:80
  74.3 0.0 copy-start.1
  74.3 1.0 %copy-done.1 = bf16[1024,512]{1,0:T(8,128)(2,1)} copy-done((bf16[1024,512]{1,0:T(8,128)(2,1)}, bf16[1024,512]{1,0:T(8,128)(2,1)S(1)}, u32[]{:S(2)}) %copy-start.1) | copy-done | bytes 1048600
  (9 shorter events, 0.1 us)
Async XLA Ops:
  0.6 61.1 %copy-start = (bf16[512,512]{1,0:T(8,128)(2,1)S(1)}, bf16[512,512]{1,0:T(8,128)(2,1)}, u32[]{:S(2)}) copy-start(bf16[512,512]{1,0:T(8,128)(2,1)} %param.22) | copy-start | bytes 1572868
  0.6 1.3 %copy-start.10 = (s32[1,4]{1,0:T(1,128)S(1)}, s32[1,4]{1,0:T(1,128)}, u32[]{:S(2)}) copy-start(s32[1,4]{1,0:T(1,128)} %param.16) | copy-start | bytes 52
  0.7 19.2 %copy-start.2 = (bf16[256,512]{1,0:T(8,128)(2,1)S(1)}, bf16[256,512]{1,0:T(8,128)(2,1)}, u32[]{:S(2)}) copy-start(bf16[256,512]{1,0:T(8,128)(2,1)} %param.12) | copy-start | bytes 786436
  2.7 13.6 %all-to-all-start = ((s32[8,1,1]{2,1,0:T(1,128)}), s32[8,1,1]{2,1,0:T(1,128)S(1)}, u32[]{:S(2)}, u32[]{:S(2)}) async-start(s32[8,1,1]{2,1,0:T(1,128)} %copy.18), calls=%async_computation | async-start | bytes 8192 | tf_op jit(solution)/shard_map/all_to_all | solution.py:50
  10.1 0.7 copy-start.9
  10.7 0.7 copy-start.8
  16.4 6.9 %all-to-all-start.2 = ((s32[4,1,128]{2,1,0:T(1,128)}), s32[4,1,128]{2,1,0:T(1,128)S(1)}, u32[]{:S(2)}, u32[]{:S(2)}) async-start(s32[4,1,128]{2,1,0:T(1,128)} %bitcast.12), calls=%async_computation.2 | async-start | bytes 4096 | tf_op jit(solution)/shard_map/all_to_all | solution.py:35
  23.3 6.9 %all-to-all-start.4 = ((s32[4,1,64]{2,1,0:T(1,128)}), s32[4,1,64]{2,1,0:T(1,128)S(1)}, u32[]{:S(2)}, u32[]{:S(2)}) async-start(s32[4,1,64]{2,1,0:T(1,128)} %all_to_all.39), calls=%async_computation.4 | async-start | bytes 4096 | tf_op jit(solution)/shard_map/all_to_all | solution.py:76
  30.2 12.3 %all-to-all-start.3 = ((bf16[4,128,512]{2,1,0:T(8,128)(2,1)}), bf16[4,128,512]{2,1,0:T(8,128)(2,1)S(1)}, u32[]{:S(2)}, u32[]{:S(2)}) async-start(bf16[4,128,512]{2,1,0:T(8,128)(2,1)} %broadcast_select_fusion), calls=%async_computation.3 | async-start | bytes 1048576 | tf_op jit(solution)/shard_map/all_to_all | solution.py:37
  34.6 11.4 %copy-start.7 = (bf16[4,64,64]{2,1,0:T(8,128)(2,1)S(1)}, bf16[4,64,64]{2,1,0:T(8,128)(2,1)}, u32[]{:S(2)}) copy-start(bf16[4,64,64]{2,1,0:T(8,128)(2,1)} %param.15) | copy-start | bytes 98308
  42.5 18.0 %all-to-all-start.1 = ((bf16[8,1,64,512]{3,2,1,0:T(8,128)(2,1)}), bf16[8,1,64,512]{3,2,1,0:T(8,128)(2,1)S(1)}, u32[]{:S(2)}, u32[]{:S(2)}) async-start(bf16[8,1,64,512]{3,2,1,0:T(8,128)(2,1)} %bitcast_select_fusion), calls=%async_computation.1 | async-start | bytes 1048576 | tf_op jit(solution)/shard_map/all_to_all | solution.py:54
  47.4 0.7 copy-start.11
  49.4 1.0 %copy-start.4 = (bf16[256,512]{1,0:T(8,128)(2,1)S(1)}, bf16[256,512]{1,0:T(8,128)(2,1)}, u32[]{:S(2)}) copy-start(bf16[256,512]{1,0:T(8,128)(2,1)} %param.21) | copy-start | bytes 786436
  50.4 10.1 %copy-start.3 = (bf16[256,512]{1,0:T(8,128)(2,1)S(1)}, bf16[256,512]{1,0:T(8,128)(2,1)}, u32[]{:S(2)}) copy-start(bf16[256,512]{1,0:T(8,128)(2,1)} %reshape.227) | copy-start | bytes 786436
  60.5 1.0 %copy-start.5 = (bf16[256,512]{1,0:T(8,128)(2,1)S(1)}, bf16[256,512]{1,0:T(8,128)(2,1)}, u32[]{:S(2)}) copy-start(bf16[256,512]{1,0:T(8,128)(2,1)} %param.13) | copy-start | bytes 786436
  60.5 1.0 %copy-start.6 = (bf16[256,256]{1,0:T(8,128)(2,1)S(1)}, bf16[256,256]{1,0:T(8,128)(2,1)}, u32[]{:S(2)}) copy-start(bf16[256,256]{1,0:T(8,128)(2,1)} %param.14) | copy-start | bytes 393220
  62.7 9.4 %all-to-all-start.5 = ((bf16[4,64,512]{2,1,0:T(8,128)(2,1)}), bf16[4,64,512]{2,1,0:T(8,128)(2,1)S(1)}, u32[]{:S(2)}, u32[]{:S(2)}) async-start(bf16[4,64,512]{2,1,0:T(8,128)(2,1)} %bitcast.20), calls=%async_computation.5 | async-start | bytes 524288 | tf_op jit(solution)/shard_map/all_to_all | solution.py:69
  74.3 1.0 %copy-start.1 = (bf16[1024,512]{1,0:T(8,128)(2,1)}, bf16[1024,512]{1,0:T(8,128)(2,1)S(1)}, u32[]{:S(2)}) copy-start(bf16[1024,512]{1,0:T(8,128)(2,1)S(1)} %scatter_fusion) | copy-start | bytes 3145732
where the time goes:
time: 75.8 us; the launch traced here: 75.2 us
  waiting for transfers between devices  31.5 us (42%)
  starting transfers between devices  24 us (32%)
  local copies, waits for them, and re-layouts  13.3 us (18%)
  other arithmetic  3.16 us (4%)
  matrix products  2.28 us (3%)
  between operations  0.85 us (1%)
    all_to_all x1, waiting for transfers between devices, local(): lax.all_to_all(picked, 'blk', split_axis=0, concat_axis=0, tiled=True)  9.79 us
    all_to_all x1, waiting for transfers between devices, local(): lax.all_to_all(fetched, 'hist', split_axis=0, concat_axis=0, tiled=True)  7.89 us
    all_to_all x1, starting transfers between devices, local(): lax.all_to_all(wanted[:, None], 'blk', split_axis=0, concat_axis=0, tiled...  7.25 us
    all_to_all x1, waiting for transfers between devices, local(): lax.all_to_all(refreshed.reshape(n_hist, per_owner, feature), 'hist', spl...  5.99 us
    unnamed x25, local copies, waits for them, and re-layouts  5.76 us
    all_to_all x1, waiting for transfers between devices, local(): lax.all_to_all(wanted[:, None], 'blk', split_axis=0, concat_axis=0, tiled...  4.33 us
    all_to_all x1, starting transfers between devices, local(): lax.all_to_all(picked, 'blk', split_axis=0, concat_axis=0, tiled=True)  3.49 us
    all_to_all x1, starting transfers between devices, local(): lax.all_to_all(fetched, 'hist', split_axis=0, concat_axis=0, tiled=True)  3.47 us
  transfers between devices with their start and end apart: 6, of which 6 were waited for; matrix products, arithmetic and copies ran while one was open for 11% of the time, Pallas kernels for 0%

commit v1 on v0

v1 whole, which is shorter than its diff:
```python
import functools

import jax
import jax.numpy as jnp
from jax import lax
from jax.experimental import pallas as pl
from jax.experimental.pallas import tpu as pltpu
from jax.sharding import PartitionSpec as P

alpha_init = 0.1
beta_map = 0.4

VMEM = pltpu.VMEM
SMEM = pltpu.SMEM
LIMIT = 24 * 1024 * 1024


def vmem():
    return pl.BlockSpec(memory_space=VMEM)


def smem():
    return pl.BlockSpec(memory_space=SMEM)


def cost(flops, size):
    return pl.CostEstimate(flops=flops, bytes_accessed=size, transcendentals=0)


def params():
    return pltpu.CompilerParams(vmem_limit_bytes=LIMIT)


def swap(x, axis, n, k):
    return lax.ppermute(x, axis, [(i, i ^ k) for i in range(n)])


def message_kernel(n_blk, n_hist, per_dev, src, count, rows, push, out):
    tiles = src.shape[1]
    cap = rows.shape[2]
    per_owner = push.shape[1] // n_hist
    rest = out.shape[2] - cap - per_owner
    lane = lax.broadcasted_iota(jnp.int32, (1, cap), 1)
    for h in range(n_hist):
        asked = jnp.where(lane < count[0, h], rows[0, h : h + 1, :], -1)
        pushed = push[:, h * per_owner : (h + 1) * per_owner]
        for b in range(n_blk):
            out[b * n_hist + h, :, :cap] = asked
            out[b * n_hist + h, :, cap : cap + per_owner] = pushed
    for b in range(n_blk):
        wanted = 0
        for k in range(tiles):
            wanted = jnp.where(src[0, k] // per_dev == b, src[0, k] % per_dev, wanted)
        for h in range(n_hist):
            out[b * n_hist + h, :, cap + per_owner :] = jnp.full((1, rest), wanted, jnp.int32)


def pick_kernel(n_blk, n_hist, at, place, asked, hidden, out):
    rows = out.shape[1]
    h = place[1]
    per_dev = hidden.shape[0] // rows
    for b in range(n_blk):
        wanted = asked[b * n_hist + h][:, at : at + 1]
        block = hidden[:rows, :]
        for j in range(1, per_dev):
            block = jnp.where(
                jnp.broadcast_to(wanted == j, block.shape), hidden[j * rows : (j + 1) * rows, :], block
            )
        out[b] = block


def pull_kernel(n_hist, cap, place, asked, history, *outs):
    b, h = place[0], place[1]
    for k in range(n_hist):
        rows = asked[b * n_hist + (h ^ k)][:, :cap]
        held = lax.broadcasted_iota(jnp.int32, (history.shape[0], cap), 0)
        hot = jnp.where(held == rows, 1.0, 0.0).astype(jnp.bfloat16)
        outs[k][...] = lax.dot_general(
            hot, history[...], (((0,), (0,)), ((), ())), preferred_element_type=jnp.float32
        ).astype(jnp.bfloat16)


def partial_kernel(n_hist, cap, place, own_adj, hidden, pull_adj, initial, *refs):
    arrived, out = refs[:n_hist], refs[n_hist]
    h = place[1]
    total = jnp.dot(own_adj[...], hidden[...], preferred_element_type=jnp.float32)
    for k in range(n_hist):
        columns = pl.ds(pl.multiple_of((h ^ k) * cap, cap), cap)
        total += jnp.dot(pull_adj[:, columns], arrived[k][...], preferred_element_type=jnp.float32)
    out[...] = (1.0 - alpha_init) * total + alpha_init * initial[...].astype(jnp.float32)


def final_kernel(n_hist, per_dev, place, src, dst, part, tiles, received, weight, refreshed, *refs):
    sent, total = refs[:n_hist], refs[n_hist]
    block = tiles.shape[1]
    h = place[1]
    total[...] = part[...]
    for k in range(tiles.shape[0]):
        product = jnp.dot(
            tiles[k], received[src[0, k] // per_dev], preferred_element_type=jnp.float32
        )
        rows = pl.ds(pl.multiple_of(dst[0, k] * block, block), block)
        total[rows, :] += (1.0 - alpha_init) * product
    support = total[...].astype(jnp.bfloat16)
    projected = jnp.dot(support, weight[...], preferred_element_type=jnp.float32)
    refreshed[...] = jnp.maximum(
        (1.0 - beta_map) * support.astype(jnp.float32) + beta_map * projected, 0.0
    ).astype(jnp.bfloat16)
    size = refreshed.shape[0] // n_hist
    for k in range(n_hist):
        sent[k][...] = refreshed[pl.ds(pl.multiple_of((h ^ k) * size, size), size), :]


def scatter_kernel(n_hist, cap, place, asked, history, *refs):
    pushed, out, index, rows = refs[:n_hist], refs[n_hist], refs[n_hist + 1], refs[n_hist + 2]
    b, h = place[0], place[1]
    size = pushed[0].shape[0]
    for k in range(n_hist):
        index[:, k * size : (k + 1) * size] = asked[b * n_hist + (h ^ k)][:, cap : cap + size]
        rows[k * size : (k + 1) * size, :] = pushed[k][...]
    held = lax.broadcasted_iota(jnp.int32, (history.shape[0], index.shape[1]), 0)
    hot = jnp.where(
        held + pl.program_id(0) * history.shape[0] == index[...], 1.0, 0.0
    )
    hit = jnp.sum(hot, axis=1, keepdims=True)
    new = jnp.dot(hot.astype(jnp.bfloat16), rows[...], preferred_element_type=jnp.float32)
    out[...] = jnp.where(hit > 0.0, new, history[...].astype(jnp.float32)).astype(jnp.bfloat16)


def local(
    hidden,
    initial,
    own_adj,
    tiles,
    tile_src,
    tile_dst,
    history,
    pull_rows,
    pull_count,
    pull_adj,
    weight,
    push_rows,
):
    rows_dev, feature = hidden.shape
    block_rows = tiles.shape[1]
    per_dev = rows_dev // block_rows
    n_blk = lax.axis_size("blk")
    n_hist = lax.axis_size("hist")
    cap = pull_rows.shape[2]
    per_owner = rows_dev // n_hist
    held = history.shape[0]
    width = cap + -(-(per_owner + 1) // 128) * 128
    place = jnp.stack([lax.axis_index("blk"), lax.axis_index("hist")]).astype(jnp.int32)

    def shape(s, dtype=jnp.bfloat16):
        return jax.ShapeDtypeStruct(s, dtype)

    message = pl.pallas_call(
        functools.partial(message_kernel, n_blk, n_hist, per_dev),
        out_shape=shape((n_blk * n_hist, 1, width), jnp.int32),
        in_specs=[smem(), smem(), vmem(), vmem()],
        out_specs=vmem(),
        compiler_params=params(),
        name="message",
    )(tile_src, pull_count, pull_rows, push_rows.reshape(1, rows_dev))
    asked = lax.all_to_all(message, ("blk", "hist"), split_axis=0, concat_axis=0, tiled=True)

    picked = pl.pallas_call(
        functools.partial(pick_kernel, n_blk, n_hist, cap + per_owner),
        out_shape=shape((n_blk, block_rows, feature)),
        in_specs=[smem(), vmem(), vmem()],
        out_specs=vmem(),
        compiler_params=params(),
        name="pick",
    )(place, asked, hidden)
    received = lax.all_to_all(picked, "blk", split_axis=0, concat_axis=0, tiled=True)

    fetched = pl.pallas_call(
        functools.partial(pull_kernel, n_hist, cap),
        out_shape=[shape((cap, feature))] * n_hist,
        in_specs=[smem(), vmem(), vmem()],
        out_specs=[vmem()] * n_hist,
        compiler_params=params(),
        cost_estimate=cost(2 * n_hist * cap * held * feature, held * feature * 4),
        name="pull",
    )(place, asked, history)
    arrived = [fetched[0]] + [swap(fetched[k], "hist", n_hist, k) for k in range(1, n_hist)]

    part = pl.pallas_call(
        functools.partial(partial_kernel, n_hist, cap),
        out_shape=shape((rows_dev, feature), jnp.float32),
        in_specs=[smem()] + [vmem()] * (4 + n_hist),
        out_specs=vmem(),
        compiler_params=params(),
        cost_estimate=cost(2 * rows_dev * feature * (rows_dev + n_hist * cap), rows_dev * feature * 12),
        name="partial",
    )(place, own_adj, hidden, pull_adj, initial, *arrived)

    refreshed, *sent = pl.pallas_call(
        functools.partial(final_kernel, n_hist, per_dev),
        out_shape=[shape((rows_dev, feature))] + [shape((per_owner, feature))] * n_hist,
        in_specs=[smem()] * 3 + [vmem()] * 4,
        out_specs=[vmem()] * (1 + n_hist),
        scratch_shapes=[VMEM((rows_dev, feature), jnp.float32)],
        compiler_params=params(),
        cost_estimate=cost(2 * rows_dev * feature * feature, rows_dev * feature * 12),
        name="final",
    )(place, tile_src, tile_dst, part, tiles, received, weight)
    pushed = [sent[0]] + [swap(sent[k], "hist", n_hist, k) for k in range(1, n_hist)]

    steps = 4
    whole = lambda s: pl.BlockSpec(s, lambda i: (0,) * len(s))
    new_history = pl.pallas_call(
        functools.partial(scatter_kernel, n_hist, cap),
        grid=(steps,),
        out_shape=shape((held, feature)),
        in_specs=[
            smem(),
            whole((n_blk * n_hist, 1, width)),
            pl.BlockSpec((held // steps, feature), lambda i: (i, 0)),
        ]
        + [whole((per_owner, feature))] * n_hist,
        out_specs=pl.BlockSpec((held // steps, feature), lambda i: (i, 0)),
        scratch_shapes=[VMEM((1, rows_dev), jnp.int32), VMEM((rows_dev, feature), jnp.bfloat16)],
        compiler_params=params(),
        name="scatter",
    )(place, asked, history, *pushed)
    return (refreshed, new_history)


def solution(mesh):
    both = P(("blk", "hist"))
    return jax.shard_map(
        local,
        mesh=mesh,
        in_specs=(both,) * 10 + (P(), both),
        out_specs=(both, both),
        check_vma=False,
    )
```

time: 75.8 us -> 49.9 us (0.66)
  local copies, waits for them, and re-layouts: 13.3 us -> 3.01 us
  waiting for transfers between devices: 31.5 us -> 21.4 us
  Pallas kernels: 0 us -> 9.7 us
  starting transfers between devices: 24 us -> 14.6 us
  other arithmetic: 3.16 us -> 0.08 us
  matrix products: 2.28 us -> 0 us
    all_to_all x5 -> x1, waiting for transfers between devices: 21.8 us -> 7.17 us  [local(): lax.all_to_all(message, ('blk', 'hist'), split_axis=0, concat_axis=0, til...]
    all_to_all x5 -> x1, starting transfers between devices: 20.6 us -> 7.3 us  [local(): lax.all_to_all(message, ('blk', 'hist'), split_axis=0, concat_axis=0, til...]
    ppermute x0 -> x6, waiting for transfers between devices: none -> 9.96 us  [swap(): return lax.ppermute(x, axis, [(i, i ^ k) for i in range(n)])]
    pallas_call x0 -> x6, Pallas kernels: none -> 9.7 us  [the longest x1 2.82 us: local(): pl.pallas_call(functools.partial(scatter_kernel, n_hist, cap), grid=(step...]
    all_to_all x1, waiting for transfers between devices: 9.79 us -> 4.28 us  [local(): lax.all_to_all(picked, 'blk', split_axis=0, concat_axis=0, tiled=True)]
    ppermute x0 -> x6, starting transfers between devices: none -> 3.79 us  [swap(): return lax.ppermute(x, axis, [(i, i ^ k) for i in range(n)])]
    unnamed x25 -> x26, local copies, waits for them, and re-layouts: 5.76 us -> 3.01 us
    gather x2 -> x0, local copies, waits for them, and re-layouts: 2.55 us -> none  [the longest x1 1.97 us: local(): jnp.take(history, requested.reshape(-1), axis=0)]
  transfers between devices with their start and end apart: 6 -> 8, of which waited for: 6 -> 6; matrix products, arithmetic and copies ran while one was open for 11% -> 0% of each run, Pallas kernels for 0% -> 5%
where the time goes in v1:
time: 49.9 us; the launch traced here: 49.6 us
  waiting for transfers between devices  21.4 us (43%)
  starting transfers between devices  14.6 us (29%)
  Pallas kernels  9.7 us (19%)
  local copies, waits for them, and re-layouts  3.01 us (6%)
  between operations  0.78 us (2%)
    ppermute x6, waiting for transfers between devices, swap(): return lax.ppermute(x, axis, [(i, i ^ k) for i in range(n)])  9.96 us
    all_to_all x1, starting transfers between devices, local(): lax.all_to_all(message, ('blk', 'hist'), split_axis=0, concat_axis=0, til...  7.3 us
    all_to_all x1, waiting for transfers between devices, local(): lax.all_to_all(message, ('blk', 'hist'), split_axis=0, concat_axis=0, til...  7.17 us
    all_to_all x1, waiting for transfers between devices, local(): lax.all_to_all(picked, 'blk', split_axis=0, concat_axis=0, tiled=True)  4.28 us
    ppermute x6, starting transfers between devices, swap(): return lax.ppermute(x, axis, [(i, i ^ k) for i in range(n)])  3.79 us
    all_to_all x1, starting transfers between devices, local(): lax.all_to_all(picked, 'blk', split_axis=0, concat_axis=0, tiled=True)  3.49 us
    unnamed x26, local copies, waits for them, and re-layouts  3.01 us
    pallas_call x1, Pallas kernels, local(): pl.pallas_call(functools.partial(scatter_kernel, n_hist, cap), grid=(step...  2.82 us
  transfers between devices with their start and end apart: 8, of which 6 were waited for; matrix products, arithmetic and copies ran while one was open for 0% of the time, Pallas kernels for 5%

profile of v1, /device:TPU:0, one launch (start us, length us, event | category | flops | bytes accessed | tf_op | source)
XLA Modules:
  0.0 49.6 jit_solution(8038541808722483434)
XLA Ops:
  0.6 0.0 copy-start.8
  0.6 0.0 copy-start.10
  0.7 0.6 %copy-done.8 = s32[1,4]{1,0:T(1,128)S(1)} copy-done((s32[1,4]{1,0:T(1,128)S(1)}, s32[1,4]{1,0:T(1,128)}, u32[]{:S(2)}) %copy-start.8) | copy-done | bytes 40
  1.3 0.0 copy-done.10
  1.3 0.0 copy-start.9
  1.3 0.7 %copy-done.9 = s32[1,4,128]{2,1,0:T(4,128)S(1)} copy-done((s32[1,4,128]{2,1,0:T(4,128)S(1)}, s32[1,4,128]{2,1,0:T(4,128)}, u32[]{:S(2)}) %copy-start.9) | copy-done | bytes 2072
  2.0 0.0 copy-start.11
  2.0 0.7 %copy-done.11 = s32[1,4]{1,0:T(1,128)S(1)} copy-done((s32[1,4]{1,0:T(1,128)S(1)}, s32[1,4]{1,0:T(1,128)}, u32[]{:S(2)}) %copy-start.11) | copy-done | bytes 40
  2.7 1.2 %message.1 = s32[32,1,256]{2,1,0:T(1,128)} custom-call(s32[1,4]{1,0:T(1,128)S(1)} %copy-done.8, s32[1,4]{1,0:T(1,128)S(1)} %copy-done.11, s32[1,4,128]{2,1,0:T(4,128)S(1)} %copy-done.9, s32[1,256]{1,0:T(1,128)S(1)} %bitcast.3), custom_call_target="tpu_custom_call" | custom-call | tf_op jit(solution)/shard_map/message/pallas_call | solution.py:158
  3.9 7.3 %all-to-all-start = ((s32[32,1,256]{2,1,0:T(1,128)}), s32[32,1,256]{2,1,0:T(1,128)S(1)}, u32[]{:S(2)}, u32[]{:S(2)}) async-start(s32[32,1,256]{2,1,0:T(1,128)} %message.1), calls=%async_computation | async-start | bytes 65536 | tf_op jit(solution)/shard_map/all_to_all | solution.py:166
  11.2 0.1 pad_add_fusion.place
  11.3 7.2 %all-to-all-done.asked = s32[32,1,256]{2,1,0:T(1,128)S(1)} async-done(((s32[32,1,256]{2,1,0:T(1,128)}), s32[32,1,256]{2,1,0:T(1,128)S(1)}, u32[]{:S(2)}, u32[]{:S(2)}) %all-to-all-start) | async-done | bytes 32800 | tf_op jit(solution)/shard_map/all_to_all | solution.py:166
  18.5 0.0 copy-start
  18.5 0.9 %copy-done = bf16[256,512]{1,0:T(8,128)(2,1)S(1)} copy-done((bf16[256,512]{1,0:T(8,128)(2,1)S(1)}, bf16[256,512]{1,0:T(8,128)(2,1)}, u32[]{:S(2)}) %copy-start) | copy-done | bytes 262168
  19.4 0.0 copy-start.2
  19.4 1.6 %pick.1 = bf16[8,64,512]{2,1,0:T(8,128)(2,1)} custom-call(s32[2]{0:T(128)S(1)} %pad_add_fusion.place, s32[32,1,256]{2,1,0:T(1,128)S(1)} %all-to-all-done.asked, bf16[256,512]{1,0:T(8,128)(2,1)S(1)} %copy-done), custom_call_target="tpu_custom_call" | custom-call | tf_op jit(solution)/shard_map/pick/pallas_call | solution.py:168
  21.0 3.5 %all-to-all-start.1 = ((bf16[8,64,512]{2,1,0:T(8,128)(2,1)}), bf16[8,64,512]{2,1,0:T(8,128)(2,1)S(1)}, u32[]{:S(2)}, u32[]{:S(2)}) async-start(bf16[8,64,512]{2,1,0:T(8,128)(2,1)} %pick.1), calls=%async_computation.1 | async-start | bytes 1048576 | tf_op jit(solution)/shard_map/all_to_all | solution.py:176
  24.5 0.0 copy-done.2
  24.5 0.0 copy-start.1
  24.5 0.0 copy-start.4
  24.5 0.0 copy-start.5
  24.5 0.0 copy-start.6
  24.5 1.3 %pull.1 = (bf16[128,512]{1,0:T(8,128)(2,1)S(1)}, bf16[128,512]{1,0:T(8,128)(2,1)S(1)}, bf16[128,512]{1,0:T(8,128)(2,1)S(1)}, bf16[128,512]{1,0:T(8,128)(2,1)S(1)}) custom-call(s32[2]{0:T(128)S(1)} %pad_add_fusion.place, s32[32,1,256]{2,1,0:T(1,128)S(1)} %all-to-all-done.asked, bf16[1024,512]{1,0:T(8,128)(2,1)S(1)} %copy-done.2), custom_call_target="tpu_custom_call" | custom-call | flops 536870912 | bytes 2097152 | tf_op jit(solution)/shard_map/pull/pallas_call | solution.py:178
  25.8 0.2 collective-permute-start
  26.0 0.5 %collective-permute-start.1 = (bf16[128,512]{1,0:T(8,128)(2,1)S(1)}, bf16[128,512]{1,0:T(8,128)(2,1)S(1)}, u32[]{:S(2)}, u32[]{:S(2)}) collective-permute-start(bf16[128,512]{1,0:T(8,128)(2,1)S(1)} %get-tuple-element.13), channel_id=1, source_target_pairs={{0,2},{1,3},{2,0},{3,1},{4,6},{5,7},{6,4},{7,5},{8,10},{9,11},{10,... | collective-permute-start | bytes 393224 | tf_op jit(solution)/shard_map/ppermute | solution.py:35
  26.5 1.2 %collective-permute-start.2 = (bf16[128,512]{1,0:T(8,128)(2,1)S(1)}, bf16[128,512]{1,0:T(8,128)(2,1)S(1)}, u32[]{:S(2)}, u32[]{:S(2)}) collective-permute-start(bf16[128,512]{1,0:T(8,128)(2,1)S(1)} %get-tuple-element.14), channel_id=1, source_target_pairs={{0,3},{1,2},{2,1},{3,0},{4,7},{5,6},{6,5},{7,4},{8,11},{9,10},{10,... | collective-permute-start | bytes 393224 | tf_op jit(solution)/shard_map/ppermute | solution.py:35
  27.7 0.0 collective-permute-done.refs_1_
  27.8 4.6 %collective-permute-done.1.refs_2_ = bf16[128,512]{1,0:T(8,128)(2,1)S(1)} collective-permute-done((bf16[128,512]{1,0:T(8,128)(2,1)S(1)}, bf16[128,512]{1,0:T(8,128)(2,1)S(1)}, u32[]{:S(2)}, u32[]{:S(2)}) %collective-permute-start.1) | collective-permute-done | bytes 131104 | tf_op jit(solution)/shard_map/ppermute | solution.py:35
  32.3 1.7 %collective-permute-done.2.refs_3_ = bf16[128,512]{1,0:T(8,128)(2,1)S(1)} collective-permute-done((bf16[128,512]{1,0:T(8,128)(2,1)S(1)}, bf16[128,512]{1,0:T(8,128)(2,1)S(1)}, u32[]{:S(2)}, u32[]{:S(2)}) %collective-permute-start.2) | collective-permute-done | bytes 131104 | tf_op jit(solution)/shard_map/ppermute | solution.py:35
  34.1 0.0 copy-done.1
  34.1 0.0 copy-done.4
  34.1 0.0 copy-done.5
  34.1 0.0 copy-done.6
  34.1 0.0 copy-start.3
  34.1 0.0 copy-start.7
  34.1 0.0 copy-start.12
  34.1 1.0 %partial.1.part = f32[256,512]{1,0:T(8,128)S(1)} custom-call(s32[2]{0:T(128)S(1)} %pad_add_fusion.place, bf16[256,256]{1,0:T(8,128)(2,1)S(1)} %copy-done.6, bf16[256,512]{1,0:T(8,128)(2,1)S(1)} %copy-done.1, bf16[256,512]{1,0:T(8,128)(2,1)S(1)} %copy-done.4, bf16[256,512]{1,0:T(8,128)(2,1)S(1)} %copy-done.5, bf16[128,512]{1,0:T(8,128)(2,1)S(1)} %get-tuple-element.11.refs_0_, ...), custom_call_target="tpu_custom_call" | custom-call | flops 201326592 | bytes 1572864 | tf_op jit(solution)/shard_map/partial/pallas_call | solution.py:189
  35.1 4.3 %all-to-all-done.1.received = bf16[8,64,512]{2,1,0:T(8,128)(2,1)S(1)} async-done(((bf16[8,64,512]{2,1,0:T(8,128)(2,1)}), bf16[8,64,512]{2,1,0:T(8,128)(2,1)S(1)}, u32[]{:S(2)}, u32[]{:S(2)}) %all-to-all-start.1) | async-done | bytes 524320 | tf_op jit(solution)/shard_map/all_to_all | solution.py:176
  39.4 0.0 copy-done.3
  39.4 0.0 copy-done.7
  39.4 0.0 copy-done.12
  39.4 1.8 %final.1 = (bf16[256,512]{1,0:T(8,128)(2,1)}, bf16[64,512]{1,0:T(8,128)(2,1)S(1)}, bf16[64,512]{1,0:T(8,128)(2,1)S(1)}, bf16[64,512]{1,0:T(8,128)(2,1)S(1)}, bf16[64,512]{1,0:T(8,128)(2,1)S(1)}) custom-call(s32[2]{0:T(128)S(1)} %pad_add_fusion.place, s32[1,4]{1,0:T(1,128)S(1)} %copy-done.8, s32[1,4]{1,0:T(1,128)S(1)} %copy-done.12, ...), custom_call_target="tpu_custom_call" | custom-call | flops 134217728 | bytes 1572864 | tf_op jit(solution)/shard_map/final/pallas_call | solution.py:199
  41.2 0.0 collective-permute-start.3
  41.2 0.5 %collective-permute-start.4 = (bf16[64,512]{1,0:T(8,128)(2,1)S(1)}, bf16[64,512]{1,0:T(8,128)(2,1)S(1)}, u32[]{:S(2)}, u32[]{:S(2)}) collective-permute-start(bf16[64,512]{1,0:T(8,128)(2,1)S(1)} %get-tuple-element.18), channel_id=1, source_target_pairs={{0,2},{1,3},{2,0},{3,1},{4,6},{5,7},{6,4},{7,5},{8,10},{9,11},{10,... | collective-permute-start | bytes 196616 | tf_op jit(solution)/shard_map/ppermute | solution.py:35
  41.7 1.4 %collective-permute-start.5 = (bf16[64,512]{1,0:T(8,128)(2,1)S(1)}, bf16[64,512]{1,0:T(8,128)(2,1)S(1)}, u32[]{:S(2)}, u32[]{:S(2)}) collective-permute-start(bf16[64,512]{1,0:T(8,128)(2,1)S(1)} %get-tuple-element.19), channel_id=1, source_target_pairs={{0,3},{1,2},{2,1},{3,0},{4,7},{5,6},{6,5},{7,4},{8,11},{9,10},{10,... | collective-permute-start | bytes 196616 | tf_op jit(solution)/shard_map/ppermute | solution.py:35
  43.1 0.0 collective-permute-done.3.refs_1_
  43.1 3.0 %collective-permute-done.4.refs_2_ = bf16[64,512]{1,0:T(8,128)(2,1)S(1)} collective-permute-done((bf16[64,512]{1,0:T(8,128)(2,1)S(1)}, bf16[64,512]{1,0:T(8,128)(2,1)S(1)}, u32[]{:S(2)}, u32[]{:S(2)}) %collective-permute-start.4) | collective-permute-done | bytes 65568 | tf_op jit(solution)/shard_map/ppermute | solution.py:35
  46.1 0.6 %collective-permute-done.5.refs_3_ = bf16[64,512]{1,0:T(8,128)(2,1)S(1)} collective-permute-done((bf16[64,512]{1,0:T(8,128)(2,1)S(1)}, bf16[64,512]{1,0:T(8,128)(2,1)S(1)}, u32[]{:S(2)}, u32[]{:S(2)}) %collective-permute-start.5) | collective-permute-done | bytes 65568 | tf_op jit(solution)/shard_map/ppermute | solution.py:35
  46.7 2.8 %scatter.1 = bf16[1024,512]{1,0:T(8,128)(2,1)} custom-call(s32[2]{0:T(128)S(1)} %pad_add_fusion.place, s32[32,1,256]{2,1,0:T(1,128)S(1)} %all-to-all-done.asked, bf16[1024,512]{1,0:T(8,128)(2,1)S(1)} %copy-done.2, bf16[64,512]{1,0:T(8,128)(2,1)S(1)} %get-tuple-element.16.refs_0_, bf16[64,512]{1,0:T(8,128)(2,1)S(1)} %collective-permute-done.3.refs_1_, ...), custom_call_target="tpu_custom_call" | custom-call | tf_op jit(solution)/shard_map/scatter/pallas_call | solution.py:213
Async XLA Ops:
  0.6 0.7 %copy-start.8 = (s32[1,4]{1,0:T(1,128)S(1)}, s32[1,4]{1,0:T(1,128)}, u32[]{:S(2)}) copy-start(s32[1,4]{1,0:T(1,128)} %src.3) | copy-start | bytes 52
  0.6 0.7 %copy-start.10 = (s32[256]{0:T(256)S(1)}, s32[256]{0:T(256)}, u32[]{:S(2)}) copy-start(s32[256]{0:T(256)} %param.23) | copy-start | bytes 3076
  1.3 0.7 %copy-start.9 = (s32[1,4,128]{2,1,0:T(4,128)S(1)}, s32[1,4,128]{2,1,0:T(4,128)}, u32[]{:S(2)}) copy-start(s32[1,4,128]{2,1,0:T(4,128)} %rows.1) | copy-start | bytes 6148
  2.0 0.7 %copy-start.11 = (s32[1,4]{1,0:T(1,128)S(1)}, s32[1,4]{1,0:T(1,128)}, u32[]{:S(2)}) copy-start(s32[1,4]{1,0:T(1,128)} %count.1) | copy-start | bytes 52
  3.9 14.6 %all-to-all-start = ((s32[32,1,256]{2,1,0:T(1,128)}), s32[32,1,256]{2,1,0:T(1,128)S(1)}, u32[]{:S(2)}, u32[]{:S(2)}) async-start(s32[32,1,256]{2,1,0:T(1,128)} %message.1), calls=%async_computation | async-start | bytes 65536 | tf_op jit(solution)/shard_map/all_to_all | solution.py:166
  18.5 1.0 %copy-start = (bf16[256,512]{1,0:T(8,128)(2,1)S(1)}, bf16[256,512]{1,0:T(8,128)(2,1)}, u32[]{:S(2)}) copy-start(bf16[256,512]{1,0:T(8,128)(2,1)} %hidden.3) | copy-start | bytes 786436
  19.4 5.1 %copy-start.2 = (bf16[1024,512]{1,0:T(8,128)(2,1)S(1)}, bf16[1024,512]{1,0:T(8,128)(2,1)}, u32[]{:S(2)}) copy-start(bf16[1024,512]{1,0:T(8,128)(2,1)} %history.3) | copy-start | bytes 3145732
  21.0 18.5 %all-to-all-start.1 = ((bf16[8,64,512]{2,1,0:T(8,128)(2,1)}), bf16[8,64,512]{2,1,0:T(8,128)(2,1)S(1)}, u32[]{:S(2)}, u32[]{:S(2)}) async-start(bf16[8,64,512]{2,1,0:T(8,128)(2,1)} %pick.1), calls=%async_computation.1 | async-start | bytes 1048576 | tf_op jit(solution)/shard_map/all_to_all | solution.py:176
  24.5 9.6 %copy-start.1 = (bf16[256,512]{1,0:T(8,128)(2,1)S(1)}, bf16[256,512]{1,0:T(8,128)(2,1)}, u32[]{:S(2)}) copy-start(bf16[256,512]{1,0:T(8,128)(2,1)} %hidden.3) | copy-start | bytes 786436
  24.5 9.6 %copy-start.4 = (bf16[256,512]{1,0:T(8,128)(2,1)S(1)}, bf16[256,512]{1,0:T(8,128)(2,1)}, u32[]{:S(2)}) copy-start(bf16[256,512]{1,0:T(8,128)(2,1)} %pull_adj.1) | copy-start | bytes 786436
  24.5 9.6 %copy-start.5 = (bf16[256,512]{1,0:T(8,128)(2,1)S(1)}, bf16[256,512]{1,0:T(8,128)(2,1)}, u32[]{:S(2)}) copy-start(bf16[256,512]{1,0:T(8,128)(2,1)} %initial.1) | copy-start | bytes 786436
  24.5 9.6 %copy-start.6 = (bf16[256,256]{1,0:T(8,128)(2,1)S(1)}, bf16[256,256]{1,0:T(8,128)(2,1)}, u32[]{:S(2)}) copy-start(bf16[256,256]{1,0:T(8,128)(2,1)} %own_adj.1) | copy-start | bytes 393220
  25.8 1.9 %collective-permute-start = (bf16[128,512]{1,0:T(8,128)(2,1)S(1)}, bf16[128,512]{1,0:T(8,128)(2,1)S(1)}, u32[]{:S(2)}, u32[]{:S(2)}) collective-permute-start(bf16[128,512]{1,0:T(8,128)(2,1)S(1)} %get-tuple-element.12), channel_id=1, source_target_pairs={{0,1},{1,0},{2,3},{3,2},{4,5},{5,4},{6,7},{7,6},{8,9},{9,8},{10,11... | collective-permute-start | bytes 393224 | tf_op jit(solution)/shard_map/ppermute | solution.py:35
  26.0 6.3 %collective-permute-start.1 = (bf16[128,512]{1,0:T(8,128)(2,1)S(1)}, bf16[128,512]{1,0:T(8,128)(2,1)S(1)}, u32[]{:S(2)}, u32[]{:S(2)}) collective-permute-start(bf16[128,512]{1,0:T(8,128)(2,1)S(1)} %get-tuple-element.13), channel_id=1, source_target_pairs={{0,2},{1,3},{2,0},{3,1},{4,6},{5,7},{6,4},{7,5},{8,10},{9,11},{10,... | collective-permute-start | bytes 393224 | tf_op jit(solution)/shard_map/ppermute | solution.py:35
  26.5 7.5 %collective-permute-start.2 = (bf16[128,512]{1,0:T(8,128)(2,1)S(1)}, bf16[128,512]{1,0:T(8,128)(2,1)S(1)}, u32[]{:S(2)}, u32[]{:S(2)}) collective-permute-start(bf16[128,512]{1,0:T(8,128)(2,1)S(1)} %get-tuple-element.14), channel_id=1, source_target_pairs={{0,3},{1,2},{2,1},{3,0},{4,7},{5,6},{6,5},{7,4},{8,11},{9,10},{10,... | collective-permute-start | bytes 393224 | tf_op jit(solution)/shard_map/ppermute | solution.py:35
  34.1 5.4 %copy-start.3 = (bf16[512,512]{1,0:T(8,128)(2,1)S(1)}, bf16[512,512]{1,0:T(8,128)(2,1)}, u32[]{:S(2)}) copy-start(bf16[512,512]{1,0:T(8,128)(2,1)} %weight.1) | copy-start | bytes 1572868
  34.1 5.4 %copy-start.7 = (bf16[4,64,64]{2,1,0:T(8,128)(2,1)S(1)}, bf16[4,64,64]{2,1,0:T(8,128)(2,1)}, u32[]{:S(2)}) copy-start(bf16[4,64,64]{2,1,0:T(8,128)(2,1)} %tiles.1) | copy-start | bytes 98308
  34.1 5.3 %copy-start.12 = (s32[1,4]{1,0:T(1,128)S(1)}, s32[1,4]{1,0:T(1,128)}, u32[]{:S(2)}) copy-start(s32[1,4]{1,0:T(1,128)} %dst.1) | copy-start | bytes 52
  41.2 1.9 %collective-permute-start.3 = (bf16[64,512]{1,0:T(8,128)(2,1)S(1)}, bf16[64,512]{1,0:T(8,128)(2,1)S(1)}, u32[]{:S(2)}, u32[]{:S(2)}) collective-permute-start(bf16[64,512]{1,0:T(8,128)(2,1)S(1)} %get-tuple-element.17), channel_id=1, source_target_pairs={{0,1},{1,0},{2,3},{3,2},{4,5},{5,4},{6,7},{7,6},{8,9},{9,8},{10,11... | collective-permute-start | bytes 196616 | tf_op jit(solution)/shard_map/ppermute | solution.py:35
  41.2 4.9 %collective-permute-start.4 = (bf16[64,512]{1,0:T(8,128)(2,1)S(1)}, bf16[64,512]{1,0:T(8,128)(2,1)S(1)}, u32[]{:S(2)}, u32[]{:S(2)}) collective-permute-start(bf16[64,512]{1,0:T(8,128)(2,1)S(1)} %get-tuple-element.18), channel_id=1, source_target_pairs={{0,2},{1,3},{2,0},{3,1},{4,6},{5,7},{6,4},{7,5},{8,10},{9,11},{10,... | collective-permute-start | bytes 196616 | tf_op jit(solution)/shard_map/ppermute | solution.py:35
  41.7 5.0 %collective-permute-start.5 = (bf16[64,512]{1,0:T(8,128)(2,1)S(1)}, bf16[64,512]{1,0:T(8,128)(2,1)S(1)}, u32[]{:S(2)}, u32[]{:S(2)}) collective-permute-start(bf16[64,512]{1,0:T(8,128)(2,1)S(1)} %get-tuple-element.19), channel_id=1, source_target_pairs={{0,3},{1,2},{2,1},{3,0},{4,7},{5,6},{6,5},{7,4},{8,11},{9,10},{10,... | collective-permute-start | bytes 196616 | tf_op jit(solution)/shard_map/ppermute | solution.py:35

commit v2 on v1

v2 whole, which is shorter than its diff:
```python
import functools

import jax
import jax.numpy as jnp
from jax import lax
from jax.experimental import pallas as pl
from jax.experimental.pallas import tpu as pltpu
from jax.sharding import PartitionSpec as P

alpha_init = 0.1
beta_map = 0.4

VMEM = pltpu.VMEM
SMEM = pltpu.SMEM
LIMIT = 24 * 1024 * 1024


def vmem():
    return pl.BlockSpec(memory_space=VMEM)


def smem():
    return pl.BlockSpec(memory_space=SMEM)


def cost(flops, size):
    return pl.CostEstimate(flops=flops, bytes_accessed=size, transcendentals=0)


def params():
    return pltpu.CompilerParams(vmem_limit_bytes=LIMIT)


def swap(x, axis, n, k):
    return lax.ppermute(x, axis, [(i, i ^ k) for i in range(n)])


def message_kernel(n_hist, n_half, per_dev, place, src, count, rows, push, *outs):
    to_hist, to_half = outs[:n_hist], outs[n_hist:]
    tiles = src.shape[1]
    cap = rows.shape[2]
    per_owner = push.shape[1] // n_hist
    b, h = place[0], place[1]
    lane = lax.broadcasted_iota(jnp.int32, (1, cap), 1)
    for k in range(n_hist):
        o = h ^ k
        to_hist[k][:, :cap] = jnp.where(lane < count[0, o], rows[0, pl.ds(o, 1), :], -1)
        pushed = push[:, :per_owner]
        for j in range(1, n_hist):
            pushed = jnp.where(o == j, push[:, j * per_owner : (j + 1) * per_owner], pushed)
        to_hist[k][:, cap : cap + per_owner] = pushed
    for k in range(n_half):
        own, other = 0, 0
        for t in range(tiles):
            far = (src[0, t] // per_dev) ^ b
            own = jnp.where(far == k, src[0, t] % per_dev, own)
            other = jnp.where(far == k + n_half, src[0, t] % per_dev, other)
        to_half[k][:, :128] = jnp.full((1, 128), own, jnp.int32)
        to_half[k][:, 128:] = jnp.full((1, 128), other, jnp.int32)


def pick_kernel(n_half, hidden, mirror, *refs):
    asked, outs = refs[:n_half], refs[n_half:]
    rows = outs[0].shape[0] // 2
    per_dev = hidden.shape[0] // rows
    for k in range(n_half):
        for slot, held in enumerate((hidden, mirror)):
            wanted = asked[k][:, slot * 128 : slot * 128 + 1]
            block = held[:rows, :]
            for j in range(1, per_dev):
                block = jnp.where(
                    jnp.broadcast_to(wanted == j, block.shape), held[j * rows : (j + 1) * rows, :], block
                )
            outs[k][slot * rows : (slot + 1) * rows, :] = block


def pull_kernel(n_hist, cap, history, *refs):
    asked, outs = refs[:n_hist], refs[n_hist:]
    held = lax.broadcasted_iota(jnp.int32, (history.shape[0], cap), 0)
    for k in range(n_hist):
        hot = jnp.where(held == asked[k][:, :cap], 1.0, 0.0).astype(jnp.bfloat16)
        outs[k][...] = lax.dot_general(
            hot, history[...], (((0,), (0,)), ((), ())), preferred_element_type=jnp.float32
        ).astype(jnp.bfloat16)


def prepare_kernel(n_hist, cap, history, *refs):
    asked, (base, hot, index) = refs[:n_hist], refs[n_hist:]
    size = index.shape[1] // n_hist
    for k in range(n_hist):
        index[:, k * size : (k + 1) * size] = asked[k][:, cap : cap + size]
    held = lax.broadcasted_iota(jnp.int32, hot.shape, 0)
    found = jnp.where(held == index[...], 1.0, 0.0)
    hot[...] = found.astype(jnp.bfloat16)
    hit = jnp.sum(found, axis=1, keepdims=True)
    base[...] = jnp.where(hit > 0.0, 0.0, history[...].astype(jnp.float32)).astype(jnp.bfloat16)


def partial_kernel(n_hist, cap, place, own_adj, hidden, pull_adj, initial, *refs):
    arrived, out = refs[:n_hist], refs[n_hist]
    h = place[1]
    total = jnp.dot(own_adj[...], hidden[...], preferred_element_type=jnp.float32)
    for k in range(n_hist):
        columns = pl.ds(pl.multiple_of((h ^ k) * cap, cap), cap)
        total += jnp.dot(pull_adj[:, columns], arrived[k][...], preferred_element_type=jnp.float32)
    out[...] = (1.0 - alpha_init) * total + alpha_init * initial[...].astype(jnp.float32)


def final_kernel(n_hist, n_half, per_dev, place, src, dst, part, tiles, weight, *refs):
    received, sent = refs[:n_half], refs[n_half : n_half + n_hist]
    total, blocks, result = refs[n_half + n_hist :]
    block = tiles.shape[1]
    b, h = place[0], place[1]
    total[...] = part[...]
    for k in range(n_half):
        blocks[k] = received[k][:block, :]
        blocks[k + n_half] = received[k][block:, :]
    for t in range(tiles.shape[0]):
        product = jnp.dot(
            tiles[t], blocks[(src[0, t] // per_dev) ^ b], preferred_element_type=jnp.float32
        )
        rows = pl.ds(pl.multiple_of(dst[0, t] * block, block), block)
        total[rows, :] += (1.0 - alpha_init) * product
    support = total[...].astype(jnp.bfloat16)
    projected = jnp.dot(support, weight[...], preferred_element_type=jnp.float32)
    result[...] = jnp.maximum(
        (1.0 - beta_map) * support.astype(jnp.float32) + beta_map * projected, 0.0
    ).astype(jnp.bfloat16)
    size = result.shape[0] // n_hist
    for k in range(n_hist):
        sent[k][...] = result[pl.ds(pl.multiple_of((h ^ k) * size, size), size), :]


def scatter_kernel(n_hist, steps, place, base, hot, *refs):
    sent, pushed = refs[:n_hist], refs[n_hist : 2 * n_hist]
    refreshed, out, rows, new, sent_sem, new_sem = refs[2 * n_hist :]
    h = place[1]
    size = sent[0].shape[0]
    copies = []
    for k in range(n_hist):
        to = refreshed.at[pl.ds(pl.multiple_of((h ^ k) * size, size), size), :]
        copies.append(pltpu.make_async_copy(sent[k], to, sent_sem.at[k]))
        copies[-1].start()
        rows[k * size : (k + 1) * size, :] = pushed[k][...]
    step = base.shape[0] // steps
    for i in range(steps):
        at = slice(i * step, (i + 1) * step)
        found = jnp.dot(hot[at, :], rows[...], preferred_element_type=jnp.float32)
        new[at, :] = (base[at, :].astype(jnp.float32) + found).astype(jnp.bfloat16)
        copies.append(pltpu.make_async_copy(new.at[at, :], out.at[at, :], new_sem.at[i]))
        copies[-1].start()
    for copy in copies:
        copy.wait()


def local(
    hidden,
    initial,
    own_adj,
    tiles,
    tile_src,
    tile_dst,
    history,
    pull_rows,
    pull_count,
    pull_adj,
    weight,
    push_rows,
):
    rows_dev, feature = hidden.shape
    block_rows = tiles.shape[1]
    per_dev = rows_dev // block_rows
    n_blk = lax.axis_size("blk")
    n_hist = lax.axis_size("hist")
    cap = pull_rows.shape[2]
    per_owner = rows_dev // n_hist
    held = history.shape[0]
    n_half = n_blk // 2
    place = jnp.stack([lax.axis_index("blk"), lax.axis_index("hist")]).astype(jnp.int32)
    anywhere = pl.BlockSpec(memory_space=pl.ANY)

    def shape(s, dtype=jnp.bfloat16):
        return jax.ShapeDtypeStruct(s, dtype)

    mirror = swap(hidden, "blk", n_blk, n_half)
    asks = pl.pallas_call(
        functools.partial(message_kernel, n_hist, n_half, per_dev),
        out_shape=[shape((1, cap + 128), jnp.int32)] * n_hist + [shape((1, 256), jnp.int32)] * n_half,
        in_specs=[smem(), smem(), smem(), vmem(), vmem()],
        out_specs=[vmem()] * (n_hist + n_half),
        compiler_params=params(),
        name="message",
    )(place, tile_src, pull_count, pull_rows, push_rows.reshape(1, rows_dev))
    asked = [asks[0]] + [swap(asks[k], "hist", n_hist, k) for k in range(1, n_hist)]
    wanted = [asks[n_hist]] + [swap(asks[n_hist + k], "blk", n_blk, k) for k in range(1, n_half)]
    asked, wanted = lax.optimization_barrier((asked, wanted))

    fetched = pl.pallas_call(
        functools.partial(pull_kernel, n_hist, cap),
        out_shape=[shape((cap, feature))] * n_hist,
        in_specs=[vmem()] * (1 + n_hist),
        out_specs=[vmem()] * n_hist,
        compiler_params=params(),
        cost_estimate=cost(2 * n_hist * cap * held * feature, held * feature * 4),
        name="pull",
    )(history, *asked)
    arrived = [fetched[0]] + [swap(fetched[k], "hist", n_hist, k) for k in range(1, n_hist)]

    picked = pl.pallas_call(
        functools.partial(pick_kernel, n_half),
        out_shape=[shape((2 * block_rows, feature))] * n_half,
        in_specs=[vmem()] * (2 + n_half),
        out_specs=[vmem()] * n_half,
        compiler_params=params(),
        cost_estimate=cost(0, n_half * 4 * block_rows * feature * 2),
        name="pick",
    )(hidden, mirror, *wanted)
    received = [picked[0]] + [swap(picked[k], "blk", n_blk, k) for k in range(1, n_half)]

    base, hot = pl.pallas_call(
        functools.partial(prepare_kernel, n_hist, cap),
        out_shape=[shape((held, feature)), shape((held, rows_dev))],
        in_specs=[vmem()] * (1 + n_hist),
        out_specs=[vmem()] * 2,
        scratch_shapes=[VMEM((1, rows_dev), jnp.int32)],
        compiler_params=params(),
        cost_estimate=cost(held * rows_dev * 8, held * feature * 6),
        name="prepare",
    )(history, *asked)

    part = pl.pallas_call(
        functools.partial(partial_kernel, n_hist, cap),
        out_shape=shape((rows_dev, feature), jnp.float32),
        in_specs=[smem()] + [vmem()] * (4 + n_hist),
        out_specs=vmem(),
        compiler_params=params(),
        cost_estimate=cost(2 * rows_dev * feature * (rows_dev + n_hist * cap), rows_dev * feature * 12),
        name="partial",
    )(place, own_adj, hidden, pull_adj, initial, *arrived)

    sent = pl.pallas_call(
        functools.partial(final_kernel, n_hist, n_half, per_dev),
        out_shape=[shape((per_owner, feature))] * n_hist,
        in_specs=[smem()] * 3 + [vmem()] * (3 + n_half),
        out_specs=[vmem()] * n_hist,
        scratch_shapes=[
            VMEM((rows_dev, feature), jnp.float32),
            VMEM((n_blk, block_rows, feature), jnp.bfloat16),
            VMEM((rows_dev, feature), jnp.bfloat16),
        ],
        compiler_params=params(),
        cost_estimate=cost(2 * rows_dev * feature * feature, rows_dev * feature * 12),
        name="final",
    )(place, tile_src, tile_dst, part, tiles, weight, *received)
    pushed = [sent[0]] + [swap(sent[k], "hist", n_hist, k) for k in range(1, n_hist)]

    steps = 4
    refreshed, new_history = pl.pallas_call(
        functools.partial(scatter_kernel, n_hist, steps),
        out_shape=[shape((rows_dev, feature)), shape((held, feature))],
        in_specs=[smem()] + [vmem()] * (2 + 2 * n_hist),
        out_specs=[anywhere] * 2,
        scratch_shapes=[
            VMEM((rows_dev, feature), jnp.bfloat16),
            VMEM((held, feature), jnp.bfloat16),
            pltpu.SemaphoreType.DMA((n_hist,)),
            pltpu.SemaphoreType.DMA((steps,)),
        ],
        compiler_params=params(),
        name="scatter",
    )(place, base, hot, *sent, *pushed)
    return (refreshed, new_history)


def solution(mesh):
    both = P(("blk", "hist"))
    return jax.shard_map(
        local,
        mesh=mesh,
        in_specs=(both,) * 10 + (P(), both),
        out_specs=(both, both),
        check_vma=False,
    )
```

time: 49.9 us -> 38.6 us (0.77)
  waiting for transfers between devices: 21.4 us -> 11.8 us
  Pallas kernels: 9.7 us -> 6.15 us
  starting transfers between devices: 14.6 us -> 17.7 us
  local copies, waits for them, and re-layouts: 3.01 us -> 1.96 us
    ppermute x6 -> x16, starting transfers between devices: 3.79 us -> 17.7 us  [swap(): return lax.ppermute(x, axis, [(i, i ^ k) for i in range(n)])]
    all_to_all x2 -> x0, waiting for transfers between devices: 11.5 us -> none  [the longest x1 7.17 us: local(): lax.all_to_all(message, ('blk', 'hist'), split_axis=0, concat_axis=0, til...]
    all_to_all x2 -> x0, starting transfers between devices: 10.8 us -> none  [the longest x1 7.3 us: local(): lax.all_to_all(message, ('blk', 'hist'), split_axis=0, concat_axis=0, til...]
    pallas_call x4 -> x5, Pallas kernels: 7.38 us -> 4.38 us  [the longest x1 1.89 us: local(): pl.pallas_call(functools.partial(scatter_kernel, n_hist, steps), out_shap...]
    ppermute x6 -> x16, waiting for transfers between devices: 9.96 us -> 11.8 us  [swap(): return lax.ppermute(x, axis, [(i, i ^ k) for i in range(n)])]
    unnamed x26, local copies, waits for them, and re-layouts: 3.01 us -> 1.96 us
    pallas_call x1, Pallas kernels: 1.29 us -> 0.74 us  [local(): pl.pallas_call(functools.partial(pull_kernel, n_hist, cap), out_shape=[sh...]
  transfers between devices with their start and end apart: 8 -> 16, of which waited for: 6 -> 7; matrix products, arithmetic and copies ran while one was open for 0% -> 0% of each run, Pallas kernels for 5% -> 8%
where the time goes in v2:
time: 38.6 us; the launch traced here: 38.4 us
  starting transfers between devices  17.7 us (46%)
  waiting for transfers between devices  11.8 us (31%)
  Pallas kernels  6.15 us (16%)
  local copies, waits for them, and re-layouts  1.96 us (5%)
  between operations  0.77 us (2%)
    ppermute x16, starting transfers between devices, swap(): return lax.ppermute(x, axis, [(i, i ^ k) for i in range(n)])  17.7 us
    ppermute x16, waiting for transfers between devices, swap(): return lax.ppermute(x, axis, [(i, i ^ k) for i in range(n)])  11.8 us
    unnamed x26, local copies, waits for them, and re-layouts  1.96 us
    pallas_call x1, Pallas kernels, local(): pl.pallas_call(functools.partial(scatter_kernel, n_hist, steps), out_shap...  1.89 us
    pallas_call x1, Pallas kernels, local(): pl.pallas_call(functools.partial(final_kernel, n_hist, n_half, per_dev),...  1.11 us
    pallas_call x1, Pallas kernels, local(): pl.pallas_call(functools.partial(partial_kernel, n_hist, cap), out_shape=...  1.03 us
    pallas_call x1, Pallas kernels, local(): pl.pallas_call(functools.partial(message_kernel, n_hist, n_half, per_dev)...  0.82 us
  transfers between devices with their start and end apart: 16, of which 7 were waited for; matrix products, arithmetic and copies ran while one was open for 0% of the time, Pallas kernels for 8%

profile of v2, /device:TPU:0, one launch (start us, length us, event | category | flops | bytes accessed | tf_op | source)
XLA Modules:
  0.0 38.4 jit_solution(18229812311178925174)
XLA Ops:
  0.6 4.1 %collective-permute-start.9 = (bf16[256,512]{1,0:T(8,128)(2,1)}, bf16[256,512]{1,0:T(8,128)(2,1)S(1)}, u32[]{:S(2)}, u32[]{:S(2)}) collective-permute-start(bf16[256,512]{1,0:T(8,128)(2,1)} %hidden.3), channel_id=1, source_target_pairs={{0,16},{4,20},{8,24},{12,28},{16,0},{20,4},{24,8},{28,12},{1,17},{... | collective-permute-start | bytes 786440 | tf_op jit(solution)/shard_map/ppermute | solution.py:35
  4.7 0.0 copy-start.12
  4.7 0.0 copy-start.9
  4.7 0.1 pad_add_fusion.place
  4.8 0.0 copy-start.8
  4.8 0.0 copy-start.10
  4.8 0.6 %copy-done.12 = s32[1,4]{1,0:T(1,128)S(1)} copy-done((s32[1,4]{1,0:T(1,128)S(1)}, s32[1,4]{1,0:T(1,128)}, u32[]{:S(2)}) %copy-start.12) | copy-done | bytes 40
  5.4 0.0 copy-done.9
  5.4 0.0 copy-done.8
  5.5 0.0 copy-done.10
  5.5 0.8 %message.1 = (s32[1,256]{1,0:T(1,128)S(1)}, s32[1,256]{1,0:T(1,128)S(1)}, s32[1,256]{1,0:T(1,128)S(1)}, s32[1,256]{1,0:T(1,128)S(1)}, s32[1,256]{1,0:T(1,128)S(1...) custom-call(s32[2]{0:T(128)S(1)} %pad_add_fusion.place, s32[1,4]{1,0:T(1,128)S(1)} %copy-done.8, ...), custom_call_target="tpu_custom_call" | custom-call | tf_op jit(solution)/shard_map/message/pallas_call | solution.py:186
  6.3 0.0 collective-permute-start
  6.4 1.6 %collective-permute-start.1 = (s32[1,256]{1,0:T(1,128)S(1)}, s32[1,256]{1,0:T(1,128)S(1)}, u32[]{:S(2)}, u32[]{:S(2)}) collective-permute-start(s32[1,256]{1,0:T(1,128)S(1)} %get-tuple-element.34), channel_id=1, source_target_pairs={{0,2},{1,3},{2,0},{3,1},{4,6},{5,7},{6,4},{7,5},{8,10},{9,11},{10,... | collective-permute-start | bytes 3080 | tf_op jit(solution)/shard_map/ppermute | solution.py:35
  7.9 0.3 collective-permute-start.2
  8.2 1.5 %collective-permute-start.3 = (s32[1,256]{1,0:T(1,128)S(1)}, s32[1,256]{1,0:T(1,128)S(1)}, u32[]{:S(2)}, u32[]{:S(2)}) collective-permute-start(s32[1,256]{1,0:T(1,128)S(1)} %get-tuple-element.37), channel_id=1, source_target_pairs={{0,4},{4,0},{8,12},{12,8},{16,20},{20,16},{24,28},{28,24},{1,5},{5... | collective-permute-start | bytes 3080 | tf_op jit(solution)/shard_map/ppermute | solution.py:35
  9.7 0.0 collective-permute-done.refs_1_
  9.7 1.6 %collective-permute-start.4 = (s32[1,256]{1,0:T(1,128)S(1)}, s32[1,256]{1,0:T(1,128)S(1)}, u32[]{:S(2)}, u32[]{:S(2)}) collective-permute-start(s32[1,256]{1,0:T(1,128)S(1)} %get-tuple-element.38), channel_id=1, source_target_pairs={{0,8},{4,12},{8,0},{12,4},{16,24},{20,28},{24,16},{28,20},{1,9},{5... | collective-permute-start | bytes 3080 | tf_op jit(solution)/shard_map/ppermute | solution.py:35
  11.3 0.0 collective-permute-done.1.refs_2_
  11.3 1.2 %collective-permute-start.5 = (s32[1,256]{1,0:T(1,128)S(1)}, s32[1,256]{1,0:T(1,128)S(1)}, u32[]{:S(2)}, u32[]{:S(2)}) collective-permute-start(s32[1,256]{1,0:T(1,128)S(1)} %get-tuple-element.39), channel_id=1, source_target_pairs={{0,12},{4,8},{8,4},{12,0},{16,28},{20,24},{24,20},{28,16},{1,13},{... | collective-permute-start | bytes 3080 | tf_op jit(solution)/shard_map/ppermute | solution.py:35
  12.5 0.0 collective-permute-done.2.refs_3_
  12.5 0.0 collective-permute-done.3.refs_1_
  12.5 0.9 %collective-permute-done.4.refs_2_ = s32[1,256]{1,0:T(1,128)S(1)} collective-permute-done((s32[1,256]{1,0:T(1,128)S(1)}, s32[1,256]{1,0:T(1,128)S(1)}, u32[]{:S(2)}, u32[]{:S(2)}) %collective-permute-start.4) | collective-permute-done | bytes 1056 | tf_op jit(solution)/shard_map/ppermute | solution.py:35
  13.4 2.4 %collective-permute-done.5.refs_3_ = s32[1,256]{1,0:T(1,128)S(1)} collective-permute-done((s32[1,256]{1,0:T(1,128)S(1)}, s32[1,256]{1,0:T(1,128)S(1)}, u32[]{:S(2)}, u32[]{:S(2)}) %collective-permute-start.5) | collective-permute-done | bytes 1056 | tf_op jit(solution)/shard_map/ppermute | solution.py:35
  15.8 0.0 copy-start.1
  15.8 1.2 %copy-done.1 = bf16[1024,512]{1,0:T(8,128)(2,1)S(1)} copy-done((bf16[1024,512]{1,0:T(8,128)(2,1)S(1)}, bf16[1024,512]{1,0:T(8,128)(2,1)}, u32[]{:S(2)}) %copy-start.1) | copy-done | bytes 1048600
  17.0 0.0 copy-start
  17.0 0.0 copy-start.6
  17.0 0.7 %pull.1 = (bf16[128,512]{1,0:T(8,128)(2,1)S(1)}, bf16[128,512]{1,0:T(8,128)(2,1)S(1)}, bf16[128,512]{1,0:T(8,128)(2,1)S(1)}, bf16[128,512]{1,0:T(8,128)(2,1)S(1)}) custom-call(bf16[1024,512]{1,0:T(8,128)(2,1)S(1)} %copy-done.1, s32[1,256]{1,0:T(1,128)S(1)} %get-tuple-element.40.refs_0_, s32[1,256]{1,0:T(1,128)S(1)} %collective-permute-done.refs_1_, ...), custom_call_target="tpu_custom_call" | custom-call | flops 536870912 | bytes 2097152 | tf_op jit(solution)/shard_map/pull/pallas_call | solution.py:198
  17.8 0.1 collective-permute-start.6
  17.9 1.6 %collective-permute-start.7 = (bf16[128,512]{1,0:T(8,128)(2,1)S(1)}, bf16[128,512]{1,0:T(8,128)(2,1)S(1)}, u32[]{:S(2)}, u32[]{:S(2)}) collective-permute-start(bf16[128,512]{1,0:T(8,128)(2,1)S(1)} %get-tuple-element.48), channel_id=1, source_target_pairs={{0,2},{1,3},{2,0},{3,1},{4,6},{5,7},{6,4},{7,5},{8,10},{9,11},{10,... | collective-permute-start | bytes 393224 | tf_op jit(solution)/shard_map/ppermute | solution.py:35
  19.4 0.3 collective-permute-start.8
  19.7 0.0 collective-permute-done.9.mirror
  19.7 0.0 copy-done
  19.7 0.2 pick.1
  19.9 0.6 %collective-permute-start.10 = (bf16[128,512]{1,0:T(8,128)(2,1)S(1)}, bf16[128,512]{1,0:T(8,128)(2,1)S(1)}, u32[]{:S(2)}, u32[]{:S(2)}) collective-permute-start(bf16[128,512]{1,0:T(8,128)(2,1)S(1)} %get-tuple-element.55), channel_id=1, source_target_pairs={{0,4},{4,0},{8,12},{12,8},{16,20},{20,16},{24,28},{28,24},{1,5},{5... | collective-permute-start | bytes 393224 | tf_op jit(solution)/shard_map/ppermute | solution.py:35
  20.5 1.2 %collective-permute-start.11 = (bf16[128,512]{1,0:T(8,128)(2,1)S(1)}, bf16[128,512]{1,0:T(8,128)(2,1)S(1)}, u32[]{:S(2)}, u32[]{:S(2)}) collective-permute-start(bf16[128,512]{1,0:T(8,128)(2,1)S(1)} %get-tuple-element.56), channel_id=1, source_target_pairs={{0,8},{4,12},{8,0},{12,4},{16,24},{20,28},{24,16},{28,20},{1,9},{5... | collective-permute-start | bytes 393224 | tf_op jit(solution)/shard_map/ppermute | solution.py:35
  21.7 0.0 collective-permute-done.6.refs_1_
  21.7 1.8 %collective-permute-start.12 = (bf16[128,512]{1,0:T(8,128)(2,1)S(1)}, bf16[128,512]{1,0:T(8,128)(2,1)S(1)}, u32[]{:S(2)}, u32[]{:S(2)}) collective-permute-start(bf16[128,512]{1,0:T(8,128)(2,1)S(1)} %get-tuple-element.57), channel_id=1, source_target_pairs={{0,12},{4,8},{8,4},{12,0},{16,28},{20,24},{24,20},{28,16},{1,13},{... | collective-permute-start | bytes 393224 | tf_op jit(solution)/shard_map/ppermute | solution.py:35
  23.5 0.8 %collective-permute-done.7.refs_2_ = bf16[128,512]{1,0:T(8,128)(2,1)S(1)} collective-permute-done((bf16[128,512]{1,0:T(8,128)(2,1)S(1)}, bf16[128,512]{1,0:T(8,128)(2,1)S(1)}, u32[]{:S(2)}, u32[]{:S(2)}) %collective-permute-start.7) | collective-permute-done | bytes 131104 | tf_op jit(solution)/shard_map/ppermute | solution.py:35
  24.2 1.9 %collective-permute-done.8.refs_3_ = bf16[128,512]{1,0:T(8,128)(2,1)S(1)} collective-permute-done((bf16[128,512]{1,0:T(8,128)(2,1)S(1)}, bf16[128,512]{1,0:T(8,128)(2,1)S(1)}, u32[]{:S(2)}, u32[]{:S(2)}) %collective-permute-start.8) | collective-permute-done | bytes 131104 | tf_op jit(solution)/shard_map/ppermute | solution.py:35
  26.1 0.0 copy-done.6
  26.1 0.0 copy-done.4
  26.1 0.0 copy-done.5
  26.1 0.0 copy-start.3
  26.1 0.0 copy-start.7
  26.2 0.0 copy-start.11
  26.2 1.0 %partial.1.part = f32[256,512]{1,0:T(8,128)S(1)} custom-call(s32[2]{0:T(128)S(1)} %pad_add_fusion.place, bf16[256,256]{1,0:T(8,128)(2,1)S(1)} %copy-done.6, bf16[256,512]{1,0:T(8,128)(2,1)S(1)} %copy-done, bf16[256,512]{1,0:T(8,128)(2,1)S(1)} %copy-done.4, bf16[256,512]{1,0:T(8,128)(2,1)S(1)} %copy-done.5, bf16[128,512]{1,0:T(8,128)(2,1)S(1)} %get-tuple-element.46.refs_0_, ...), custom_call_target="tpu_custom_call" | custom-call | flops 201326592 | bytes 1572864 | tf_op jit(solution)/shard_map/partial/pallas_call | solution.py:231
  27.2 0.0 copy-start.2
  27.2 0.0 collective-permute-done.10.refs_1_
  27.2 0.0 collective-permute-done.11.refs_2_
  27.2 2.5 %collective-permute-done.12.refs_3_ = bf16[128,512]{1,0:T(8,128)(2,1)S(1)} collective-permute-done((bf16[128,512]{1,0:T(8,128)(2,1)S(1)}, bf16[128,512]{1,0:T(8,128)(2,1)S(1)}, u32[]{:S(2)}, u32[]{:S(2)}) %collective-permute-start.12) | collective-permute-done | bytes 131104 | tf_op jit(solution)/shard_map/ppermute | solution.py:35
  29.7 0.0 copy-done.3
  29.7 0.0 copy-done.7
  29.7 0.0 copy-done.11
  29.7 1.1 %final.1 = (bf16[64,512]{1,0:T(8,128)(2,1)S(1)}, bf16[64,512]{1,0:T(8,128)(2,1)S(1)}, bf16[64,512]{1,0:T(8,128)(2,1)S(1)}, bf16[64,512]{1,0:T(8,128)(2,1)S(1)}) custom-call(s32[2]{0:T(128)S(1)} %pad_add_fusion.place, s32[1,4]{1,0:T(1,128)S(1)} %copy-done.8, s32[1,4]{1,0:T(1,128)S(1)} %copy-done.11, f32[256,512]{1,0:T(8,128)S(1)} %partial.1.part, ...), custom_call_target="tpu_custom_call" | custom-call | flops 134217728 | bytes 1572864 | tf_op jit(solution)/shard_map/final/pallas_call | solution.py:241
  30.8 0.1 collective-permute-start.13
  30.9 1.6 %collective-permute-start.14 = (bf16[64,512]{1,0:T(8,128)(2,1)S(1)}, bf16[64,512]{1,0:T(8,128)(2,1)S(1)}, u32[]{:S(2)}, u32[]{:S(2)}) collective-permute-start(bf16[64,512]{1,0:T(8,128)(2,1)S(1)} %get-tuple-element.60.refs_2_), channel_id=1, source_target_pairs={{0,2},{1,3},{2,0},{3,1},{4,6},{5,7},{6,4},{7,5},{8,10},{9,11},{10,... | collective-permute-start | bytes 196616 | tf_op jit(solution)/shard_map/ppermute | solution.py:35
  32.5 0.3 collective-permute-start.15
  32.8 0.0 copy-done.2
  32.8 0.4 prepare.1
  33.2 0.0 collective-permute-done.13.refs_5_
  33.2 2.3 %collective-permute-done.14.refs_6_ = bf16[64,512]{1,0:T(8,128)(2,1)S(1)} collective-permute-done((bf16[64,512]{1,0:T(8,128)(2,1)S(1)}, bf16[64,512]{1,0:T(8,128)(2,1)S(1)}, u32[]{:S(2)}, u32[]{:S(2)}) %collective-permute-start.14) | collective-permute-done | bytes 65568 | tf_op jit(solution)/shard_map/ppermute | solution.py:35
  35.4 1.1 %collective-permute-done.15.refs_7_ = bf16[64,512]{1,0:T(8,128)(2,1)S(1)} collective-permute-done((bf16[64,512]{1,0:T(8,128)(2,1)S(1)}, bf16[64,512]{1,0:T(8,128)(2,1)S(1)}, u32[]{:S(2)}, u32[]{:S(2)}) %collective-permute-start.15) | collective-permute-done | bytes 65568 | tf_op jit(solution)/shard_map/ppermute | solution.py:35
  36.6 1.9 %scatter.1 = (bf16[256,512]{1,0:T(8,128)(2,1)}, bf16[1024,512]{1,0:T(8,128)(2,1)}) custom-call(s32[2]{0:T(128)S(1)} %pad_add_fusion.place, bf16[1024,512]{1,0:T(8,128)(2,1)S(1)} %get-tuple-element.44.base, bf16[1024,256]{1,0:T(8,128)(2,1)S(1)} %get-tuple-element.45.hot, bf16[64,512]{1,0:T(8,128)(2,1)S(1)} %get-tuple-element.58.refs_0_.refs_4_, ...), custom_call_target="tpu_custom_call" | custom-call | tf_op jit(solution)/shard_map/scatter/pallas_call | solution.py:258
  (2 shorter events, 0.0 us)
Async XLA Ops:
  0.6 19.1 %collective-permute-start.9 = (bf16[256,512]{1,0:T(8,128)(2,1)}, bf16[256,512]{1,0:T(8,128)(2,1)S(1)}, u32[]{:S(2)}, u32[]{:S(2)}) collective-permute-start(bf16[256,512]{1,0:T(8,128)(2,1)} %hidden.3), channel_id=1, source_target_pairs={{0,16},{4,20},{8,24},{12,28},{16,0},{20,4},{24,8},{28,12},{1,17},{... | collective-permute-start | bytes 786440 | tf_op jit(solution)/shard_map/ppermute | solution.py:35
  4.7 0.7 %copy-start.12 = (s32[1,4]{1,0:T(1,128)S(1)}, s32[1,4]{1,0:T(1,128)}, u32[]{:S(2)}) copy-start(s32[1,4]{1,0:T(1,128)} %count.1) | copy-start | bytes 52
  4.7 0.7 %copy-start.9 = (s32[1,4,128]{2,1,0:T(4,128)S(1)}, s32[1,4,128]{2,1,0:T(4,128)}, u32[]{:S(2)}) copy-start(s32[1,4,128]{2,1,0:T(4,128)} %rows.1) | copy-start | bytes 6148
  4.8 0.7 %copy-start.8 = (s32[1,4]{1,0:T(1,128)S(1)}, s32[1,4]{1,0:T(1,128)}, u32[]{:S(2)}) copy-start(s32[1,4]{1,0:T(1,128)} %src.3) | copy-start | bytes 52
  4.8 0.7 %copy-start.10 = (s32[256]{0:T(256)S(1)}, s32[256]{0:T(256)}, u32[]{:S(2)}) copy-start(s32[256]{0:T(256)} %param.23) | copy-start | bytes 3076
  6.3 3.4 %collective-permute-start = (s32[1,256]{1,0:T(1,128)S(1)}, s32[1,256]{1,0:T(1,128)S(1)}, u32[]{:S(2)}, u32[]{:S(2)}) collective-permute-start(s32[1,256]{1,0:T(1,128)S(1)} %get-tuple-element.33), channel_id=1, source_target_pairs={{0,1},{1,0},{2,3},{3,2},{4,5},{5,4},{6,7},{7,6},{8,9},{9,8},{10,11... | collective-permute-start | bytes 3080 | tf_op jit(solution)/shard_map/ppermute | solution.py:35
  6.4 4.9 %collective-permute-start.1 = (s32[1,256]{1,0:T(1,128)S(1)}, s32[1,256]{1,0:T(1,128)S(1)}, u32[]{:S(2)}, u32[]{:S(2)}) collective-permute-start(s32[1,256]{1,0:T(1,128)S(1)} %get-tuple-element.34), channel_id=1, source_target_pairs={{0,2},{1,3},{2,0},{3,1},{4,6},{5,7},{6,4},{7,5},{8,10},{9,11},{10,... | collective-permute-start | bytes 3080 | tf_op jit(solution)/shard_map/ppermute | solution.py:35
  7.9 4.6 %collective-permute-start.2 = (s32[1,256]{1,0:T(1,128)S(1)}, s32[1,256]{1,0:T(1,128)S(1)}, u32[]{:S(2)}, u32[]{:S(2)}) collective-permute-start(s32[1,256]{1,0:T(1,128)S(1)} %get-tuple-element.35), channel_id=1, source_target_pairs={{0,3},{1,2},{2,1},{3,0},{4,7},{5,6},{6,5},{7,4},{8,11},{9,10},{10,... | collective-permute-start | bytes 3080 | tf_op jit(solution)/shard_map/ppermute | solution.py:35
  8.2 4.3 %collective-permute-start.3 = (s32[1,256]{1,0:T(1,128)S(1)}, s32[1,256]{1,0:T(1,128)S(1)}, u32[]{:S(2)}, u32[]{:S(2)}) collective-permute-start(s32[1,256]{1,0:T(1,128)S(1)} %get-tuple-element.37), channel_id=1, source_target_pairs={{0,4},{4,0},{8,12},{12,8},{16,20},{20,16},{24,28},{28,24},{1,5},{5... | collective-permute-start | bytes 3080 | tf_op jit(solution)/shard_map/ppermute | solution.py:35
  9.7 3.7 %collective-permute-start.4 = (s32[1,256]{1,0:T(1,128)S(1)}, s32[1,256]{1,0:T(1,128)S(1)}, u32[]{:S(2)}, u32[]{:S(2)}) collective-permute-start(s32[1,256]{1,0:T(1,128)S(1)} %get-tuple-element.38), channel_id=1, source_target_pairs={{0,8},{4,12},{8,0},{12,4},{16,24},{20,28},{24,16},{28,20},{1,9},{5... | collective-permute-start | bytes 3080 | tf_op jit(solution)/shard_map/ppermute | solution.py:35
  11.3 4.5 %collective-permute-start.5 = (s32[1,256]{1,0:T(1,128)S(1)}, s32[1,256]{1,0:T(1,128)S(1)}, u32[]{:S(2)}, u32[]{:S(2)}) collective-permute-start(s32[1,256]{1,0:T(1,128)S(1)} %get-tuple-element.39), channel_id=1, source_target_pairs={{0,12},{4,8},{8,4},{12,0},{16,28},{20,24},{24,20},{28,16},{1,13},{... | collective-permute-start | bytes 3080 | tf_op jit(solution)/shard_map/ppermute | solution.py:35
  15.8 1.2 %copy-start.1 = (bf16[1024,512]{1,0:T(8,128)(2,1)S(1)}, bf16[1024,512]{1,0:T(8,128)(2,1)}, u32[]{:S(2)}) copy-start(bf16[1024,512]{1,0:T(8,128)(2,1)} %history.3) | copy-start | bytes 3145732
  17.0 2.7 %copy-start = (bf16[256,512]{1,0:T(8,128)(2,1)S(1)}, bf16[256,512]{1,0:T(8,128)(2,1)}, u32[]{:S(2)}) copy-start(bf16[256,512]{1,0:T(8,128)(2,1)} %hidden.3) | copy-start | bytes 786436
  17.0 9.1 %copy-start.6 = (bf16[256,256]{1,0:T(8,128)(2,1)S(1)}, bf16[256,256]{1,0:T(8,128)(2,1)}, u32[]{:S(2)}) copy-start(bf16[256,256]{1,0:T(8,128)(2,1)} %own_adj.1) | copy-start | bytes 393220
  17.8 3.9 %collective-permute-start.6 = (bf16[128,512]{1,0:T(8,128)(2,1)S(1)}, bf16[128,512]{1,0:T(8,128)(2,1)S(1)}, u32[]{:S(2)}, u32[]{:S(2)}) collective-permute-start(bf16[128,512]{1,0:T(8,128)(2,1)S(1)} %get-tuple-element.47), channel_id=1, source_target_pairs={{0,1},{1,0},{2,3},{3,2},{4,5},{5,4},{6,7},{7,6},{8,9},{9,8},{10,11... | collective-permute-start | bytes 393224 | tf_op jit(solution)/shard_map/ppermute | solution.py:35
  17.9 6.4 %collective-permute-start.7 = (bf16[128,512]{1,0:T(8,128)(2,1)S(1)}, bf16[128,512]{1,0:T(8,128)(2,1)S(1)}, u32[]{:S(2)}, u32[]{:S(2)}) collective-permute-start(bf16[128,512]{1,0:T(8,128)(2,1)S(1)} %get-tuple-element.48), channel_id=1, source_target_pairs={{0,2},{1,3},{2,0},{3,1},{4,6},{5,7},{6,4},{7,5},{8,10},{9,11},{10,... | collective-permute-start | bytes 393224 | tf_op jit(solution)/shard_map/ppermute | solution.py:35
  19.4 6.7 %copy-start.4 = (bf16[256,512]{1,0:T(8,128)(2,1)S(1)}, bf16[256,512]{1,0:T(8,128)(2,1)}, u32[]{:S(2)}) copy-start(bf16[256,512]{1,0:T(8,128)(2,1)} %pull_adj.1) | copy-start | bytes 786436
  19.4 6.7 %copy-start.5 = (bf16[256,512]{1,0:T(8,128)(2,1)S(1)}, bf16[256,512]{1,0:T(8,128)(2,1)}, u32[]{:S(2)}) copy-start(bf16[256,512]{1,0:T(8,128)(2,1)} %initial.1) | copy-start | bytes 786436
  19.4 6.7 %collective-permute-start.8 = (bf16[128,512]{1,0:T(8,128)(2,1)S(1)}, bf16[128,512]{1,0:T(8,128)(2,1)S(1)}, u32[]{:S(2)}, u32[]{:S(2)}) collective-permute-start(bf16[128,512]{1,0:T(8,128)(2,1)S(1)} %get-tuple-element.49), channel_id=1, source_target_pairs={{0,3},{1,2},{2,1},{3,0},{4,7},{5,6},{6,5},{7,4},{8,11},{9,10},{10,... | collective-permute-start | bytes 393224 | tf_op jit(solution)/shard_map/ppermute | solution.py:35
  19.9 7.3 %collective-permute-start.10 = (bf16[128,512]{1,0:T(8,128)(2,1)S(1)}, bf16[128,512]{1,0:T(8,128)(2,1)S(1)}, u32[]{:S(2)}, u32[]{:S(2)}) collective-permute-start(bf16[128,512]{1,0:T(8,128)(2,1)S(1)} %get-tuple-element.55), channel_id=1, source_target_pairs={{0,4},{4,0},{8,12},{12,8},{16,20},{20,16},{24,28},{28,24},{1,5},{5... | collective-permute-start | bytes 393224 | tf_op jit(solution)/shard_map/ppermute | solution.py:35
  20.5 6.7 %collective-permute-start.11 = (bf16[128,512]{1,0:T(8,128)(2,1)S(1)}, bf16[128,512]{1,0:T(8,128)(2,1)S(1)}, u32[]{:S(2)}, u32[]{:S(2)}) collective-permute-start(bf16[128,512]{1,0:T(8,128)(2,1)S(1)} %get-tuple-element.56), channel_id=1, source_target_pairs={{0,8},{4,12},{8,0},{12,4},{16,24},{20,28},{24,16},{28,20},{1,9},{5... | collective-permute-start | bytes 393224 | tf_op jit(solution)/shard_map/ppermute | solution.py:35
  21.7 8.0 %collective-permute-start.12 = (bf16[128,512]{1,0:T(8,128)(2,1)S(1)}, bf16[128,512]{1,0:T(8,128)(2,1)S(1)}, u32[]{:S(2)}, u32[]{:S(2)}) collective-permute-start(bf16[128,512]{1,0:T(8,128)(2,1)S(1)} %get-tuple-element.57), channel_id=1, source_target_pairs={{0,12},{4,8},{8,4},{12,0},{16,28},{20,24},{24,20},{28,16},{1,13},{... | collective-permute-start | bytes 393224 | tf_op jit(solution)/shard_map/ppermute | solution.py:35
  26.1 3.6 %copy-start.3 = (bf16[512,512]{1,0:T(8,128)(2,1)S(1)}, bf16[512,512]{1,0:T(8,128)(2,1)}, u32[]{:S(2)}) copy-start(bf16[512,512]{1,0:T(8,128)(2,1)} %weight.1) | copy-start | bytes 1572868
  26.1 3.6 %copy-start.7 = (bf16[4,64,64]{2,1,0:T(8,128)(2,1)S(1)}, bf16[4,64,64]{2,1,0:T(8,128)(2,1)}, u32[]{:S(2)}) copy-start(bf16[4,64,64]{2,1,0:T(8,128)(2,1)} %tiles.1) | copy-start | bytes 98308
  26.2 3.6 %copy-start.11 = (s32[1,4]{1,0:T(1,128)S(1)}, s32[1,4]{1,0:T(1,128)}, u32[]{:S(2)}) copy-start(s32[1,4]{1,0:T(1,128)} %dst.1) | copy-start | bytes 52
  27.2 5.6 %copy-start.2 = (bf16[1024,512]{1,0:T(8,128)(2,1)S(1)}, bf16[1024,512]{1,0:T(8,128)(2,1)}, u32[]{:S(2)}) copy-start(bf16[1024,512]{1,0:T(8,128)(2,1)} %history.3) | copy-start | bytes 3145732
  30.8 2.3 %collective-permute-start.13 = (bf16[64,512]{1,0:T(8,128)(2,1)S(1)}, bf16[64,512]{1,0:T(8,128)(2,1)S(1)}, u32[]{:S(2)}, u32[]{:S(2)}) collective-permute-start(bf16[64,512]{1,0:T(8,128)(2,1)S(1)} %get-tuple-element.59.refs_1_), channel_id=1, source_target_pairs={{0,1},{1,0},{2,3},{3,2},{4,5},{5,4},{6,7},{7,6},{8,9},{9,8},{10,11... | collective-permute-start | bytes 196616 | tf_op jit(solution)/shard_map/ppermute | solution.py:35
  30.9 4.5 %collective-permute-start.14 = (bf16[64,512]{1,0:T(8,128)(2,1)S(1)}, bf16[64,512]{1,0:T(8,128)(2,1)S(1)}, u32[]{:S(2)}, u32[]{:S(2)}) collective-permute-start(bf16[64,512]{1,0:T(8,128)(2,1)S(1)} %get-tuple-element.60.refs_2_), channel_id=1, source_target_pairs={{0,2},{1,3},{2,0},{3,1},{4,6},{5,7},{6,4},{7,5},{8,10},{9,11},{10,... | collective-permute-start | bytes 196616 | tf_op jit(solution)/shard_map/ppermute | solution.py:35
  32.5 4.0 %collective-permute-start.15 = (bf16[64,512]{1,0:T(8,128)(2,1)S(1)}, bf16[64,512]{1,0:T(8,128)(2,1)S(1)}, u32[]{:S(2)}, u32[]{:S(2)}) collective-permute-start(bf16[64,512]{1,0:T(8,128)(2,1)S(1)} %get-tuple-element.61.refs_3_), channel_id=1, source_target_pairs={{0,3},{1,2},{2,1},{3,0},{4,7},{5,6},{6,5},{7,4},{8,11},{9,10},{10,... | collective-permute-start | bytes 196616 | tf_op jit(solution)/shard_map/ppermute | solution.py:35

commit v3 on v2

v3 whole, which is shorter than its diff:
```python
import functools

import jax
import jax.numpy as jnp
from jax import lax
from jax.experimental import pallas as pl
from jax.experimental.pallas import tpu as pltpu
from jax.sharding import PartitionSpec as P

alpha_init = 0.1
beta_map = 0.4

VMEM = pltpu.VMEM
SMEM = pltpu.SMEM
LIMIT = 24 * 1024 * 1024


def vmem():
    return pl.BlockSpec(memory_space=VMEM)


def smem():
    return pl.BlockSpec(memory_space=SMEM)


def cost(flops, size):
    return pl.CostEstimate(flops=flops, bytes_accessed=size, transcendentals=0)


def params():
    return pltpu.CompilerParams(vmem_limit_bytes=LIMIT)


def swap(x, axis, n, k):
    return lax.ppermute(x, axis, [(i, i ^ k) for i in range(n)])


def message_kernel(n_hist, n_half, per_dev, place, src, count, rows, push, *outs):
    to_hist, to_half = outs[:n_hist], outs[n_hist:]
    cap = rows.shape[2]
    per_owner = push.shape[1] // n_hist
    b, h = place[0], place[1]
    for k in range(n_half):
        for slot, name in enumerate((k + n_half, k)):
            wanted = 0
            for t in range(src.shape[1]):
                wanted = jnp.where((src[0, t] // per_dev) ^ b == name, src[0, t] % per_dev, wanted)
            to_half[k][:, slot * 128 : slot * 128 + 128] = jnp.full((1, 128), wanted, jnp.int32)
    lane = lax.broadcasted_iota(jnp.int32, (1, cap), 1)
    for k in range(n_hist):
        o = h ^ k
        to_hist[k][:, :cap] = jnp.where(lane < count[0, o], rows[0, pl.ds(o, 1), :], -1)
        pushed = push[:, :per_owner]
        for j in range(1, n_hist):
            pushed = jnp.where(o == j, push[:, j * per_owner : (j + 1) * per_owner], pushed)
        to_hist[k][:, cap : cap + per_owner] = pushed


def pick(held, asked, slot, rows):
    wanted = asked[:, slot * 128 : slot * 128 + 1]
    block = held[:rows, :]
    for j in range(1, held.shape[0] // rows):
        block = jnp.where(
            jnp.broadcast_to(wanted == j, block.shape), held[j * rows : (j + 1) * rows, :], block
        )
    return block


def one_hop(k):
    return k > 1 and k & (k - 1) == 0


def pick_own_kernel(hidden, *refs):
    asked, outs = refs[: len(refs) // 2], refs[len(refs) // 2 :]
    for one, out in zip(asked, outs):
        out[...] = pick(hidden, one, 1, out.shape[0])


def pick_far_kernel(rows, hidden, far, *refs):
    asked, outs = refs[: len(refs) // 2], refs[len(refs) // 2 :]
    for one, out in zip(asked, outs):
        out[:rows, :] = pick(far, one, 0, rows)
        if out.shape[0] > rows:
            out[rows:, :] = pick(hidden, one, 1, rows)


def spread_kernel(per_dev, place, src, dst, tiles, out):
    block = tiles.shape[1]
    out[...] = jnp.zeros_like(out)
    for t in range(tiles.shape[0]):
        rows = pl.ds(pl.multiple_of(dst[0, t] * block, block), block)
        out[(src[0, t] // per_dev) ^ place[0], rows, :] = tiles[t]


def load_kernel(history, after, out):
    out[...] = history[...]


def pull_kernel(n_hist, cap, history, *refs):
    asked, outs = refs[:n_hist], refs[n_hist:]
    held = lax.broadcasted_iota(jnp.int32, (history.shape[0], cap), 0)
    for k in range(n_hist):
        hot = jnp.where(held == asked[k][:, :cap], 1.0, 0.0).astype(jnp.bfloat16)
        outs[k][...] = lax.dot_general(
            hot, history[...], (((0,), (0,)), ((), ())), preferred_element_type=jnp.float32
        ).astype(jnp.bfloat16)


def prepare_kernel(n_hist, cap, history, *refs):
    asked, sent = refs[:n_hist], refs[n_hist : 2 * n_hist]
    base, hot, refreshed, index, sem = refs[2 * n_hist :]
    h = lax.axis_index("hist")
    size = index.shape[1] // n_hist
    copies = []
    for k in range(n_hist):
        to = refreshed.at[pl.ds(pl.multiple_of((h ^ k) * size, size), size), :]
        copies.append(pltpu.make_async_copy(sent[k], to, sem.at[k]))
        copies[-1].start()
        index[:, k * size : (k + 1) * size] = asked[k][:, cap : cap + size]
    held = lax.broadcasted_iota(jnp.int32, hot.shape, 0)
    found = jnp.where(held == index[...], 1.0, 0.0)
    hot[...] = found.astype(jnp.bfloat16)
    hit = jnp.sum(found, axis=1, keepdims=True)
    base[...] = jnp.where(hit > 0.0, 0.0, history[...].astype(jnp.float32)).astype(jnp.bfloat16)
    for copy in copies:
        copy.wait()


def partial_kernel(n_hist, n_half, cap, own_adj, hidden, pull_adj, initial, spread, mine, *refs):
    arrived, early, out = refs[:n_hist], refs[n_hist:-1], refs[-1]
    h = lax.axis_index("hist")
    total = jnp.dot(own_adj[...], hidden[...], preferred_element_type=jnp.float32)
    total += jnp.dot(spread[n_half], mine[...], preferred_element_type=jnp.float32)
    for k, one in zip([k for k in range(n_half) if k and one_hop(k)], early):
        total += jnp.dot(spread[k], one[...], preferred_element_type=jnp.float32)
    for k in range(n_hist):
        columns = pl.ds(pl.multiple_of((h ^ k) * cap, cap), cap)
        total += jnp.dot(pull_adj[:, columns], arrived[k][...], preferred_element_type=jnp.float32)
    out[...] = (1.0 - alpha_init) * total + alpha_init * initial[...].astype(jnp.float32)


def final_kernel(n_half, chunks, first, part, spread, weight, *refs):
    late, sent, total, support = refs[: n_half - 1], refs[n_half - 1 : -2], refs[-2], refs[-1]
    block = spread.shape[2]
    size = sent[0].shape[0]
    for i, k in enumerate(chunks):
        rows = pl.ds(pl.multiple_of((lax.axis_index("hist") ^ k) * size, size), size)
        here = slice(i * size, (i + 1) * size)
        total[here, :] = part[rows, :]
        for j in range(1, n_half):
            total[here, :] += (1.0 - alpha_init) * jnp.dot(
                spread[n_half + j, rows, :], late[j - 1][:block, :], preferred_element_type=jnp.float32
            )
            if not one_hop(j):
                total[here, :] += (1.0 - alpha_init) * jnp.dot(
                    spread[j, rows, :], late[j - 1][block:, :], preferred_element_type=jnp.float32
                )
    support[...] = total[...].astype(jnp.bfloat16)
    projected = jnp.dot(support[...], weight[...], preferred_element_type=jnp.float32)
    result = jnp.maximum(
        (1.0 - beta_map) * support[...].astype(jnp.float32) + beta_map * projected, 0.0
    ).astype(jnp.bfloat16)
    for i in range(len(chunks)):
        sent[i][...] = result[i * size : (i + 1) * size, :]


def scatter_kernel(steps, base, hot, *refs):
    pushed, (out, rows, new, sem) = refs[:-4], refs[-4:]
    size = pushed[0].shape[0]
    for k, one in enumerate(pushed):
        rows[k * size : (k + 1) * size, :] = one[...]
    step = base.shape[0] // steps
    copies = []
    for i in range(steps):
        at = slice(i * step, (i + 1) * step)
        found = jnp.dot(hot[at, :], rows[...], preferred_element_type=jnp.float32)
        new[at, :] = (base[at, :].astype(jnp.float32) + found).astype(jnp.bfloat16)
        copies.append(pltpu.make_async_copy(new.at[at, :], out.at[at, :], sem.at[i]))
        copies[-1].start()
    for copy in copies:
        copy.wait()


def local(
    hidden,
    initial,
    own_adj,
    tiles,
    tile_src,
    tile_dst,
    history,
    pull_rows,
    pull_count,
    pull_adj,
    weight,
    push_rows,
):
    rows_dev, feature = hidden.shape
    block_rows = tiles.shape[1]
    per_dev = rows_dev // block_rows
    n_blk = lax.axis_size("blk")
    n_hist = lax.axis_size("hist")
    cap = pull_rows.shape[2]
    per_owner = rows_dev // n_hist
    held = history.shape[0]
    n_half = n_blk // 2
    place = jnp.stack([lax.axis_index("blk"), lax.axis_index("hist")]).astype(jnp.int32)
    anywhere = pl.BlockSpec(memory_space=pl.ANY)

    def shape(s, dtype=jnp.bfloat16):
        return jax.ShapeDtypeStruct(s, dtype)

    far = swap(hidden, "blk", n_blk, n_half)
    asks = pl.pallas_call(
        functools.partial(message_kernel, n_hist, n_half, per_dev),
        out_shape=[shape((1, cap + 128), jnp.int32)] * n_hist
        + [shape((1, 256), jnp.int32) for k in range(n_half)],
        in_specs=[smem(), smem(), smem(), vmem(), vmem()],
        out_specs=[vmem()] * (n_hist + n_half),
        compiler_params=params(),
        name="message",
    )(place, tile_src, pull_count, pull_rows, push_rows.reshape(1, rows_dev))
    wanted = [asks[n_hist]] + [swap(asks[n_hist + k], "blk", n_blk, k) for k in range(1, n_half)]
    asked = [asks[0]] + [swap(asks[k], "hist", n_hist, k) for k in range(1, n_hist)]
    spread = pl.pallas_call(
        functools.partial(spread_kernel, per_dev),
        out_shape=shape((n_blk, rows_dev, block_rows)),
        in_specs=[smem()] * 3 + [vmem()],
        out_specs=vmem(),
        compiler_params=params(),
        cost_estimate=cost(0, n_blk * rows_dev * block_rows * 2),
        name="spread",
    )(place, tile_src, tile_dst, tiles)

    history = pl.pallas_call(
        load_kernel,
        out_shape=shape(history.shape),
        in_specs=[vmem(), anywhere],
        out_specs=vmem(),
        compiler_params=params(),
        cost_estimate=cost(0, held * feature * 4),
        name="load",
    )(history, spread)
    asked, wanted, history = lax.optimization_barrier((asked, wanted, history))

    fetched = pl.pallas_call(
        functools.partial(pull_kernel, n_hist, cap),
        out_shape=[shape((cap, feature))] * n_hist,
        in_specs=[vmem()] * (1 + n_hist),
        out_specs=[vmem()] * n_hist,
        compiler_params=params(),
        cost_estimate=cost(2 * n_hist * cap * held * feature, held * feature * 4),
        name="pull",
    )(history, *asked)
    arrived = [fetched[0]] + [swap(fetched[k], "hist", n_hist, k) for k in range(1, n_hist)]

    peers = range(1, n_half)
    soon = [k for k in peers if one_hop(k)]
    picked = pl.pallas_call(
        pick_own_kernel,
        out_shape=[shape((block_rows, feature))] * len(soon),
        in_specs=[vmem()] * (1 + len(soon)),
        out_specs=[vmem()] * len(soon),
        compiler_params=params(),
        cost_estimate=cost(0, n_half * 4 * block_rows * feature),
        name="pick_own",
    )(hidden, *[wanted[k] for k in soon])
    early = [swap(one, "blk", n_blk, k) for one, k in zip(picked, soon)]

    picked = pl.pallas_call(
        functools.partial(pick_far_kernel, block_rows),
        out_shape=[
            shape((2 * block_rows if k and not one_hop(k) else block_rows, feature))
            for k in range(n_half)
        ],
        in_specs=[vmem()] * (n_half + 2),
        out_specs=[vmem()] * n_half,
        compiler_params=params(),
        cost_estimate=cost(0, n_half * 4 * block_rows * feature),
        name="pick_far",
    )(hidden, far, *wanted)
    mine = picked[0]
    late = [swap(picked[k], "blk", n_blk, k) for k in peers]

    part = pl.pallas_call(
        functools.partial(partial_kernel, n_hist, n_half, cap),
        out_shape=shape((rows_dev, feature), jnp.float32),
        in_specs=[vmem()] * (6 + n_hist + len(early)),
        out_specs=vmem(),
        compiler_params=params(),
        cost_estimate=cost(2 * rows_dev * feature * (rows_dev + n_hist * cap), rows_dev * feature * 12),
        name="partial",
    )(own_adj, hidden, pull_adj, initial, spread, mine, *arrived, *early)

    def final(chunks, name, first):
        rows = len(chunks) * per_owner
        return pl.pallas_call(
            functools.partial(final_kernel, n_half, chunks),
            out_shape=[shape((per_owner, feature))] * len(chunks),
            in_specs=[anywhere] + [vmem()] * (2 + n_half),
            out_specs=[vmem()] * len(chunks),
            scratch_shapes=[VMEM((rows, feature), jnp.float32), VMEM((rows, feature), jnp.bfloat16)],
            compiler_params=params(),
            cost_estimate=cost(2 * rows * feature * feature, rows * feature * 12),
            name=name,
        )(first, part, spread, weight, *late)

    outer = final(list(range(2, n_hist)), "final_outer", mine)
    inner = final([0, 1], "final_inner", outer[0])
    sent = inner + outer
    pushed = [sent[0]] + [swap(sent[k], "hist", n_hist, k) for k in range(1, n_hist)]

    base, hot, refreshed = pl.pallas_call(
        functools.partial(prepare_kernel, n_hist, cap),
        out_shape=[shape((held, feature)), shape((held, rows_dev)), shape((rows_dev, feature))],
        in_specs=[vmem()] * (1 + 2 * n_hist),
        out_specs=[vmem(), vmem(), anywhere],
        scratch_shapes=[VMEM((1, rows_dev), jnp.int32), pltpu.SemaphoreType.DMA((n_hist,))],
        compiler_params=params(),
        cost_estimate=cost(held * rows_dev * 8, held * feature * 6),
        name="prepare",
    )(history, *asked, *sent)

    steps = 4
    new_history = pl.pallas_call(
        functools.partial(scatter_kernel, steps),
        out_shape=shape((held, feature)),
        in_specs=[vmem()] * (2 + n_hist),
        out_specs=anywhere,
        scratch_shapes=[
            VMEM((rows_dev, feature), jnp.bfloat16),
            VMEM((held, feature), jnp.bfloat16),
            pltpu.SemaphoreType.DMA((steps,)),
        ],
        compiler_params=params(),
        name="scatter",
    )(base, hot, *pushed)
    return (refreshed, new_history)


def solution(mesh):
    both = P(("blk", "hist"))
    return jax.shard_map(
        local,
        mesh=mesh,
        in_specs=(both,) * 10 + (P(), both),
        out_specs=(both, both),
        check_vma=False,
    )
```

time: 38.6 us -> 36 us (0.933)
  waiting for transfers between devices: 11.8 us -> 7.59 us
  local copies, waits for them, and re-layouts: 1.96 us -> 2.9 us
  starting transfers between devices: 17.7 us -> 18.1 us
    ppermute x16 -> x17, waiting for transfers between devices: 11.8 us -> 7.59 us  [swap(): return lax.ppermute(x, axis, [(i, i ^ k) for i in range(n)])]
    unnamed x26 -> x24, local copies, waits for them, and re-layouts: 1.96 us -> 2.9 us
    pallas_call x1, Pallas kernels: 0.38 us -> 0.97 us  [local(): pl.pallas_call(functools.partial(prepare_kernel, n_hist, cap), out_shape=...]
    pallas_call x4 -> x8, Pallas kernels: 4.21 us -> 3.76 us  [the longest x1 1.23 us: local(): pl.pallas_call(functools.partial(scatter_kernel, steps), out_shape=shape(...]
    ppermute x16 -> x17, starting transfers between devices: 17.7 us -> 18.1 us  [swap(): return lax.ppermute(x, axis, [(i, i ^ k) for i in range(n)])]
  transfers between devices with their start and end apart: 16 -> 17, of which waited for: 7 -> 8; matrix products, arithmetic and copies ran while one was open for 0% -> 0% of each run, Pallas kernels for 8% -> 13%
where the time goes in v3:
time: 36 us; the launch traced here: 35.7 us
  starting transfers between devices  18.1 us (50%)
  waiting for transfers between devices  7.59 us (21%)
  Pallas kernels  6.3 us (18%)
  local copies, waits for them, and re-layouts  2.9 us (8%)
  between operations  0.79 us (2%)
    ppermute x17, starting transfers between devices, swap(): return lax.ppermute(x, axis, [(i, i ^ k) for i in range(n)])  18.1 us
    ppermute x17, waiting for transfers between devices, swap(): return lax.ppermute(x, axis, [(i, i ^ k) for i in range(n)])  7.59 us
    unnamed x24, local copies, waits for them, and re-layouts  2.9 us
    pallas_call x1, Pallas kernels, local(): pl.pallas_call(functools.partial(scatter_kernel, steps), out_shape=shape(...  1.23 us
    pallas_call x2, Pallas kernels, final(): pl.pallas_call(functools.partial(final_kernel, n_half, chunks), out_shape...  0.98 us
    pallas_call x1, Pallas kernels, local(): pl.pallas_call(functools.partial(prepare_kernel, n_hist, cap), out_shape=...  0.97 us
    pallas_call x1, Pallas kernels, local(): pl.pallas_call(functools.partial(message_kernel, n_hist, n_half, per_dev)...  0.82 us
    pallas_call x1, Pallas kernels, local(): pl.pallas_call(functools.partial(pull_kernel, n_hist, cap), out_shape=[sh...  0.74 us
  transfers between devices with their start and end apart: 17, of which 8 were waited for; matrix products, arithmetic and copies ran while one was open for 0% of the time, Pallas kernels for 13%

profile of v3, /device:TPU:0, one launch (start us, length us, event | category | flops | bytes accessed | tf_op | source)
XLA Modules:
  0.0 35.7 jit_solution(256115273453558281)
XLA Ops:
  0.6 4.1 %collective-permute-start.6 = (bf16[256,512]{1,0:T(8,128)(2,1)}, bf16[256,512]{1,0:T(8,128)(2,1)S(1)}, u32[]{:S(2)}, u32[]{:S(2)}) collective-permute-start(bf16[256,512]{1,0:T(8,128)(2,1)} %hidden.5), channel_id=1, source_target_pairs={{0,16},{4,20},{8,24},{12,28},{16,0},{20,4},{24,8},{28,12},{1,17},{... | collective-permute-start | bytes 786440 | tf_op jit(solution)/shard_map/ppermute | solution.py:35
  4.7 0.0 copy-start.10
  4.7 0.0 copy-start.7
  4.7 0.1 pad_add_fusion.place
  4.8 0.0 copy-start.8
  4.8 0.0 copy-start.9
  4.8 0.6 %copy-done.10 = s32[1,4]{1,0:T(1,128)S(1)} copy-done((s32[1,4]{1,0:T(1,128)S(1)}, s32[1,4]{1,0:T(1,128)}, u32[]{:S(2)}) %copy-start.10) | copy-done | bytes 40
  5.4 0.0 copy-done.7
  5.4 0.0 copy-done.8
  5.5 0.0 copy-done.9
  5.5 0.8 %message.1 = (s32[1,256]{1,0:T(1,128)S(1)}, s32[1,256]{1,0:T(1,128)S(1)}, s32[1,256]{1,0:T(1,128)S(1)}, s32[1,256]{1,0:T(1,128)S(1)}, s32[1,256]{1,0:T(1,128)S(1...) custom-call(s32[2]{0:T(128)S(1)} %pad_add_fusion.place, s32[1,4]{1,0:T(1,128)S(1)} %copy-done.8, ...), custom_call_target="tpu_custom_call" | custom-call | tf_op jit(solution)/shard_map/message/pallas_call | solution.py:214
  6.3 0.0 collective-permute-start
  6.4 1.6 %collective-permute-start.1 = (s32[1,256]{1,0:T(1,128)S(1)}, s32[1,256]{1,0:T(1,128)S(1)}, u32[]{:S(2)}, u32[]{:S(2)}) collective-permute-start(s32[1,256]{1,0:T(1,128)S(1)} %get-tuple-element.36), channel_id=1, source_target_pairs={{0,2},{1,3},{2,0},{3,1},{4,6},{5,7},{6,4},{7,5},{8,10},{9,11},{10,... | collective-permute-start | bytes 3080 | tf_op jit(solution)/shard_map/ppermute | solution.py:35
  7.9 0.3 collective-permute-start.2
  8.2 1.5 %collective-permute-start.3 = (s32[1,256]{1,0:T(1,128)S(1)}, s32[1,256]{1,0:T(1,128)S(1)}, u32[]{:S(2)}, u32[]{:S(2)}) collective-permute-start(s32[1,256]{1,0:T(1,128)S(1)} %get-tuple-element.39), channel_id=1, source_target_pairs={{0,4},{4,0},{8,12},{12,8},{16,20},{20,16},{24,28},{28,24},{1,5},{5... | collective-permute-start | bytes 3080 | tf_op jit(solution)/shard_map/ppermute | solution.py:35
  9.7 0.0 collective-permute-done.refs_1_
  9.7 1.6 %collective-permute-start.4 = (s32[1,256]{1,0:T(1,128)S(1)}, s32[1,256]{1,0:T(1,128)S(1)}, u32[]{:S(2)}, u32[]{:S(2)}) collective-permute-start(s32[1,256]{1,0:T(1,128)S(1)} %get-tuple-element.40), channel_id=1, source_target_pairs={{0,8},{4,12},{8,0},{12,4},{16,24},{20,28},{24,16},{28,20},{1,9},{5... | collective-permute-start | bytes 3080 | tf_op jit(solution)/shard_map/ppermute | solution.py:35
  11.3 0.0 collective-permute-done.1.refs_2_
  11.3 1.2 %collective-permute-start.5 = (s32[1,256]{1,0:T(1,128)S(1)}, s32[1,256]{1,0:T(1,128)S(1)}, u32[]{:S(2)}, u32[]{:S(2)}) collective-permute-start(s32[1,256]{1,0:T(1,128)S(1)} %get-tuple-element.41), channel_id=1, source_target_pairs={{0,12},{4,8},{8,4},{12,0},{16,28},{20,24},{24,20},{28,16},{1,13},{... | collective-permute-start | bytes 3080 | tf_op jit(solution)/shard_map/ppermute | solution.py:35
  12.5 0.0 copy-done.11
  12.5 0.8 %copy-done.6 = bf16[4,64,64]{2,1,0:T(8,128)(2,1)S(1)} copy-done((bf16[4,64,64]{2,1,0:T(8,128)(2,1)S(1)}, bf16[4,64,64]{2,1,0:T(8,128)(2,1)}, u32[]{:S(2)}) %copy-start.6) | copy-done | bytes 32792
  13.3 0.6 %spread.1.after = bf16[8,256,64]{2,1,0:T(8,128)(2,1)S(1)} custom-call(s32[2]{0:T(128)S(1)} %pad_add_fusion.place, s32[1,4]{1,0:T(1,128)S(1)} %copy-done.8, s32[1,4]{1,0:T(1,128)S(1)} %copy-done.11, bf16[4,64,64]{2,1,0:T(8,128)(2,1)S(1)} %copy-done.6), custom_call_target="tpu_custom_call" | custom-call | bytes 262144 | tf_op jit(solution)/shard_map/spread/pallas_call | solution.py:225
  14.0 0.0 copy-start.2
  14.0 1.2 %copy-done.2 = bf16[1024,512]{1,0:T(8,128)(2,1)S(1)} copy-done((bf16[1024,512]{1,0:T(8,128)(2,1)S(1)}, bf16[1024,512]{1,0:T(8,128)(2,1)}, u32[]{:S(2)}) %copy-start.2) | copy-done | bytes 1048600
  15.2 0.1 load.1.history
  15.3 0.0 collective-permute-done.2.refs_3_
  15.3 0.0 collective-permute-done.3.refs_1_
  15.3 0.0 collective-permute-done.4.refs_2_.refs_0_
  15.3 0.5 %collective-permute-done.5.refs_3_ = s32[1,256]{1,0:T(1,128)S(1)} collective-permute-done((s32[1,256]{1,0:T(1,128)S(1)}, s32[1,256]{1,0:T(1,128)S(1)}, u32[]{:S(2)}, u32[]{:S(2)}) %collective-permute-start.5) | collective-permute-done | bytes 1056 | tf_op jit(solution)/shard_map/ppermute | solution.py:35
  15.8 0.7 %pull.1 = (bf16[128,512]{1,0:T(8,128)(2,1)S(1)}, bf16[128,512]{1,0:T(8,128)(2,1)S(1)}, bf16[128,512]{1,0:T(8,128)(2,1)S(1)}, bf16[128,512]{1,0:T(8,128)(2,1)S(1)}) custom-call(bf16[1024,512]{1,0:T(8,128)(2,1)S(1)} %load.1.history, s32[1,256]{1,0:T(1,128)S(1)} %get-tuple-element.43.refs_0_, s32[1,256]{1,0:T(1,128)S(1)} %collective-permute-done.refs_1_, ...), custom_call_target="tpu_custom_call" | custom-call | flops 536870912 | bytes 2097152 | tf_op jit(solution)/shard_map/pull/pallas_call | solution.py:246
  16.6 0.1 collective-permute-start.7
  16.6 0.1 copy-done
  16.8 0.1 pick_own.1
  16.9 0.5 %collective-permute-start.10 = (bf16[64,512]{1,0:T(8,128)(2,1)S(1)}, bf16[64,512]{1,0:T(8,128)(2,1)S(1)}, u32[]{:S(2)}, u32[]{:S(2)}) collective-permute-start(bf16[64,512]{1,0:T(8,128)(2,1)S(1)} %pick_own.1), channel_id=1, source_target_pairs={{0,8},{4,12},{8,0},{12,4},{16,24},{20,28},{24,16},{28,20},{1,9},{5... | collective-permute-start | bytes 196616 | tf_op jit(solution)/shard_map/ppermute | solution.py:35
  17.3 1.5 %collective-permute-start.8 = (bf16[128,512]{1,0:T(8,128)(2,1)S(1)}, bf16[128,512]{1,0:T(8,128)(2,1)S(1)}, u32[]{:S(2)}, u32[]{:S(2)}) collective-permute-start(bf16[128,512]{1,0:T(8,128)(2,1)S(1)} %get-tuple-element.54), channel_id=1, source_target_pairs={{0,2},{1,3},{2,0},{3,1},{4,6},{5,7},{6,4},{7,5},{8,10},{9,11},{10,... | collective-permute-start | bytes 393224 | tf_op jit(solution)/shard_map/ppermute | solution.py:35
  18.9 0.0 collective-permute-start.9
  18.9 0.0 collective-permute-done.6.far
  18.9 0.1 pick_far.1
  19.0 1.5 %collective-permute-start.11 = (bf16[128,512]{1,0:T(8,128)(2,1)S(1)}, bf16[128,512]{1,0:T(8,128)(2,1)S(1)}, u32[]{:S(2)}, u32[]{:S(2)}) collective-permute-start(bf16[128,512]{1,0:T(8,128)(2,1)S(1)} %get-tuple-element.56), channel_id=1, source_target_pairs={{0,4},{4,0},{8,12},{12,8},{16,20},{20,16},{24,28},{28,24},{1,5},{5... | collective-permute-start | bytes 393224 | tf_op jit(solution)/shard_map/ppermute | solution.py:35
  20.5 0.8 %collective-permute-done.10.refs_4_ = bf16[64,512]{1,0:T(8,128)(2,1)S(1)} collective-permute-done((bf16[64,512]{1,0:T(8,128)(2,1)S(1)}, bf16[64,512]{1,0:T(8,128)(2,1)S(1)}, u32[]{:S(2)}, u32[]{:S(2)}) %collective-permute-start.10) | collective-permute-done | bytes 65568 | tf_op jit(solution)/shard_map/ppermute | solution.py:35
  21.3 1.2 %collective-permute-start.13 = (bf16[128,512]{1,0:T(8,128)(2,1)S(1)}, bf16[128,512]{1,0:T(8,128)(2,1)S(1)}, u32[]{:S(2)}, u32[]{:S(2)}) collective-permute-start(bf16[128,512]{1,0:T(8,128)(2,1)S(1)} %get-tuple-element.58), channel_id=1, source_target_pairs={{0,12},{4,8},{8,4},{12,0},{16,28},{20,24},{24,20},{28,16},{1,13},{... | collective-permute-start | bytes 393224 | tf_op jit(solution)/shard_map/ppermute | solution.py:35
  22.5 0.0 collective-permute-done.7.refs_1_
  22.5 0.8 %collective-permute-start.12 = (bf16[64,512]{1,0:T(8,128)(2,1)S(1)}, bf16[64,512]{1,0:T(8,128)(2,1)S(1)}, u32[]{:S(2)}, u32[]{:S(2)}) collective-permute-start(bf16[64,512]{1,0:T(8,128)(2,1)S(1)} %get-tuple-element.57), channel_id=1, source_target_pairs={{0,8},{4,12},{8,0},{12,4},{16,24},{20,28},{24,16},{28,20},{1,9},{5... | collective-permute-start | bytes 196616 | tf_op jit(solution)/shard_map/ppermute | solution.py:35
  23.3 0.4 %collective-permute-done.8.refs_2_ = bf16[128,512]{1,0:T(8,128)(2,1)S(1)} collective-permute-done((bf16[128,512]{1,0:T(8,128)(2,1)S(1)}, bf16[128,512]{1,0:T(8,128)(2,1)S(1)}, u32[]{:S(2)}, u32[]{:S(2)}) %collective-permute-start.8) | collective-permute-done | bytes 131104 | tf_op jit(solution)/shard_map/ppermute | solution.py:35
  23.7 1.1 %collective-permute-done.9.refs_3_ = bf16[128,512]{1,0:T(8,128)(2,1)S(1)} collective-permute-done((bf16[128,512]{1,0:T(8,128)(2,1)S(1)}, bf16[128,512]{1,0:T(8,128)(2,1)S(1)}, u32[]{:S(2)}, u32[]{:S(2)}) %collective-permute-start.9) | collective-permute-done | bytes 131104 | tf_op jit(solution)/shard_map/ppermute | solution.py:35
  24.7 0.0 copy-done.5
  24.8 0.0 copy-done.3
  24.8 0.0 copy-done.4
  24.8 0.0 copy-start.1
  24.8 0.6 %partial.1.part = f32[256,512]{1,0:T(8,128)S(1)} custom-call(bf16[256,256]{1,0:T(8,128)(2,1)S(1)} %copy-done.5, bf16[256,512]{1,0:T(8,128)(2,1)S(1)} %copy-done, bf16[256,512]{1,0:T(8,128)(2,1)S(1)} %copy-done.3, bf16[256,512]{1,0:T(8,128)(2,1)S(1)} %copy-done.4, bf16[8,256,64]{2,1,0:T(8,128)(2,1)S(1)} %spread.1.after, ...), custom_call_target="tpu_custom_call" | custom-call | flops 201326592 | bytes 1572864 | tf_op jit(solution)/shard_map/partial/pallas_call | solution.py:285
  25.4 2.3 %collective-permute-done.12.refs_1_ = bf16[64,512]{1,0:T(8,128)(2,1)S(1)} collective-permute-done((bf16[64,512]{1,0:T(8,128)(2,1)S(1)}, bf16[64,512]{1,0:T(8,128)(2,1)S(1)}, u32[]{:S(2)}, u32[]{:S(2)}) %collective-permute-start.12) | collective-permute-done | bytes 65568 | tf_op jit(solution)/shard_map/ppermute | solution.py:35
  27.7 0.0 collective-permute-done.11.refs_0_
  27.7 0.2 collective-permute-done.13.refs_2_
  27.9 0.0 copy-done.1
  27.9 0.5 %final_outer.1 = (bf16[64,512]{1,0:T(8,128)(2,1)S(1)}, bf16[64,512]{1,0:T(8,128)(2,1)S(1)}) custom-call(bf16[64,512]{1,0:T(8,128)(2,1)S(1)} %get-tuple-element.51.mine.first, f32[256,512]{1,0:T(8,128)S(1)} %partial.1.part, bf16[8,256,64]{2,1,0:T(8,128)(2,1)S(1)} %spread.1.after, bf16[512,512]{1,0:T(8,128)(2,1)S(1)} %copy-done.1, ...), custom_call_target="tpu_custom_call" | custom-call | flops 67108864 | bytes 786432 | tf_op jit(solution)/shard_map/final_outer/pallas_call | solution.py:297
  28.4 1.6 %collective-permute-start.15 = (bf16[64,512]{1,0:T(8,128)(2,1)S(1)}, bf16[64,512]{1,0:T(8,128)(2,1)S(1)}, u32[]{:S(2)}, u32[]{:S(2)}) collective-permute-start(bf16[64,512]{1,0:T(8,128)(2,1)S(1)} %get-tuple-element.59.first.refs_6_), channel_id=1, source_target_pairs={{0,2},{1,3},{2,0},{3,1},{4,6},{5,7},{6,4},{7,5},{8,10},{9,11},{10,... | collective-permute-start | bytes 196616 | tf_op jit(solution)/shard_map/ppermute | solution.py:35
  30.0 0.5 %final_inner.1 = (bf16[64,512]{1,0:T(8,128)(2,1)S(1)}, bf16[64,512]{1,0:T(8,128)(2,1)S(1)}) custom-call(bf16[64,512]{1,0:T(8,128)(2,1)S(1)} %get-tuple-element.59.first.refs_6_, f32[256,512]{1,0:T(8,128)S(1)} %partial.1.part, bf16[8,256,64]{2,1,0:T(8,128)(2,1)S(1)} %spread.1.after, bf16[512,512]{1,0:T(8,128)(2,1)S(1)} %copy-done.1, ...), custom_call_target="tpu_custom_call" | custom-call | flops 67108864 | bytes 786432 | tf_op jit(solution)/shard_map/final_inner/pallas_call | solution.py:297
  30.5 0.1 collective-permute-start.14
  30.6 0.6 %collective-permute-start.16 = (bf16[64,512]{1,0:T(8,128)(2,1)S(1)}, bf16[64,512]{1,0:T(8,128)(2,1)S(1)}, u32[]{:S(2)}, u32[]{:S(2)}) collective-permute-start(bf16[64,512]{1,0:T(8,128)(2,1)S(1)} %get-tuple-element.62.refs_7_), channel_id=1, source_target_pairs={{0,3},{1,2},{2,1},{3,0},{4,7},{5,6},{6,5},{7,4},{8,11},{9,10},{10,... | collective-permute-start | bytes 196616 | tf_op jit(solution)/shard_map/ppermute | solution.py:35
  31.2 1.0 %prepare.1 = (bf16[1024,512]{1,0:T(8,128)(2,1)S(1)}, bf16[1024,256]{1,0:T(8,128)(2,1)S(1)}, bf16[256,512]{1,0:T(8,128)(2,1)}) custom-call(bf16[1024,512]{1,0:T(8,128)(2,1)S(1)} %load.1.history, s32[1,256]{1,0:T(1,128)S(1)} %get-tuple-element.43.refs_0_, s32[1,256]{1,0:T(1,128)S(1)} %collective-permute-done.refs_1_, ...), custom_call_target="tpu_custom_call" | custom-call | flops 2097152 | bytes 3145728 | tf_op jit(solution)/shard_map/prepare/pallas_call | solution.py:313
  32.2 0.0 collective-permute-done.14.refs_1_
  32.2 0.6 %collective-permute-done.15.refs_2_ = bf16[64,512]{1,0:T(8,128)(2,1)S(1)} collective-permute-done((bf16[64,512]{1,0:T(8,128)(2,1)S(1)}, bf16[64,512]{1,0:T(8,128)(2,1)S(1)}, u32[]{:S(2)}, u32[]{:S(2)}) %collective-permute-start.15) | collective-permute-done | bytes 65568 | tf_op jit(solution)/shard_map/ppermute | solution.py:35
  32.7 1.7 %collective-permute-done.16.refs_3_ = bf16[64,512]{1,0:T(8,128)(2,1)S(1)} collective-permute-done((bf16[64,512]{1,0:T(8,128)(2,1)S(1)}, bf16[64,512]{1,0:T(8,128)(2,1)S(1)}, u32[]{:S(2)}, u32[]{:S(2)}) %collective-permute-start.16) | collective-permute-done | bytes 65568 | tf_op jit(solution)/shard_map/ppermute | solution.py:35
  34.5 1.2 %scatter.1 = bf16[1024,512]{1,0:T(8,128)(2,1)} custom-call(bf16[1024,512]{1,0:T(8,128)(2,1)S(1)} %get-tuple-element.64.base, bf16[1024,256]{1,0:T(8,128)(2,1)S(1)} %get-tuple-element.65.hot, bf16[64,512]{1,0:T(8,128)(2,1)S(1)} %get-tuple-element.60.refs_4_.refs_0_, bf16[64,512]{1,0:T(8,128)(2,1)S(1)} %collective-permute-done.14.refs_1_, ...), custom_call_target="tpu_custom_call" | custom-call | tf_op jit(solution)/shard_map/scatter/pallas_call | solution.py:325
  (6 shorter events, 0.0 us)
Async XLA Ops:
  0.6 18.2 %collective-permute-start.6 = (bf16[256,512]{1,0:T(8,128)(2,1)}, bf16[256,512]{1,0:T(8,128)(2,1)S(1)}, u32[]{:S(2)}, u32[]{:S(2)}) collective-permute-start(bf16[256,512]{1,0:T(8,128)(2,1)} %hidden.5), channel_id=1, source_target_pairs={{0,16},{4,20},{8,24},{12,28},{16,0},{20,4},{24,8},{28,12},{1,17},{... | collective-permute-start | bytes 786440 | tf_op jit(solution)/shard_map/ppermute | solution.py:35
  4.7 0.7 %copy-start.10 = (s32[1,4]{1,0:T(1,128)S(1)}, s32[1,4]{1,0:T(1,128)}, u32[]{:S(2)}) copy-start(s32[1,4]{1,0:T(1,128)} %count.1) | copy-start | bytes 52
  4.7 0.7 %copy-start.7 = (s32[1,4,128]{2,1,0:T(4,128)S(1)}, s32[1,4,128]{2,1,0:T(4,128)}, u32[]{:S(2)}) copy-start(s32[1,4,128]{2,1,0:T(4,128)} %rows.1) | copy-start | bytes 6148
  4.8 0.7 %copy-start.8 = (s32[1,4]{1,0:T(1,128)S(1)}, s32[1,4]{1,0:T(1,128)}, u32[]{:S(2)}) copy-start(s32[1,4]{1,0:T(1,128)} %src.3) | copy-start | bytes 52
  4.8 0.7 %copy-start.9 = (s32[256]{0:T(256)S(1)}, s32[256]{0:T(256)}, u32[]{:S(2)}) copy-start(s32[256]{0:T(256)} %param.23) | copy-start | bytes 3076
  6.3 3.4 %collective-permute-start = (s32[1,256]{1,0:T(1,128)S(1)}, s32[1,256]{1,0:T(1,128)S(1)}, u32[]{:S(2)}, u32[]{:S(2)}) collective-permute-start(s32[1,256]{1,0:T(1,128)S(1)} %get-tuple-element.35), channel_id=1, source_target_pairs={{0,1},{1,0},{2,3},{3,2},{4,5},{5,4},{6,7},{7,6},{8,9},{9,8},{10,11... | collective-permute-start | bytes 3080 | tf_op jit(solution)/shard_map/ppermute | solution.py:35
  6.4 4.9 %collective-permute-start.1 = (s32[1,256]{1,0:T(1,128)S(1)}, s32[1,256]{1,0:T(1,128)S(1)}, u32[]{:S(2)}, u32[]{:S(2)}) collective-permute-start(s32[1,256]{1,0:T(1,128)S(1)} %get-tuple-element.36), channel_id=1, source_target_pairs={{0,2},{1,3},{2,0},{3,1},{4,6},{5,7},{6,4},{7,5},{8,10},{9,11},{10,... | collective-permute-start | bytes 3080 | tf_op jit(solution)/shard_map/ppermute | solution.py:35
  7.9 7.3 %collective-permute-start.2 = (s32[1,256]{1,0:T(1,128)S(1)}, s32[1,256]{1,0:T(1,128)S(1)}, u32[]{:S(2)}, u32[]{:S(2)}) collective-permute-start(s32[1,256]{1,0:T(1,128)S(1)} %get-tuple-element.37), channel_id=1, source_target_pairs={{0,3},{1,2},{2,1},{3,0},{4,7},{5,6},{6,5},{7,4},{8,11},{9,10},{10,... | collective-permute-start | bytes 3080 | tf_op jit(solution)/shard_map/ppermute | solution.py:35
  8.2 7.1 %collective-permute-start.3 = (s32[1,256]{1,0:T(1,128)S(1)}, s32[1,256]{1,0:T(1,128)S(1)}, u32[]{:S(2)}, u32[]{:S(2)}) collective-permute-start(s32[1,256]{1,0:T(1,128)S(1)} %get-tuple-element.39), channel_id=1, source_target_pairs={{0,4},{4,0},{8,12},{12,8},{16,20},{20,16},{24,28},{28,24},{1,5},{5... | collective-permute-start | bytes 3080 | tf_op jit(solution)/shard_map/ppermute | solution.py:35
  9.7 2.8 %copy-start.11 = (s32[1,4]{1,0:T(1,128)S(1)}, s32[1,4]{1,0:T(1,128)}, u32[]{:S(2)}) copy-start(s32[1,4]{1,0:T(1,128)} %dst.1) | copy-start | bytes 52
  9.7 5.6 %collective-permute-start.4 = (s32[1,256]{1,0:T(1,128)S(1)}, s32[1,256]{1,0:T(1,128)S(1)}, u32[]{:S(2)}, u32[]{:S(2)}) collective-permute-start(s32[1,256]{1,0:T(1,128)S(1)} %get-tuple-element.40), channel_id=1, source_target_pairs={{0,8},{4,12},{8,0},{12,4},{16,24},{20,28},{24,16},{28,20},{1,9},{5... | collective-permute-start | bytes 3080 | tf_op jit(solution)/shard_map/ppermute | solution.py:35
  11.3 4.5 %collective-permute-start.5 = (s32[1,256]{1,0:T(1,128)S(1)}, s32[1,256]{1,0:T(1,128)S(1)}, u32[]{:S(2)}, u32[]{:S(2)}) collective-permute-start(s32[1,256]{1,0:T(1,128)S(1)} %get-tuple-element.41), channel_id=1, source_target_pairs={{0,12},{4,8},{8,4},{12,0},{16,28},{20,24},{24,20},{28,16},{1,13},{... | collective-permute-start | bytes 3080 | tf_op jit(solution)/shard_map/ppermute | solution.py:35
  12.5 0.8 %copy-start.6 = (bf16[4,64,64]{2,1,0:T(8,128)(2,1)S(1)}, bf16[4,64,64]{2,1,0:T(8,128)(2,1)}, u32[]{:S(2)}) copy-start(bf16[4,64,64]{2,1,0:T(8,128)(2,1)} %tiles.1) | copy-start | bytes 98308
  14.0 1.2 %copy-start.2 = (bf16[1024,512]{1,0:T(8,128)(2,1)S(1)}, bf16[1024,512]{1,0:T(8,128)(2,1)}, u32[]{:S(2)}) copy-start(bf16[1024,512]{1,0:T(8,128)(2,1)} %history.1) | copy-start | bytes 3145732
  15.8 1.0 %copy-start = (bf16[256,512]{1,0:T(8,128)(2,1)S(1)}, bf16[256,512]{1,0:T(8,128)(2,1)}, u32[]{:S(2)}) copy-start(bf16[256,512]{1,0:T(8,128)(2,1)} %hidden.5) | copy-start | bytes 786436
  16.6 6.0 %collective-permute-start.7 = (bf16[128,512]{1,0:T(8,128)(2,1)S(1)}, bf16[128,512]{1,0:T(8,128)(2,1)S(1)}, u32[]{:S(2)}, u32[]{:S(2)}) collective-permute-start(bf16[128,512]{1,0:T(8,128)(2,1)S(1)} %get-tuple-element.53), channel_id=1, source_target_pairs={{0,1},{1,0},{2,3},{3,2},{4,5},{5,4},{6,7},{7,6},{8,9},{9,8},{10,11... | collective-permute-start | bytes 393224 | tf_op jit(solution)/shard_map/ppermute | solution.py:35
  16.8 8.0 %copy-start.5 = (bf16[256,256]{1,0:T(8,128)(2,1)S(1)}, bf16[256,256]{1,0:T(8,128)(2,1)}, u32[]{:S(2)}) copy-start(bf16[256,256]{1,0:T(8,128)(2,1)} %own_adj.1) | copy-start | bytes 393220
  16.9 4.4 %collective-permute-start.10 = (bf16[64,512]{1,0:T(8,128)(2,1)S(1)}, bf16[64,512]{1,0:T(8,128)(2,1)S(1)}, u32[]{:S(2)}, u32[]{:S(2)}) collective-permute-start(bf16[64,512]{1,0:T(8,128)(2,1)S(1)} %pick_own.1), channel_id=1, source_target_pairs={{0,8},{4,12},{8,0},{12,4},{16,24},{20,28},{24,16},{28,20},{1,9},{5... | collective-permute-start | bytes 196616 | tf_op jit(solution)/shard_map/ppermute | solution.py:35
  17.3 6.4 %collective-permute-start.8 = (bf16[128,512]{1,0:T(8,128)(2,1)S(1)}, bf16[128,512]{1,0:T(8,128)(2,1)S(1)}, u32[]{:S(2)}, u32[]{:S(2)}) collective-permute-start(bf16[128,512]{1,0:T(8,128)(2,1)S(1)} %get-tuple-element.54), channel_id=1, source_target_pairs={{0,2},{1,3},{2,0},{3,1},{4,6},{5,7},{6,4},{7,5},{8,10},{9,11},{10,... | collective-permute-start | bytes 393224 | tf_op jit(solution)/shard_map/ppermute | solution.py:35
  18.9 5.9 %copy-start.3 = (bf16[256,512]{1,0:T(8,128)(2,1)S(1)}, bf16[256,512]{1,0:T(8,128)(2,1)}, u32[]{:S(2)}) copy-start(bf16[256,512]{1,0:T(8,128)(2,1)} %pull_adj.1) | copy-start | bytes 786436
  18.9 5.9 %copy-start.4 = (bf16[256,512]{1,0:T(8,128)(2,1)S(1)}, bf16[256,512]{1,0:T(8,128)(2,1)}, u32[]{:S(2)}) copy-start(bf16[256,512]{1,0:T(8,128)(2,1)} %initial.1) | copy-start | bytes 786436
  18.9 5.9 %collective-permute-start.9 = (bf16[128,512]{1,0:T(8,128)(2,1)S(1)}, bf16[128,512]{1,0:T(8,128)(2,1)S(1)}, u32[]{:S(2)}, u32[]{:S(2)}) collective-permute-start(bf16[128,512]{1,0:T(8,128)(2,1)S(1)} %get-tuple-element.55), channel_id=1, source_target_pairs={{0,3},{1,2},{2,1},{3,0},{4,7},{5,6},{6,5},{7,4},{8,11},{9,10},{10,... | collective-permute-start | bytes 393224 | tf_op jit(solution)/shard_map/ppermute | solution.py:35
  19.0 8.7 %collective-permute-start.11 = (bf16[128,512]{1,0:T(8,128)(2,1)S(1)}, bf16[128,512]{1,0:T(8,128)(2,1)S(1)}, u32[]{:S(2)}, u32[]{:S(2)}) collective-permute-start(bf16[128,512]{1,0:T(8,128)(2,1)S(1)} %get-tuple-element.56), channel_id=1, source_target_pairs={{0,4},{4,0},{8,12},{12,8},{16,20},{20,16},{24,28},{28,24},{1,5},{5... | collective-permute-start | bytes 393224 | tf_op jit(solution)/shard_map/ppermute | solution.py:35
  21.3 6.6 %collective-permute-start.13 = (bf16[128,512]{1,0:T(8,128)(2,1)S(1)}, bf16[128,512]{1,0:T(8,128)(2,1)S(1)}, u32[]{:S(2)}, u32[]{:S(2)}) collective-permute-start(bf16[128,512]{1,0:T(8,128)(2,1)S(1)} %get-tuple-element.58), channel_id=1, source_target_pairs={{0,12},{4,8},{8,4},{12,0},{16,28},{20,24},{24,20},{28,16},{1,13},{... | collective-permute-start | bytes 393224 | tf_op jit(solution)/shard_map/ppermute | solution.py:35
  22.5 5.2 %collective-permute-start.12 = (bf16[64,512]{1,0:T(8,128)(2,1)S(1)}, bf16[64,512]{1,0:T(8,128)(2,1)S(1)}, u32[]{:S(2)}, u32[]{:S(2)}) collective-permute-start(bf16[64,512]{1,0:T(8,128)(2,1)S(1)} %get-tuple-element.57), channel_id=1, source_target_pairs={{0,8},{4,12},{8,0},{12,4},{16,24},{20,28},{24,16},{28,20},{1,9},{5... | collective-permute-start | bytes 196616 | tf_op jit(solution)/shard_map/ppermute | solution.py:35
  24.8 3.2 %copy-start.1 = (bf16[512,512]{1,0:T(8,128)(2,1)S(1)}, bf16[512,512]{1,0:T(8,128)(2,1)}, u32[]{:S(2)}) copy-start(bf16[512,512]{1,0:T(8,128)(2,1)} %weight.3) | copy-start | bytes 1572868
  28.4 4.3 %collective-permute-start.15 = (bf16[64,512]{1,0:T(8,128)(2,1)S(1)}, bf16[64,512]{1,0:T(8,128)(2,1)S(1)}, u32[]{:S(2)}, u32[]{:S(2)}) collective-permute-start(bf16[64,512]{1,0:T(8,128)(2,1)S(1)} %get-tuple-element.59.first.refs_6_), channel_id=1, source_target_pairs={{0,2},{1,3},{2,0},{3,1},{4,6},{5,7},{6,4},{7,5},{8,10},{9,11},{10,... | collective-permute-start | bytes 196616 | tf_op jit(solution)/shard_map/ppermute | solution.py:35
  30.5 1.7 %collective-permute-start.14 = (bf16[64,512]{1,0:T(8,128)(2,1)S(1)}, bf16[64,512]{1,0:T(8,128)(2,1)S(1)}, u32[]{:S(2)}, u32[]{:S(2)}) collective-permute-start(bf16[64,512]{1,0:T(8,128)(2,1)S(1)} %get-tuple-element.61.refs_5_), channel_id=1, source_target_pairs={{0,1},{1,0},{2,3},{3,2},{4,5},{5,4},{6,7},{7,6},{8,9},{9,8},{10,11... | collective-permute-start | bytes 196616 | tf_op jit(solution)/shard_map/ppermute | solution.py:35
  30.6 3.9 %collective-permute-start.16 = (bf16[64,512]{1,0:T(8,128)(2,1)S(1)}, bf16[64,512]{1,0:T(8,128)(2,1)S(1)}, u32[]{:S(2)}, u32[]{:S(2)}) collective-permute-start(bf16[64,512]{1,0:T(8,128)(2,1)S(1)} %get-tuple-element.62.refs_7_), channel_id=1, source_target_pairs={{0,3},{1,2},{2,1},{3,0},{4,7},{5,6},{6,5},{7,4},{8,11},{9,10},{10,... | collective-permute-start | bytes 196616 | tf_op jit(solution)/shard_map/ppermute | solution.py:35

commit v4 on v3

--- a/solution.py
+++ b/solution.py
@@ -76,7 +76,7 @@
         out[...] = pick(hidden, one, 1, out.shape[0])
 
 
-def pick_far_kernel(rows, hidden, far, *refs):
+def pick_far_kernel(rows, hidden, far, after, *refs):
     asked, outs = refs[: len(refs) // 2], refs[len(refs) // 2 :]
     for one, out in zip(asked, outs):
         out[:rows, :] = pick(far, one, 0, rows)
@@ -273,12 +273,12 @@
             shape((2 * block_rows if k and not one_hop(k) else block_rows, feature))
             for k in range(n_half)
         ],
-        in_specs=[vmem()] * (n_half + 2),
+        in_specs=[vmem(), vmem(), anywhere] + [vmem()] * n_half,
         out_specs=[vmem()] * n_half,
         compiler_params=params(),
         cost_estimate=cost(0, n_half * 4 * block_rows * feature),
         name="pick_far",
-    )(hidden, far, *wanted)
+    )(hidden, far, arrived[1], *wanted)
     mine = picked[0]
     late = [swap(picked[k], "blk", n_blk, k) for k in peers]
 
@@ -305,8 +305,8 @@
             name=name,
         )(first, part, spread, weight, *late)
 
-    outer = final(list(range(2, n_hist)), "final_outer", mine)
-    inner = final([0, 1], "final_inner", outer[0])
+    outer = final(list(range(1, n_hist)), "final_sent", mine)
+    inner = final([0], "final_kept", outer[0])
     sent = inner + outer
     pushed = [sent[0]] + [swap(sent[k], "hist", n_hist, k) for k in range(1, n_hist)]
 

time: 36 us -> 35.4 us (0.983)
  waiting for transfers between devices: 7.59 us -> 7.03 us
    ppermute x17, waiting for transfers between devices: 7.59 us -> 7.03 us  [swap(): return lax.ppermute(x, axis, [(i, i ^ k) for i in range(n)])]
  transfers between devices with their start and end apart: 17 -> 17, of which waited for: 8 -> 7; matrix products, arithmetic and copies ran while one was open for 0% -> 0% of each run, Pallas kernels for 13% -> 13%
where the time goes in v4:
time: 35.4 us; the launch traced here: 35.2 us
  starting transfers between devices  18.1 us (51%)
  waiting for transfers between devices  7.03 us (20%)
  Pallas kernels  6.32 us (18%)
  local copies, waits for them, and re-layouts  2.79 us (8%)
  between operations  0.81 us (2%)
    ppermute x17, starting transfers between devices, swap(): return lax.ppermute(x, axis, [(i, i ^ k) for i in range(n)])  18.1 us
    ppermute x17, waiting for transfers between devices, swap(): return lax.ppermute(x, axis, [(i, i ^ k) for i in range(n)])  7.03 us
    unnamed x24, local copies, waits for them, and re-layouts  2.79 us
    pallas_call x1, Pallas kernels, local(): pl.pallas_call(functools.partial(scatter_kernel, steps), out_shape=shape(...  1.23 us
    pallas_call x2, Pallas kernels, final(): pl.pallas_call(functools.partial(final_kernel, n_half, chunks), out_shape...  1.01 us
    pallas_call x1, Pallas kernels, local(): pl.pallas_call(functools.partial(prepare_kernel, n_hist, cap), out_shape=...  0.98 us
    pallas_call x1, Pallas kernels, local(): pl.pallas_call(functools.partial(message_kernel, n_hist, n_half, per_dev)...  0.82 us
    pallas_call x1, Pallas kernels, local(): pl.pallas_call(functools.partial(pull_kernel, n_hist, cap), out_shape=[sh...  0.74 us
  transfers between devices with their start and end apart: 17, of which 7 were waited for; matrix products, arithmetic and copies ran while one was open for 0% of the time, Pallas kernels for 13%

profile of v4, /device:TPU:0, one launch (start us, length us, event | category | flops | bytes accessed | tf_op | source)
XLA Modules:
  0.0 35.2 jit_solution(7658802754066185622)
XLA Ops:
  0.6 4.1 %collective-permute-start.6 = (bf16[256,512]{1,0:T(8,128)(2,1)}, bf16[256,512]{1,0:T(8,128)(2,1)S(1)}, u32[]{:S(2)}, u32[]{:S(2)}) collective-permute-start(bf16[256,512]{1,0:T(8,128)(2,1)} %hidden.5), channel_id=1, source_target_pairs={{0,16},{4,20},{8,24},{12,28},{16,0},{20,4},{24,8},{28,12},{1,17},{... | collective-permute-start | bytes 786440 | tf_op jit(solution)/shard_map/ppermute | solution.py:35
  4.7 0.0 copy-start.10
  4.7 0.1 pad_add_fusion.place
  4.8 0.6 %copy-done.10 = s32[1,4]{1,0:T(1,128)S(1)} copy-done((s32[1,4]{1,0:T(1,128)S(1)}, s32[1,4]{1,0:T(1,128)}, u32[]{:S(2)}) %copy-start.10) | copy-done | bytes 40
  5.4 0.0 copy-done.7
  5.4 0.0 copy-done.8
  5.5 0.0 copy-done.9
  5.5 0.8 %message.1 = (s32[1,256]{1,0:T(1,128)S(1)}, s32[1,256]{1,0:T(1,128)S(1)}, s32[1,256]{1,0:T(1,128)S(1)}, s32[1,256]{1,0:T(1,128)S(1)}, s32[1,256]{1,0:T(1,128)S(1...) custom-call(s32[2]{0:T(128)S(1)} %pad_add_fusion.place, s32[1,4]{1,0:T(1,128)S(1)} %copy-done.8, ...), custom_call_target="tpu_custom_call" | custom-call | tf_op jit(solution)/shard_map/message/pallas_call | solution.py:214
  6.3 0.0 collective-permute-start
  6.4 1.6 %collective-permute-start.1 = (s32[1,256]{1,0:T(1,128)S(1)}, s32[1,256]{1,0:T(1,128)S(1)}, u32[]{:S(2)}, u32[]{:S(2)}) collective-permute-start(s32[1,256]{1,0:T(1,128)S(1)} %get-tuple-element.35), channel_id=1, source_target_pairs={{0,2},{1,3},{2,0},{3,1},{4,6},{5,7},{6,4},{7,5},{8,10},{9,11},{10,... | collective-permute-start | bytes 3080 | tf_op jit(solution)/shard_map/ppermute | solution.py:35
  7.9 0.3 collective-permute-start.2
  8.2 1.5 %collective-permute-start.3 = (s32[1,256]{1,0:T(1,128)S(1)}, s32[1,256]{1,0:T(1,128)S(1)}, u32[]{:S(2)}, u32[]{:S(2)}) collective-permute-start(s32[1,256]{1,0:T(1,128)S(1)} %get-tuple-element.38), channel_id=1, source_target_pairs={{0,4},{4,0},{8,12},{12,8},{16,20},{20,16},{24,28},{28,24},{1,5},{5... | collective-permute-start | bytes 3080 | tf_op jit(solution)/shard_map/ppermute | solution.py:35
  9.7 0.0 collective-permute-done.refs_1_
  9.7 1.6 %collective-permute-start.4 = (s32[1,256]{1,0:T(1,128)S(1)}, s32[1,256]{1,0:T(1,128)S(1)}, u32[]{:S(2)}, u32[]{:S(2)}) collective-permute-start(s32[1,256]{1,0:T(1,128)S(1)} %get-tuple-element.39), channel_id=1, source_target_pairs={{0,8},{4,12},{8,0},{12,4},{16,24},{20,28},{24,16},{28,20},{1,9},{5... | collective-permute-start | bytes 3080 | tf_op jit(solution)/shard_map/ppermute | solution.py:35
  11.3 0.0 collective-permute-done.1.refs_2_
  11.3 1.2 %collective-permute-start.5 = (s32[1,256]{1,0:T(1,128)S(1)}, s32[1,256]{1,0:T(1,128)S(1)}, u32[]{:S(2)}, u32[]{:S(2)}) collective-permute-start(s32[1,256]{1,0:T(1,128)S(1)} %get-tuple-element.40), channel_id=1, source_target_pairs={{0,12},{4,8},{8,4},{12,0},{16,28},{20,24},{24,20},{28,16},{1,13},{... | collective-permute-start | bytes 3080 | tf_op jit(solution)/shard_map/ppermute | solution.py:35
  12.5 0.0 copy-done.11
  12.5 0.8 %copy-done.6 = bf16[4,64,64]{2,1,0:T(8,128)(2,1)S(1)} copy-done((bf16[4,64,64]{2,1,0:T(8,128)(2,1)S(1)}, bf16[4,64,64]{2,1,0:T(8,128)(2,1)}, u32[]{:S(2)}) %copy-start.6) | copy-done | bytes 32792
  13.3 0.6 %spread.1.after = bf16[8,256,64]{2,1,0:T(8,128)(2,1)S(1)} custom-call(s32[2]{0:T(128)S(1)} %pad_add_fusion.place, s32[1,4]{1,0:T(1,128)S(1)} %copy-done.8, s32[1,4]{1,0:T(1,128)S(1)} %copy-done.11, bf16[4,64,64]{2,1,0:T(8,128)(2,1)S(1)} %copy-done.6), custom_call_target="tpu_custom_call" | custom-call | bytes 262144 | tf_op jit(solution)/shard_map/spread/pallas_call | solution.py:225
  14.0 0.0 copy-start.2
  14.0 1.2 %copy-done.2 = bf16[1024,512]{1,0:T(8,128)(2,1)S(1)} copy-done((bf16[1024,512]{1,0:T(8,128)(2,1)S(1)}, bf16[1024,512]{1,0:T(8,128)(2,1)}, u32[]{:S(2)}) %copy-start.2) | copy-done | bytes 1048600
  15.2 0.1 load.1.history
  15.3 0.0 collective-permute-done.2.refs_3_
  15.3 0.0 collective-permute-done.3.refs_1_
  15.3 0.0 collective-permute-done.4.refs_2_.refs_0_
  15.3 0.5 %collective-permute-done.5.refs_3_ = s32[1,256]{1,0:T(1,128)S(1)} collective-permute-done((s32[1,256]{1,0:T(1,128)S(1)}, s32[1,256]{1,0:T(1,128)S(1)}, u32[]{:S(2)}, u32[]{:S(2)}) %collective-permute-start.5) | collective-permute-done | bytes 1056 | tf_op jit(solution)/shard_map/ppermute | solution.py:35
  15.8 0.7 %pull.1 = (bf16[128,512]{1,0:T(8,128)(2,1)S(1)}, bf16[128,512]{1,0:T(8,128)(2,1)S(1)}, bf16[128,512]{1,0:T(8,128)(2,1)S(1)}, bf16[128,512]{1,0:T(8,128)(2,1)S(1)}) custom-call(bf16[1024,512]{1,0:T(8,128)(2,1)S(1)} %load.1.history, s32[1,256]{1,0:T(1,128)S(1)} %get-tuple-element.42.refs_0_, s32[1,256]{1,0:T(1,128)S(1)} %collective-permute-done.refs_1_, ...), custom_call_target="tpu_custom_call" | custom-call | flops 536870912 | bytes 2097152 | tf_op jit(solution)/shard_map/pull/pallas_call | solution.py:246
  16.6 0.1 collective-permute-start.7
  16.6 1.6 %collective-permute-start.8 = (bf16[128,512]{1,0:T(8,128)(2,1)S(1)}, bf16[128,512]{1,0:T(8,128)(2,1)S(1)}, u32[]{:S(2)}, u32[]{:S(2)}) collective-permute-start(bf16[128,512]{1,0:T(8,128)(2,1)S(1)} %get-tuple-element.53), channel_id=1, source_target_pairs={{0,2},{1,3},{2,0},{3,1},{4,6},{5,7},{6,4},{7,5},{8,10},{9,11},{10,... | collective-permute-start | bytes 393224 | tf_op jit(solution)/shard_map/ppermute | solution.py:35
  18.2 0.3 collective-permute-start.9
  18.5 0.0 copy-done
  18.5 0.1 pick_own.1
  18.6 0.0 copy-start.3
  18.6 0.0 copy-start.4
  18.6 0.0 copy-start.5
  18.6 0.5 %collective-permute-start.10 = (bf16[64,512]{1,0:T(8,128)(2,1)S(1)}, bf16[64,512]{1,0:T(8,128)(2,1)S(1)}, u32[]{:S(2)}, u32[]{:S(2)}) collective-permute-start(bf16[64,512]{1,0:T(8,128)(2,1)S(1)} %pick_own.1), channel_id=1, source_target_pairs={{0,8},{4,12},{8,0},{12,4},{16,24},{20,28},{24,16},{28,20},{1,9},{5... | collective-permute-start | bytes 196616 | tf_op jit(solution)/shard_map/ppermute | solution.py:35
  19.1 0.0 collective-permute-done.7.after.refs_1_
  19.1 0.0 collective-permute-done.6.far
  19.1 0.1 pick_far.1
  19.3 1.5 %collective-permute-start.11 = (bf16[128,512]{1,0:T(8,128)(2,1)S(1)}, bf16[128,512]{1,0:T(8,128)(2,1)S(1)}, u32[]{:S(2)}, u32[]{:S(2)}) collective-permute-start(bf16[128,512]{1,0:T(8,128)(2,1)S(1)} %get-tuple-element.55), channel_id=1, source_target_pairs={{0,4},{4,0},{8,12},{12,8},{16,20},{20,16},{24,28},{28,24},{1,5},{5... | collective-permute-start | bytes 393224 | tf_op jit(solution)/shard_map/ppermute | solution.py:35
  20.7 1.7 %collective-permute-start.13 = (bf16[128,512]{1,0:T(8,128)(2,1)S(1)}, bf16[128,512]{1,0:T(8,128)(2,1)S(1)}, u32[]{:S(2)}, u32[]{:S(2)}) collective-permute-start(bf16[128,512]{1,0:T(8,128)(2,1)S(1)} %get-tuple-element.57), channel_id=1, source_target_pairs={{0,12},{4,8},{8,4},{12,0},{16,28},{20,24},{24,20},{28,16},{1,13},{... | collective-permute-start | bytes 393224 | tf_op jit(solution)/shard_map/ppermute | solution.py:35
  22.4 0.6 %collective-permute-done.10.refs_4_ = bf16[64,512]{1,0:T(8,128)(2,1)S(1)} collective-permute-done((bf16[64,512]{1,0:T(8,128)(2,1)S(1)}, bf16[64,512]{1,0:T(8,128)(2,1)S(1)}, u32[]{:S(2)}, u32[]{:S(2)}) %collective-permute-start.10) | collective-permute-done | bytes 65568 | tf_op jit(solution)/shard_map/ppermute | solution.py:35
  23.0 0.4 %collective-permute-start.12 = (bf16[64,512]{1,0:T(8,128)(2,1)S(1)}, bf16[64,512]{1,0:T(8,128)(2,1)S(1)}, u32[]{:S(2)}, u32[]{:S(2)}) collective-permute-start(bf16[64,512]{1,0:T(8,128)(2,1)S(1)} %get-tuple-element.56), channel_id=1, source_target_pairs={{0,8},{4,12},{8,0},{12,4},{16,24},{20,28},{24,16},{28,20},{1,9},{5... | collective-permute-start | bytes 196616 | tf_op jit(solution)/shard_map/ppermute | solution.py:35
  23.4 0.0 collective-permute-done.8.refs_2_
  23.4 1.5 %collective-permute-done.9.refs_3_ = bf16[128,512]{1,0:T(8,128)(2,1)S(1)} collective-permute-done((bf16[128,512]{1,0:T(8,128)(2,1)S(1)}, bf16[128,512]{1,0:T(8,128)(2,1)S(1)}, u32[]{:S(2)}, u32[]{:S(2)}) %collective-permute-start.9) | collective-permute-done | bytes 131104 | tf_op jit(solution)/shard_map/ppermute | solution.py:35
  24.9 0.0 copy-done.3
  24.9 0.0 copy-done.4
  24.9 0.0 copy-done.5
  24.9 0.0 copy-start.1
  24.9 0.6 %partial.1.part = f32[256,512]{1,0:T(8,128)S(1)} custom-call(bf16[256,256]{1,0:T(8,128)(2,1)S(1)} %copy-done.5, bf16[256,512]{1,0:T(8,128)(2,1)S(1)} %copy-done, bf16[256,512]{1,0:T(8,128)(2,1)S(1)} %copy-done.3, bf16[256,512]{1,0:T(8,128)(2,1)S(1)} %copy-done.4, bf16[8,256,64]{2,1,0:T(8,128)(2,1)S(1)} %spread.1.after, ...), custom_call_target="tpu_custom_call" | custom-call | flops 201326592 | bytes 1572864 | tf_op jit(solution)/shard_map/partial/pallas_call | solution.py:285
  25.6 1.9 %collective-permute-done.12.refs_1_ = bf16[64,512]{1,0:T(8,128)(2,1)S(1)} collective-permute-done((bf16[64,512]{1,0:T(8,128)(2,1)S(1)}, bf16[64,512]{1,0:T(8,128)(2,1)S(1)}, u32[]{:S(2)}, u32[]{:S(2)}) %collective-permute-start.12) | collective-permute-done | bytes 65568 | tf_op jit(solution)/shard_map/ppermute | solution.py:35
  27.4 0.0 collective-permute-done.11.refs_0_
  27.4 0.2 collective-permute-done.13.refs_2_
  27.6 0.0 copy-done.1
  27.6 0.6 %final_sent.1 = (bf16[64,512]{1,0:T(8,128)(2,1)S(1)}, bf16[64,512]{1,0:T(8,128)(2,1)S(1)}, bf16[64,512]{1,0:T(8,128)(2,1)S(1)}) custom-call(bf16[64,512]{1,0:T(8,128)(2,1)S(1)} %get-tuple-element.51.mine.first, f32[256,512]{1,0:T(8,128)S(1)} %partial.1.part, bf16[8,256,64]{2,1,0:T(8,128)(2,1)S(1)} %spread.1.after, bf16[512,512]{1,0:T(8,128)(2,1)S(1)} %copy-done.1, ...), custom_call_target="tpu_custom_call" | custom-call | flops 100663296 | bytes 1179648 | tf_op jit(solution)/shard_map/final_sent/pallas_call | solution.py:297
  28.2 0.1 collective-permute-start.14
  28.3 1.6 %collective-permute-start.15 = (bf16[64,512]{1,0:T(8,128)(2,1)S(1)}, bf16[64,512]{1,0:T(8,128)(2,1)S(1)}, u32[]{:S(2)}, u32[]{:S(2)}) collective-permute-start(bf16[64,512]{1,0:T(8,128)(2,1)S(1)} %get-tuple-element.59.refs_6_), channel_id=1, source_target_pairs={{0,2},{1,3},{2,0},{3,1},{4,6},{5,7},{6,4},{7,5},{8,10},{9,11},{10,... | collective-permute-start | bytes 196616 | tf_op jit(solution)/shard_map/ppermute | solution.py:35
  29.9 0.3 collective-permute-start.16
  30.2 0.4 %final_kept.1.refs_4_.refs_0_ = bf16[64,512]{1,0:T(8,128)(2,1)S(1)} custom-call(bf16[64,512]{1,0:T(8,128)(2,1)S(1)} %get-tuple-element.58.first.refs_5_, f32[256,512]{1,0:T(8,128)S(1)} %partial.1.part, bf16[8,256,64]{2,1,0:T(8,128)(2,1)S(1)} %spread.1.after, bf16[512,512]{1,0:T(8,128)(2,1)S(1)} %copy-done.1, ...), custom_call_target="tpu_custom_call" | custom-call | flops 33554432 | bytes 393216 | tf_op jit(solution)/shard_map/final_kept/pallas_call | solution.py:297
  30.6 1.0 %prepare.1 = (bf16[1024,512]{1,0:T(8,128)(2,1)S(1)}, bf16[1024,256]{1,0:T(8,128)(2,1)S(1)}, bf16[256,512]{1,0:T(8,128)(2,1)}) custom-call(bf16[1024,512]{1,0:T(8,128)(2,1)S(1)} %load.1.history, s32[1,256]{1,0:T(1,128)S(1)} %get-tuple-element.42.refs_0_, s32[1,256]{1,0:T(1,128)S(1)} %collective-permute-done.refs_1_, ...), custom_call_target="tpu_custom_call" | custom-call | flops 2097152 | bytes 3145728 | tf_op jit(solution)/shard_map/prepare/pallas_call | solution.py:313
  31.5 0.0 collective-permute-done.14.refs_1_
  31.6 1.2 %collective-permute-done.15.refs_2_ = bf16[64,512]{1,0:T(8,128)(2,1)S(1)} collective-permute-done((bf16[64,512]{1,0:T(8,128)(2,1)S(1)}, bf16[64,512]{1,0:T(8,128)(2,1)S(1)}, u32[]{:S(2)}, u32[]{:S(2)}) %collective-permute-start.15) | collective-permute-done | bytes 65568 | tf_op jit(solution)/shard_map/ppermute | solution.py:35
  32.8 1.1 %collective-permute-done.16.refs_3_ = bf16[64,512]{1,0:T(8,128)(2,1)S(1)} collective-permute-done((bf16[64,512]{1,0:T(8,128)(2,1)S(1)}, bf16[64,512]{1,0:T(8,128)(2,1)S(1)}, u32[]{:S(2)}, u32[]{:S(2)}) %collective-permute-start.16) | collective-permute-done | bytes 65568 | tf_op jit(solution)/shard_map/ppermute | solution.py:35
  33.9 1.2 %scatter.1 = bf16[1024,512]{1,0:T(8,128)(2,1)} custom-call(bf16[1024,512]{1,0:T(8,128)(2,1)S(1)} %get-tuple-element.62.base, bf16[1024,256]{1,0:T(8,128)(2,1)S(1)} %get-tuple-element.63.hot, bf16[64,512]{1,0:T(8,128)(2,1)S(1)} %final_kept.1.refs_4_.refs_0_, bf16[64,512]{1,0:T(8,128)(2,1)S(1)} %collective-permute-done.14.refs_1_, ...), custom_call_target="tpu_custom_call" | custom-call | tf_op jit(solution)/shard_map/scatter/pallas_call | solution.py:325
  (6 shorter events, 0.0 us)
Async XLA Ops:
  0.6 18.5 %collective-permute-start.6 = (bf16[256,512]{1,0:T(8,128)(2,1)}, bf16[256,512]{1,0:T(8,128)(2,1)S(1)}, u32[]{:S(2)}, u32[]{:S(2)}) collective-permute-start(bf16[256,512]{1,0:T(8,128)(2,1)} %hidden.5), channel_id=1, source_target_pairs={{0,16},{4,20},{8,24},{12,28},{16,0},{20,4},{24,8},{28,12},{1,17},{... | collective-permute-start | bytes 786440 | tf_op jit(solution)/shard_map/ppermute | solution.py:35
  4.7 0.7 %copy-start.10 = (s32[1,4]{1,0:T(1,128)S(1)}, s32[1,4]{1,0:T(1,128)}, u32[]{:S(2)}) copy-start(s32[1,4]{1,0:T(1,128)} %count.1) | copy-start | bytes 52
  4.7 0.7 %copy-start.7 = (s32[1,4,128]{2,1,0:T(4,128)S(1)}, s32[1,4,128]{2,1,0:T(4,128)}, u32[]{:S(2)}) copy-start(s32[1,4,128]{2,1,0:T(4,128)} %rows.1) | copy-start | bytes 6148
  4.8 0.7 %copy-start.8 = (s32[1,4]{1,0:T(1,128)S(1)}, s32[1,4]{1,0:T(1,128)}, u32[]{:S(2)}) copy-start(s32[1,4]{1,0:T(1,128)} %src.3) | copy-start | bytes 52
  4.8 0.7 %copy-start.9 = (s32[256]{0:T(256)S(1)}, s32[256]{0:T(256)}, u32[]{:S(2)}) copy-start(s32[256]{0:T(256)} %param.23) | copy-start | bytes 3076
  6.3 3.4 %collective-permute-start = (s32[1,256]{1,0:T(1,128)S(1)}, s32[1,256]{1,0:T(1,128)S(1)}, u32[]{:S(2)}, u32[]{:S(2)}) collective-permute-start(s32[1,256]{1,0:T(1,128)S(1)} %get-tuple-element.34), channel_id=1, source_target_pairs={{0,1},{1,0},{2,3},{3,2},{4,5},{5,4},{6,7},{7,6},{8,9},{9,8},{10,11... | collective-permute-start | bytes 3080 | tf_op jit(solution)/shard_map/ppermute | solution.py:35
  6.4 4.9 %collective-permute-start.1 = (s32[1,256]{1,0:T(1,128)S(1)}, s32[1,256]{1,0:T(1,128)S(1)}, u32[]{:S(2)}, u32[]{:S(2)}) collective-permute-start(s32[1,256]{1,0:T(1,128)S(1)} %get-tuple-element.35), channel_id=1, source_target_pairs={{0,2},{1,3},{2,0},{3,1},{4,6},{5,7},{6,4},{7,5},{8,10},{9,11},{10,... | collective-permute-start | bytes 3080 | tf_op jit(solution)/shard_map/ppermute | solution.py:35
  7.9 7.3 %collective-permute-start.2 = (s32[1,256]{1,0:T(1,128)S(1)}, s32[1,256]{1,0:T(1,128)S(1)}, u32[]{:S(2)}, u32[]{:S(2)}) collective-permute-start(s32[1,256]{1,0:T(1,128)S(1)} %get-tuple-element.36), channel_id=1, source_target_pairs={{0,3},{1,2},{2,1},{3,0},{4,7},{5,6},{6,5},{7,4},{8,11},{9,10},{10,... | collective-permute-start | bytes 3080 | tf_op jit(solution)/shard_map/ppermute | solution.py:35
  8.2 7.1 %collective-permute-start.3 = (s32[1,256]{1,0:T(1,128)S(1)}, s32[1,256]{1,0:T(1,128)S(1)}, u32[]{:S(2)}, u32[]{:S(2)}) collective-permute-start(s32[1,256]{1,0:T(1,128)S(1)} %get-tuple-element.38), channel_id=1, source_target_pairs={{0,4},{4,0},{8,12},{12,8},{16,20},{20,16},{24,28},{28,24},{1,5},{5... | collective-permute-start | bytes 3080 | tf_op jit(solution)/shard_map/ppermute | solution.py:35
  9.7 2.8 %copy-start.11 = (s32[1,4]{1,0:T(1,128)S(1)}, s32[1,4]{1,0:T(1,128)}, u32[]{:S(2)}) copy-start(s32[1,4]{1,0:T(1,128)} %dst.1) | copy-start | bytes 52
  9.7 5.6 %collective-permute-start.4 = (s32[1,256]{1,0:T(1,128)S(1)}, s32[1,256]{1,0:T(1,128)S(1)}, u32[]{:S(2)}, u32[]{:S(2)}) collective-permute-start(s32[1,256]{1,0:T(1,128)S(1)} %get-tuple-element.39), channel_id=1, source_target_pairs={{0,8},{4,12},{8,0},{12,4},{16,24},{20,28},{24,16},{28,20},{1,9},{5... | collective-permute-start | bytes 3080 | tf_op jit(solution)/shard_map/ppermute | solution.py:35
  11.3 4.5 %collective-permute-start.5 = (s32[1,256]{1,0:T(1,128)S(1)}, s32[1,256]{1,0:T(1,128)S(1)}, u32[]{:S(2)}, u32[]{:S(2)}) collective-permute-start(s32[1,256]{1,0:T(1,128)S(1)} %get-tuple-element.40), channel_id=1, source_target_pairs={{0,12},{4,8},{8,4},{12,0},{16,28},{20,24},{24,20},{28,16},{1,13},{... | collective-permute-start | bytes 3080 | tf_op jit(solution)/shard_map/ppermute | solution.py:35
  12.5 0.8 %copy-start.6 = (bf16[4,64,64]{2,1,0:T(8,128)(2,1)S(1)}, bf16[4,64,64]{2,1,0:T(8,128)(2,1)}, u32[]{:S(2)}) copy-start(bf16[4,64,64]{2,1,0:T(8,128)(2,1)} %tiles.1) | copy-start | bytes 98308
  14.0 1.2 %copy-start.2 = (bf16[1024,512]{1,0:T(8,128)(2,1)S(1)}, bf16[1024,512]{1,0:T(8,128)(2,1)}, u32[]{:S(2)}) copy-start(bf16[1024,512]{1,0:T(8,128)(2,1)} %history.1) | copy-start | bytes 3145732
  15.8 2.7 %copy-start = (bf16[256,512]{1,0:T(8,128)(2,1)S(1)}, bf16[256,512]{1,0:T(8,128)(2,1)}, u32[]{:S(2)}) copy-start(bf16[256,512]{1,0:T(8,128)(2,1)} %hidden.5) | copy-start | bytes 786436
  16.6 2.5 %collective-permute-start.7 = (bf16[128,512]{1,0:T(8,128)(2,1)S(1)}, bf16[128,512]{1,0:T(8,128)(2,1)S(1)}, u32[]{:S(2)}, u32[]{:S(2)}) collective-permute-start(bf16[128,512]{1,0:T(8,128)(2,1)S(1)} %get-tuple-element.46), channel_id=1, source_target_pairs={{0,1},{1,0},{2,3},{3,2},{4,5},{5,4},{6,7},{7,6},{8,9},{9,8},{10,11... | collective-permute-start | bytes 393224 | tf_op jit(solution)/shard_map/ppermute | solution.py:35
  16.6 6.8 %collective-permute-start.8 = (bf16[128,512]{1,0:T(8,128)(2,1)S(1)}, bf16[128,512]{1,0:T(8,128)(2,1)S(1)}, u32[]{:S(2)}, u32[]{:S(2)}) collective-permute-start(bf16[128,512]{1,0:T(8,128)(2,1)S(1)} %get-tuple-element.53), channel_id=1, source_target_pairs={{0,2},{1,3},{2,0},{3,1},{4,6},{5,7},{6,4},{7,5},{8,10},{9,11},{10,... | collective-permute-start | bytes 393224 | tf_op jit(solution)/shard_map/ppermute | solution.py:35
  18.2 6.7 %collective-permute-start.9 = (bf16[128,512]{1,0:T(8,128)(2,1)S(1)}, bf16[128,512]{1,0:T(8,128)(2,1)S(1)}, u32[]{:S(2)}, u32[]{:S(2)}) collective-permute-start(bf16[128,512]{1,0:T(8,128)(2,1)S(1)} %get-tuple-element.54), channel_id=1, source_target_pairs={{0,3},{1,2},{2,1},{3,0},{4,7},{5,6},{6,5},{7,4},{8,11},{9,10},{10,... | collective-permute-start | bytes 393224 | tf_op jit(solution)/shard_map/ppermute | solution.py:35
  18.6 6.3 %copy-start.3 = (bf16[256,512]{1,0:T(8,128)(2,1)S(1)}, bf16[256,512]{1,0:T(8,128)(2,1)}, u32[]{:S(2)}) copy-start(bf16[256,512]{1,0:T(8,128)(2,1)} %pull_adj.1) | copy-start | bytes 786436
  18.6 6.3 %copy-start.4 = (bf16[256,512]{1,0:T(8,128)(2,1)S(1)}, bf16[256,512]{1,0:T(8,128)(2,1)}, u32[]{:S(2)}) copy-start(bf16[256,512]{1,0:T(8,128)(2,1)} %initial.1) | copy-start | bytes 786436
  18.6 6.3 %copy-start.5 = (bf16[256,256]{1,0:T(8,128)(2,1)S(1)}, bf16[256,256]{1,0:T(8,128)(2,1)}, u32[]{:S(2)}) copy-start(bf16[256,256]{1,0:T(8,128)(2,1)} %own_adj.1) | copy-start | bytes 393220
  18.6 4.4 %collective-permute-start.10 = (bf16[64,512]{1,0:T(8,128)(2,1)S(1)}, bf16[64,512]{1,0:T(8,128)(2,1)S(1)}, u32[]{:S(2)}, u32[]{:S(2)}) collective-permute-start(bf16[64,512]{1,0:T(8,128)(2,1)S(1)} %pick_own.1), channel_id=1, source_target_pairs={{0,8},{4,12},{8,0},{12,4},{16,24},{20,28},{24,16},{28,20},{1,9},{5... | collective-permute-start | bytes 196616 | tf_op jit(solution)/shard_map/ppermute | solution.py:35
  19.3 8.2 %collective-permute-start.11 = (bf16[128,512]{1,0:T(8,128)(2,1)S(1)}, bf16[128,512]{1,0:T(8,128)(2,1)S(1)}, u32[]{:S(2)}, u32[]{:S(2)}) collective-permute-start(bf16[128,512]{1,0:T(8,128)(2,1)S(1)} %get-tuple-element.55), channel_id=1, source_target_pairs={{0,4},{4,0},{8,12},{12,8},{16,20},{20,16},{24,28},{28,24},{1,5},{5... | collective-permute-start | bytes 393224 | tf_op jit(solution)/shard_map/ppermute | solution.py:35
  20.7 6.9 %collective-permute-start.13 = (bf16[128,512]{1,0:T(8,128)(2,1)S(1)}, bf16[128,512]{1,0:T(8,128)(2,1)S(1)}, u32[]{:S(2)}, u32[]{:S(2)}) collective-permute-start(bf16[128,512]{1,0:T(8,128)(2,1)S(1)} %get-tuple-element.57), channel_id=1, source_target_pairs={{0,12},{4,8},{8,4},{12,0},{16,28},{20,24},{24,20},{28,16},{1,13},{... | collective-permute-start | bytes 393224 | tf_op jit(solution)/shard_map/ppermute | solution.py:35
  23.0 4.4 %collective-permute-start.12 = (bf16[64,512]{1,0:T(8,128)(2,1)S(1)}, bf16[64,512]{1,0:T(8,128)(2,1)S(1)}, u32[]{:S(2)}, u32[]{:S(2)}) collective-permute-start(bf16[64,512]{1,0:T(8,128)(2,1)S(1)} %get-tuple-element.56), channel_id=1, source_target_pairs={{0,8},{4,12},{8,0},{12,4},{16,24},{20,28},{24,16},{28,20},{1,9},{5... | collective-permute-start | bytes 196616 | tf_op jit(solution)/shard_map/ppermute | solution.py:35
  24.9 2.7 %copy-start.1 = (bf16[512,512]{1,0:T(8,128)(2,1)S(1)}, bf16[512,512]{1,0:T(8,128)(2,1)}, u32[]{:S(2)}) copy-start(bf16[512,512]{1,0:T(8,128)(2,1)} %weight.3) | copy-start | bytes 1572868
  28.2 3.3 %collective-permute-start.14 = (bf16[64,512]{1,0:T(8,128)(2,1)S(1)}, bf16[64,512]{1,0:T(8,128)(2,1)S(1)}, u32[]{:S(2)}, u32[]{:S(2)}) collective-permute-start(bf16[64,512]{1,0:T(8,128)(2,1)S(1)} %get-tuple-element.58.first.refs_5_), channel_id=1, source_target_pairs={{0,1},{1,0},{2,3},{3,2},{4,5},{5,4},{6,7},{7,6},{8,9},{9,8},{10,11... | collective-permute-start | bytes 196616 | tf_op jit(solution)/shard_map/ppermute | solution.py:35
  28.3 4.5 %collective-permute-start.15 = (bf16[64,512]{1,0:T(8,128)(2,1)S(1)}, bf16[64,512]{1,0:T(8,128)(2,1)S(1)}, u32[]{:S(2)}, u32[]{:S(2)}) collective-permute-start(bf16[64,512]{1,0:T(8,128)(2,1)S(1)} %get-tuple-element.59.refs_6_), channel_id=1, source_target_pairs={{0,2},{1,3},{2,0},{3,1},{4,6},{5,7},{6,4},{7,5},{8,10},{9,11},{10,... | collective-permute-start | bytes 196616 | tf_op jit(solution)/shard_map/ppermute | solution.py:35
  29.9 4.0 %collective-permute-start.16 = (bf16[64,512]{1,0:T(8,128)(2,1)S(1)}, bf16[64,512]{1,0:T(8,128)(2,1)S(1)}, u32[]{:S(2)}, u32[]{:S(2)}) collective-permute-start(bf16[64,512]{1,0:T(8,128)(2,1)S(1)} %get-tuple-element.60.refs_7_), channel_id=1, source_target_pairs={{0,3},{1,2},{2,1},{3,0},{4,7},{5,6},{6,5},{7,4},{8,11},{9,10},{10,... | collective-permute-start | bytes 196616 | tf_op jit(solution)/shard_map/ppermute | solution.py:35

commit v5 on v4

--- a/solution.py
+++ b/solution.py
@@ -35,21 +35,23 @@
     return lax.ppermute(x, axis, [(i, i ^ k) for i in range(n)])
 
 
-def message_kernel(n_hist, n_half, per_dev, place, src, count, rows, push, *outs):
+def message_kernel(n_hist, n_half, per_dev, after, src, count, rows, push, *outs):
     to_hist, to_half = outs[:n_hist], outs[n_hist:]
     cap = rows.shape[2]
     per_owner = push.shape[1] // n_hist
-    b, h = place[0], place[1]
+    b, h = lax.axis_index("blk"), lax.axis_index("hist")
+    name = lax.div(src[...], per_dev) ^ b
+    local = lax.rem(src[...], per_dev)
     for k in range(n_half):
-        for slot, name in enumerate((k + n_half, k)):
-            wanted = 0
-            for t in range(src.shape[1]):
-                wanted = jnp.where((src[0, t] // per_dev) ^ b == name, src[0, t] % per_dev, wanted)
-            to_half[k][:, slot * 128 : slot * 128 + 128] = jnp.full((1, 128), wanted, jnp.int32)
+        for slot, wanted in enumerate((k + n_half, k)):
+            found = jnp.sum(jnp.where(name == wanted, local, 0), axis=1, keepdims=True)
+            to_half[k][:, slot * 128 : slot * 128 + 128] = jnp.broadcast_to(found, (1, 128))
+    owner = lax.broadcasted_iota(jnp.int32, count.shape, 1)
     lane = lax.broadcasted_iota(jnp.int32, (1, cap), 1)
     for k in range(n_hist):
         o = h ^ k
-        to_hist[k][:, :cap] = jnp.where(lane < count[0, o], rows[0, pl.ds(o, 1), :], -1)
+        used = jnp.sum(jnp.where(owner == o, count[...], 0), axis=1, keepdims=True)
+        to_hist[k][:, :cap] = jnp.where(lane < used, rows[0, pl.ds(o, 1), :], -1)
         pushed = push[:, :per_owner]
         for j in range(1, n_hist):
             pushed = jnp.where(o == j, push[:, j * per_owner : (j + 1) * per_owner], pushed)
@@ -215,7 +217,7 @@
         functools.partial(message_kernel, n_hist, n_half, per_dev),
         out_shape=[shape((1, cap + 128), jnp.int32)] * n_hist
         + [shape((1, 256), jnp.int32) for k in range(n_half)],
-        in_specs=[smem(), smem(), smem(), vmem(), vmem()],
+        in_specs=[anywhere] + [vmem()] * 4,
         out_specs=[vmem()] * (n_hist + n_half),
         compiler_params=params(),
         name="message",

time: 35.4 us -> 34.9 us (0.986)
  Pallas kernels: 6.32 us -> 5.78 us
    pallas_call x1, Pallas kernels: 0.82 us -> 0.3 us  [local(): pl.pallas_call(functools.partial(message_kernel, n_hist, n_half, per_dev)...]
  transfers between devices with their start and end apart: 17 -> 17, of which waited for: 7 -> 7; matrix products, arithmetic and copies ran while one was open for 0% -> 0% of each run, Pallas kernels for 13% -> 11%
where the time goes in v5:
time: 34.9 us; the launch traced here: 34.7 us
  starting transfers between devices  18.2 us (52%)
  waiting for transfers between devices  7.04 us (20%)
  Pallas kernels  5.78 us (17%)
  local copies, waits for them, and re-layouts  2.79 us (8%)
  between operations  0.81 us (2%)
    ppermute x17, starting transfers between devices, swap(): return lax.ppermute(x, axis, [(i, i ^ k) for i in range(n)])  18.2 us
    ppermute x17, waiting for transfers between devices, swap(): return lax.ppermute(x, axis, [(i, i ^ k) for i in range(n)])  7.04 us
    unnamed x24, local copies, waits for them, and re-layouts  2.79 us
    pallas_call x1, Pallas kernels, local(): pl.pallas_call(functools.partial(scatter_kernel, steps), out_shape=shape(...  1.23 us
    pallas_call x2, Pallas kernels, final(): pl.pallas_call(functools.partial(final_kernel, n_half, chunks), out_shape...  1 us
    pallas_call x1, Pallas kernels, local(): pl.pallas_call(functools.partial(prepare_kernel, n_hist, cap), out_shape=...  0.98 us
    pallas_call x1, Pallas kernels, local(): pl.pallas_call(functools.partial(pull_kernel, n_hist, cap), out_shape=[sh...  0.74 us
  transfers between devices with their start and end apart: 17, of which 7 were waited for; matrix products, arithmetic and copies ran while one was open for 0% of the time, Pallas kernels for 11%

profile of v5, /device:TPU:0, one launch (start us, length us, event | category | flops | bytes accessed | tf_op | source)
XLA Modules:
  0.0 34.7 jit_solution(653916098752755601)
XLA Ops:
  0.6 4.1 %collective-permute-start.6 = (bf16[256,512]{1,0:T(8,128)(2,1)}, bf16[256,512]{1,0:T(8,128)(2,1)S(1)}, u32[]{:S(2)}, u32[]{:S(2)}) collective-permute-start(bf16[256,512]{1,0:T(8,128)(2,1)} %hidden.5), channel_id=1, source_target_pairs={{0,16},{4,20},{8,24},{12,28},{16,0},{20,4},{24,8},{28,12},{1,17},{... | collective-permute-start | bytes 786440 | tf_op jit(solution)/shard_map/ppermute | solution.py:35
  4.7 0.0 copy-start.10
  4.7 0.1 pad_add_fusion.after.place
  4.8 0.6 %copy-done.10 = s32[1,4]{1,0:T(1,128)S(1)} copy-done((s32[1,4]{1,0:T(1,128)S(1)}, s32[1,4]{1,0:T(1,128)}, u32[]{:S(2)}) %copy-start.10) | copy-done | bytes 40
  5.4 0.0 copy-done.7
  5.4 0.0 copy-done.8
  5.5 0.0 copy-done.9
  5.5 0.3 message.1
  5.8 0.0 collective-permute-start
  5.9 1.6 %collective-permute-start.1 = (s32[1,256]{1,0:T(1,128)S(1)}, s32[1,256]{1,0:T(1,128)S(1)}, u32[]{:S(2)}, u32[]{:S(2)}) collective-permute-start(s32[1,256]{1,0:T(1,128)S(1)} %get-tuple-element.35), channel_id=1, source_target_pairs={{0,2},{1,3},{2,0},{3,1},{4,6},{5,7},{6,4},{7,5},{8,10},{9,11},{10,... | collective-permute-start | bytes 3080 | tf_op jit(solution)/shard_map/ppermute | solution.py:35
  7.4 0.3 collective-permute-start.2
  7.7 1.5 %collective-permute-start.3 = (s32[1,256]{1,0:T(1,128)S(1)}, s32[1,256]{1,0:T(1,128)S(1)}, u32[]{:S(2)}, u32[]{:S(2)}) collective-permute-start(s32[1,256]{1,0:T(1,128)S(1)} %get-tuple-element.38), channel_id=1, source_target_pairs={{0,4},{4,0},{8,12},{12,8},{16,20},{20,16},{24,28},{28,24},{1,5},{5... | collective-permute-start | bytes 3080 | tf_op jit(solution)/shard_map/ppermute | solution.py:35
  9.2 0.0 collective-permute-done.refs_1_
  9.2 1.6 %collective-permute-start.4 = (s32[1,256]{1,0:T(1,128)S(1)}, s32[1,256]{1,0:T(1,128)S(1)}, u32[]{:S(2)}, u32[]{:S(2)}) collective-permute-start(s32[1,256]{1,0:T(1,128)S(1)} %get-tuple-element.39), channel_id=1, source_target_pairs={{0,8},{4,12},{8,0},{12,4},{16,24},{20,28},{24,16},{28,20},{1,9},{5... | collective-permute-start | bytes 3080 | tf_op jit(solution)/shard_map/ppermute | solution.py:35
  10.8 0.0 collective-permute-done.1.refs_2_
  10.8 1.2 %collective-permute-start.5 = (s32[1,256]{1,0:T(1,128)S(1)}, s32[1,256]{1,0:T(1,128)S(1)}, u32[]{:S(2)}, u32[]{:S(2)}) collective-permute-start(s32[1,256]{1,0:T(1,128)S(1)} %get-tuple-element.40), channel_id=1, source_target_pairs={{0,12},{4,8},{8,4},{12,0},{16,28},{20,24},{24,20},{28,16},{1,13},{... | collective-permute-start | bytes 3080 | tf_op jit(solution)/shard_map/ppermute | solution.py:35
  12.0 0.0 copy-done.11
  12.0 0.8 %copy-done.6 = bf16[4,64,64]{2,1,0:T(8,128)(2,1)S(1)} copy-done((bf16[4,64,64]{2,1,0:T(8,128)(2,1)S(1)}, bf16[4,64,64]{2,1,0:T(8,128)(2,1)}, u32[]{:S(2)}) %copy-start.6) | copy-done | bytes 32792
  12.8 0.6 %spread.1.after = bf16[8,256,64]{2,1,0:T(8,128)(2,1)S(1)} custom-call(s32[2]{0:T(128)S(1)} %pad_add_fusion.after.place, s32[1,4]{1,0:T(1,128)S(1)} %copy-done.8, s32[1,4]{1,0:T(1,128)S(1)} %copy-done.11, bf16[4,64,64]{2,1,0:T(8,128)(2,1)S(1)} %copy-done.6), custom_call_target="tpu_custom_call" | custom-call | bytes 262144 | tf_op jit(solution)/shard_map/spread/pallas_call | solution.py:227
  13.5 0.0 copy-start.2
  13.5 1.2 %copy-done.2 = bf16[1024,512]{1,0:T(8,128)(2,1)S(1)} copy-done((bf16[1024,512]{1,0:T(8,128)(2,1)S(1)}, bf16[1024,512]{1,0:T(8,128)(2,1)}, u32[]{:S(2)}) %copy-start.2) | copy-done | bytes 1048600
  14.7 0.1 load.1.history
  14.8 0.0 collective-permute-done.2.refs_3_
  14.8 0.0 collective-permute-done.3.refs_1_
  14.8 0.0 collective-permute-done.4.refs_2_.refs_0_
  14.8 0.5 %collective-permute-done.5.refs_3_ = s32[1,256]{1,0:T(1,128)S(1)} collective-permute-done((s32[1,256]{1,0:T(1,128)S(1)}, s32[1,256]{1,0:T(1,128)S(1)}, u32[]{:S(2)}, u32[]{:S(2)}) %collective-permute-start.5) | collective-permute-done | bytes 1056 | tf_op jit(solution)/shard_map/ppermute | solution.py:35
  15.3 0.7 %pull.1 = (bf16[128,512]{1,0:T(8,128)(2,1)S(1)}, bf16[128,512]{1,0:T(8,128)(2,1)S(1)}, bf16[128,512]{1,0:T(8,128)(2,1)S(1)}, bf16[128,512]{1,0:T(8,128)(2,1)S(1)}) custom-call(bf16[1024,512]{1,0:T(8,128)(2,1)S(1)} %load.1.history, s32[1,256]{1,0:T(1,128)S(1)} %get-tuple-element.42.refs_0_, s32[1,256]{1,0:T(1,128)S(1)} %collective-permute-done.refs_1_, ...), custom_call_target="tpu_custom_call" | custom-call | flops 536870912 | bytes 2097152 | tf_op jit(solution)/shard_map/pull/pallas_call | solution.py:248
  16.1 0.1 collective-permute-start.7
  16.1 1.6 %collective-permute-start.8 = (bf16[128,512]{1,0:T(8,128)(2,1)S(1)}, bf16[128,512]{1,0:T(8,128)(2,1)S(1)}, u32[]{:S(2)}, u32[]{:S(2)}) collective-permute-start(bf16[128,512]{1,0:T(8,128)(2,1)S(1)} %get-tuple-element.53), channel_id=1, source_target_pairs={{0,2},{1,3},{2,0},{3,1},{4,6},{5,7},{6,4},{7,5},{8,10},{9,11},{10,... | collective-permute-start | bytes 393224 | tf_op jit(solution)/shard_map/ppermute | solution.py:35
  17.7 0.3 collective-permute-start.9
  18.0 0.0 copy-done
  18.0 0.1 pick_own.1
  18.1 0.0 copy-start.3
  18.1 0.0 copy-start.4
  18.1 0.0 copy-start.5
  18.1 0.5 %collective-permute-start.10 = (bf16[64,512]{1,0:T(8,128)(2,1)S(1)}, bf16[64,512]{1,0:T(8,128)(2,1)S(1)}, u32[]{:S(2)}, u32[]{:S(2)}) collective-permute-start(bf16[64,512]{1,0:T(8,128)(2,1)S(1)} %pick_own.1), channel_id=1, source_target_pairs={{0,8},{4,12},{8,0},{12,4},{16,24},{20,28},{24,16},{28,20},{1,9},{5... | collective-permute-start | bytes 196616 | tf_op jit(solution)/shard_map/ppermute | solution.py:35
  18.6 0.0 collective-permute-done.7.after.refs_1_
  18.6 0.0 collective-permute-done.6.far
  18.6 0.1 pick_far.1
  18.8 1.5 %collective-permute-start.11 = (bf16[128,512]{1,0:T(8,128)(2,1)S(1)}, bf16[128,512]{1,0:T(8,128)(2,1)S(1)}, u32[]{:S(2)}, u32[]{:S(2)}) collective-permute-start(bf16[128,512]{1,0:T(8,128)(2,1)S(1)} %get-tuple-element.55), channel_id=1, source_target_pairs={{0,4},{4,0},{8,12},{12,8},{16,20},{20,16},{24,28},{28,24},{1,5},{5... | collective-permute-start | bytes 393224 | tf_op jit(solution)/shard_map/ppermute | solution.py:35
  20.2 1.7 %collective-permute-start.13 = (bf16[128,512]{1,0:T(8,128)(2,1)S(1)}, bf16[128,512]{1,0:T(8,128)(2,1)S(1)}, u32[]{:S(2)}, u32[]{:S(2)}) collective-permute-start(bf16[128,512]{1,0:T(8,128)(2,1)S(1)} %get-tuple-element.57), channel_id=1, source_target_pairs={{0,12},{4,8},{8,4},{12,0},{16,28},{20,24},{24,20},{28,16},{1,13},{... | collective-permute-start | bytes 393224 | tf_op jit(solution)/shard_map/ppermute | solution.py:35
  21.9 0.6 %collective-permute-done.10.refs_4_ = bf16[64,512]{1,0:T(8,128)(2,1)S(1)} collective-permute-done((bf16[64,512]{1,0:T(8,128)(2,1)S(1)}, bf16[64,512]{1,0:T(8,128)(2,1)S(1)}, u32[]{:S(2)}, u32[]{:S(2)}) %collective-permute-start.10) | collective-permute-done | bytes 65568 | tf_op jit(solution)/shard_map/ppermute | solution.py:35
  22.5 0.4 %collective-permute-start.12 = (bf16[64,512]{1,0:T(8,128)(2,1)S(1)}, bf16[64,512]{1,0:T(8,128)(2,1)S(1)}, u32[]{:S(2)}, u32[]{:S(2)}) collective-permute-start(bf16[64,512]{1,0:T(8,128)(2,1)S(1)} %get-tuple-element.56), channel_id=1, source_target_pairs={{0,8},{4,12},{8,0},{12,4},{16,24},{20,28},{24,16},{28,20},{1,9},{5... | collective-permute-start | bytes 196616 | tf_op jit(solution)/shard_map/ppermute | solution.py:35
  22.9 0.0 collective-permute-done.8.refs_2_
  22.9 1.5 %collective-permute-done.9.refs_3_ = bf16[128,512]{1,0:T(8,128)(2,1)S(1)} collective-permute-done((bf16[128,512]{1,0:T(8,128)(2,1)S(1)}, bf16[128,512]{1,0:T(8,128)(2,1)S(1)}, u32[]{:S(2)}, u32[]{:S(2)}) %collective-permute-start.9) | collective-permute-done | bytes 131104 | tf_op jit(solution)/shard_map/ppermute | solution.py:35
  24.4 0.0 copy-done.3
  24.4 0.0 copy-done.4
  24.4 0.0 copy-done.5
  24.4 0.0 copy-start.1
  24.4 0.6 %partial.1.part = f32[256,512]{1,0:T(8,128)S(1)} custom-call(bf16[256,256]{1,0:T(8,128)(2,1)S(1)} %copy-done.5, bf16[256,512]{1,0:T(8,128)(2,1)S(1)} %copy-done, bf16[256,512]{1,0:T(8,128)(2,1)S(1)} %copy-done.3, bf16[256,512]{1,0:T(8,128)(2,1)S(1)} %copy-done.4, bf16[8,256,64]{2,1,0:T(8,128)(2,1)S(1)} %spread.1.after, ...), custom_call_target="tpu_custom_call" | custom-call | flops 201326592 | bytes 1572864 | tf_op jit(solution)/shard_map/partial/pallas_call | solution.py:287
  25.1 1.9 %collective-permute-done.12.refs_1_ = bf16[64,512]{1,0:T(8,128)(2,1)S(1)} collective-permute-done((bf16[64,512]{1,0:T(8,128)(2,1)S(1)}, bf16[64,512]{1,0:T(8,128)(2,1)S(1)}, u32[]{:S(2)}, u32[]{:S(2)}) %collective-permute-start.12) | collective-permute-done | bytes 65568 | tf_op jit(solution)/shard_map/ppermute | solution.py:35
  26.9 0.0 collective-permute-done.11.refs_0_
  26.9 0.2 collective-permute-done.13.refs_2_
  27.1 0.0 copy-done.1
  27.1 0.6 %final_sent.1 = (bf16[64,512]{1,0:T(8,128)(2,1)S(1)}, bf16[64,512]{1,0:T(8,128)(2,1)S(1)}, bf16[64,512]{1,0:T(8,128)(2,1)S(1)}) custom-call(bf16[64,512]{1,0:T(8,128)(2,1)S(1)} %get-tuple-element.51.mine.first, f32[256,512]{1,0:T(8,128)S(1)} %partial.1.part, bf16[8,256,64]{2,1,0:T(8,128)(2,1)S(1)} %spread.1.after, bf16[512,512]{1,0:T(8,128)(2,1)S(1)} %copy-done.1, ...), custom_call_target="tpu_custom_call" | custom-call | flops 100663296 | bytes 1179648 | tf_op jit(solution)/shard_map/final_sent/pallas_call | solution.py:299
  27.7 0.1 collective-permute-start.14
  27.8 1.6 %collective-permute-start.15 = (bf16[64,512]{1,0:T(8,128)(2,1)S(1)}, bf16[64,512]{1,0:T(8,128)(2,1)S(1)}, u32[]{:S(2)}, u32[]{:S(2)}) collective-permute-start(bf16[64,512]{1,0:T(8,128)(2,1)S(1)} %get-tuple-element.59.refs_6_), channel_id=1, source_target_pairs={{0,2},{1,3},{2,0},{3,1},{4,6},{5,7},{6,4},{7,5},{8,10},{9,11},{10,... | collective-permute-start | bytes 196616 | tf_op jit(solution)/shard_map/ppermute | solution.py:35
  29.4 0.3 collective-permute-start.16
  29.7 0.4 %final_kept.1.refs_4_.refs_0_ = bf16[64,512]{1,0:T(8,128)(2,1)S(1)} custom-call(bf16[64,512]{1,0:T(8,128)(2,1)S(1)} %get-tuple-element.58.first.refs_5_, f32[256,512]{1,0:T(8,128)S(1)} %partial.1.part, bf16[8,256,64]{2,1,0:T(8,128)(2,1)S(1)} %spread.1.after, bf16[512,512]{1,0:T(8,128)(2,1)S(1)} %copy-done.1, ...), custom_call_target="tpu_custom_call" | custom-call | flops 33554432 | bytes 393216 | tf_op jit(solution)/shard_map/final_kept/pallas_call | solution.py:299
  30.1 1.0 %prepare.1 = (bf16[1024,512]{1,0:T(8,128)(2,1)S(1)}, bf16[1024,256]{1,0:T(8,128)(2,1)S(1)}, bf16[256,512]{1,0:T(8,128)(2,1)}) custom-call(bf16[1024,512]{1,0:T(8,128)(2,1)S(1)} %load.1.history, s32[1,256]{1,0:T(1,128)S(1)} %get-tuple-element.42.refs_0_, s32[1,256]{1,0:T(1,128)S(1)} %collective-permute-done.refs_1_, ...), custom_call_target="tpu_custom_call" | custom-call | flops 2097152 | bytes 3145728 | tf_op jit(solution)/shard_map/prepare/pallas_call | solution.py:315
  31.0 0.0 collective-permute-done.14.refs_1_
  31.1 1.2 %collective-permute-done.15.refs_2_ = bf16[64,512]{1,0:T(8,128)(2,1)S(1)} collective-permute-done((bf16[64,512]{1,0:T(8,128)(2,1)S(1)}, bf16[64,512]{1,0:T(8,128)(2,1)S(1)}, u32[]{:S(2)}, u32[]{:S(2)}) %collective-permute-start.15) | collective-permute-done | bytes 65568 | tf_op jit(solution)/shard_map/ppermute | solution.py:35
  32.3 1.1 %collective-permute-done.16.refs_3_ = bf16[64,512]{1,0:T(8,128)(2,1)S(1)} collective-permute-done((bf16[64,512]{1,0:T(8,128)(2,1)S(1)}, bf16[64,512]{1,0:T(8,128)(2,1)S(1)}, u32[]{:S(2)}, u32[]{:S(2)}) %collective-permute-start.16) | collective-permute-done | bytes 65568 | tf_op jit(solution)/shard_map/ppermute | solution.py:35
  33.4 1.2 %scatter.1 = bf16[1024,512]{1,0:T(8,128)(2,1)} custom-call(bf16[1024,512]{1,0:T(8,128)(2,1)S(1)} %get-tuple-element.62.base, bf16[1024,256]{1,0:T(8,128)(2,1)S(1)} %get-tuple-element.63.hot, bf16[64,512]{1,0:T(8,128)(2,1)S(1)} %final_kept.1.refs_4_.refs_0_, bf16[64,512]{1,0:T(8,128)(2,1)S(1)} %collective-permute-done.14.refs_1_, ...), custom_call_target="tpu_custom_call" | custom-call | tf_op jit(solution)/shard_map/scatter/pallas_call | solution.py:327
  (6 shorter events, 0.0 us)
Async XLA Ops:
  0.6 18.0 %collective-permute-start.6 = (bf16[256,512]{1,0:T(8,128)(2,1)}, bf16[256,512]{1,0:T(8,128)(2,1)S(1)}, u32[]{:S(2)}, u32[]{:S(2)}) collective-permute-start(bf16[256,512]{1,0:T(8,128)(2,1)} %hidden.5), channel_id=1, source_target_pairs={{0,16},{4,20},{8,24},{12,28},{16,0},{20,4},{24,8},{28,12},{1,17},{... | collective-permute-start | bytes 786440 | tf_op jit(solution)/shard_map/ppermute | solution.py:35
  4.7 0.7 %copy-start.10 = (s32[1,4]{1,0:T(1,128)S(1)}, s32[1,4]{1,0:T(1,128)}, u32[]{:S(2)}) copy-start(s32[1,4]{1,0:T(1,128)} %count.1) | copy-start | bytes 52
  4.7 0.7 %copy-start.7 = (s32[1,4,128]{2,1,0:T(4,128)S(1)}, s32[1,4,128]{2,1,0:T(4,128)}, u32[]{:S(2)}) copy-start(s32[1,4,128]{2,1,0:T(4,128)} %rows.1) | copy-start | bytes 6148
  4.8 0.7 %copy-start.8 = (s32[1,4]{1,0:T(1,128)S(1)}, s32[1,4]{1,0:T(1,128)}, u32[]{:S(2)}) copy-start(s32[1,4]{1,0:T(1,128)} %src.3) | copy-start | bytes 52
  4.8 0.7 %copy-start.9 = (s32[256]{0:T(256)S(1)}, s32[256]{0:T(256)}, u32[]{:S(2)}) copy-start(s32[256]{0:T(256)} %param.23) | copy-start | bytes 3076
  5.8 3.4 %collective-permute-start = (s32[1,256]{1,0:T(1,128)S(1)}, s32[1,256]{1,0:T(1,128)S(1)}, u32[]{:S(2)}, u32[]{:S(2)}) collective-permute-start(s32[1,256]{1,0:T(1,128)S(1)} %get-tuple-element.34), channel_id=1, source_target_pairs={{0,1},{1,0},{2,3},{3,2},{4,5},{5,4},{6,7},{7,6},{8,9},{9,8},{10,11... | collective-permute-start | bytes 3080 | tf_op jit(solution)/shard_map/ppermute | solution.py:35
  5.9 4.9 %collective-permute-start.1 = (s32[1,256]{1,0:T(1,128)S(1)}, s32[1,256]{1,0:T(1,128)S(1)}, u32[]{:S(2)}, u32[]{:S(2)}) collective-permute-start(s32[1,256]{1,0:T(1,128)S(1)} %get-tuple-element.35), channel_id=1, source_target_pairs={{0,2},{1,3},{2,0},{3,1},{4,6},{5,7},{6,4},{7,5},{8,10},{9,11},{10,... | collective-permute-start | bytes 3080 | tf_op jit(solution)/shard_map/ppermute | solution.py:35
  7.4 7.3 %collective-permute-start.2 = (s32[1,256]{1,0:T(1,128)S(1)}, s32[1,256]{1,0:T(1,128)S(1)}, u32[]{:S(2)}, u32[]{:S(2)}) collective-permute-start(s32[1,256]{1,0:T(1,128)S(1)} %get-tuple-element.36), channel_id=1, source_target_pairs={{0,3},{1,2},{2,1},{3,0},{4,7},{5,6},{6,5},{7,4},{8,11},{9,10},{10,... | collective-permute-start | bytes 3080 | tf_op jit(solution)/shard_map/ppermute | solution.py:35
  7.7 7.1 %collective-permute-start.3 = (s32[1,256]{1,0:T(1,128)S(1)}, s32[1,256]{1,0:T(1,128)S(1)}, u32[]{:S(2)}, u32[]{:S(2)}) collective-permute-start(s32[1,256]{1,0:T(1,128)S(1)} %get-tuple-element.38), channel_id=1, source_target_pairs={{0,4},{4,0},{8,12},{12,8},{16,20},{20,16},{24,28},{28,24},{1,5},{5... | collective-permute-start | bytes 3080 | tf_op jit(solution)/shard_map/ppermute | solution.py:35
  9.2 2.8 %copy-start.11 = (s32[1,4]{1,0:T(1,128)S(1)}, s32[1,4]{1,0:T(1,128)}, u32[]{:S(2)}) copy-start(s32[1,4]{1,0:T(1,128)} %dst.1) | copy-start | bytes 52
  9.2 5.6 %collective-permute-start.4 = (s32[1,256]{1,0:T(1,128)S(1)}, s32[1,256]{1,0:T(1,128)S(1)}, u32[]{:S(2)}, u32[]{:S(2)}) collective-permute-start(s32[1,256]{1,0:T(1,128)S(1)} %get-tuple-element.39), channel_id=1, source_target_pairs={{0,8},{4,12},{8,0},{12,4},{16,24},{20,28},{24,16},{28,20},{1,9},{5... | collective-permute-start | bytes 3080 | tf_op jit(solution)/shard_map/ppermute | solution.py:35
  10.8 4.5 %collective-permute-start.5 = (s32[1,256]{1,0:T(1,128)S(1)}, s32[1,256]{1,0:T(1,128)S(1)}, u32[]{:S(2)}, u32[]{:S(2)}) collective-permute-start(s32[1,256]{1,0:T(1,128)S(1)} %get-tuple-element.40), channel_id=1, source_target_pairs={{0,12},{4,8},{8,4},{12,0},{16,28},{20,24},{24,20},{28,16},{1,13},{... | collective-permute-start | bytes 3080 | tf_op jit(solution)/shard_map/ppermute | solution.py:35
  12.0 0.8 %copy-start.6 = (bf16[4,64,64]{2,1,0:T(8,128)(2,1)S(1)}, bf16[4,64,64]{2,1,0:T(8,128)(2,1)}, u32[]{:S(2)}) copy-start(bf16[4,64,64]{2,1,0:T(8,128)(2,1)} %tiles.1) | copy-start | bytes 98308
  13.5 1.2 %copy-start.2 = (bf16[1024,512]{1,0:T(8,128)(2,1)S(1)}, bf16[1024,512]{1,0:T(8,128)(2,1)}, u32[]{:S(2)}) copy-start(bf16[1024,512]{1,0:T(8,128)(2,1)} %history.1) | copy-start | bytes 3145732
  15.3 2.7 %copy-start = (bf16[256,512]{1,0:T(8,128)(2,1)S(1)}, bf16[256,512]{1,0:T(8,128)(2,1)}, u32[]{:S(2)}) copy-start(bf16[256,512]{1,0:T(8,128)(2,1)} %hidden.5) | copy-start | bytes 786436
  16.1 2.5 %collective-permute-start.7 = (bf16[128,512]{1,0:T(8,128)(2,1)S(1)}, bf16[128,512]{1,0:T(8,128)(2,1)S(1)}, u32[]{:S(2)}, u32[]{:S(2)}) collective-permute-start(bf16[128,512]{1,0:T(8,128)(2,1)S(1)} %get-tuple-element.46), channel_id=1, source_target_pairs={{0,1},{1,0},{2,3},{3,2},{4,5},{5,4},{6,7},{7,6},{8,9},{9,8},{10,11... | collective-permute-start | bytes 393224 | tf_op jit(solution)/shard_map/ppermute | solution.py:35
  16.1 6.8 %collective-permute-start.8 = (bf16[128,512]{1,0:T(8,128)(2,1)S(1)}, bf16[128,512]{1,0:T(8,128)(2,1)S(1)}, u32[]{:S(2)}, u32[]{:S(2)}) collective-permute-start(bf16[128,512]{1,0:T(8,128)(2,1)S(1)} %get-tuple-element.53), channel_id=1, source_target_pairs={{0,2},{1,3},{2,0},{3,1},{4,6},{5,7},{6,4},{7,5},{8,10},{9,11},{10,... | collective-permute-start | bytes 393224 | tf_op jit(solution)/shard_map/ppermute | solution.py:35
  17.7 6.7 %collective-permute-start.9 = (bf16[128,512]{1,0:T(8,128)(2,1)S(1)}, bf16[128,512]{1,0:T(8,128)(2,1)S(1)}, u32[]{:S(2)}, u32[]{:S(2)}) collective-permute-start(bf16[128,512]{1,0:T(8,128)(2,1)S(1)} %get-tuple-element.54), channel_id=1, source_target_pairs={{0,3},{1,2},{2,1},{3,0},{4,7},{5,6},{6,5},{7,4},{8,11},{9,10},{10,... | collective-permute-start | bytes 393224 | tf_op jit(solution)/shard_map/ppermute | solution.py:35
  18.1 6.3 %copy-start.3 = (bf16[256,512]{1,0:T(8,128)(2,1)S(1)}, bf16[256,512]{1,0:T(8,128)(2,1)}, u32[]{:S(2)}) copy-start(bf16[256,512]{1,0:T(8,128)(2,1)} %pull_adj.1) | copy-start | bytes 786436
  18.1 6.3 %copy-start.4 = (bf16[256,512]{1,0:T(8,128)(2,1)S(1)}, bf16[256,512]{1,0:T(8,128)(2,1)}, u32[]{:S(2)}) copy-start(bf16[256,512]{1,0:T(8,128)(2,1)} %initial.1) | copy-start | bytes 786436
  18.1 6.3 %copy-start.5 = (bf16[256,256]{1,0:T(8,128)(2,1)S(1)}, bf16[256,256]{1,0:T(8,128)(2,1)}, u32[]{:S(2)}) copy-start(bf16[256,256]{1,0:T(8,128)(2,1)} %own_adj.1) | copy-start | bytes 393220
  18.1 4.4 %collective-permute-start.10 = (bf16[64,512]{1,0:T(8,128)(2,1)S(1)}, bf16[64,512]{1,0:T(8,128)(2,1)S(1)}, u32[]{:S(2)}, u32[]{:S(2)}) collective-permute-start(bf16[64,512]{1,0:T(8,128)(2,1)S(1)} %pick_own.1), channel_id=1, source_target_pairs={{0,8},{4,12},{8,0},{12,4},{16,24},{20,28},{24,16},{28,20},{1,9},{5... | collective-permute-start | bytes 196616 | tf_op jit(solution)/shard_map/ppermute | solution.py:35
  18.8 8.2 %collective-permute-start.11 = (bf16[128,512]{1,0:T(8,128)(2,1)S(1)}, bf16[128,512]{1,0:T(8,128)(2,1)S(1)}, u32[]{:S(2)}, u32[]{:S(2)}) collective-permute-start(bf16[128,512]{1,0:T(8,128)(2,1)S(1)} %get-tuple-element.55), channel_id=1, source_target_pairs={{0,4},{4,0},{8,12},{12,8},{16,20},{20,16},{24,28},{28,24},{1,5},{5... | collective-permute-start | bytes 393224 | tf_op jit(solution)/shard_map/ppermute | solution.py:35
  20.2 6.9 %collective-permute-start.13 = (bf16[128,512]{1,0:T(8,128)(2,1)S(1)}, bf16[128,512]{1,0:T(8,128)(2,1)S(1)}, u32[]{:S(2)}, u32[]{:S(2)}) collective-permute-start(bf16[128,512]{1,0:T(8,128)(2,1)S(1)} %get-tuple-element.57), channel_id=1, source_target_pairs={{0,12},{4,8},{8,4},{12,0},{16,28},{20,24},{24,20},{28,16},{1,13},{... | collective-permute-start | bytes 393224 | tf_op jit(solution)/shard_map/ppermute | solution.py:35
  22.5 4.4 %collective-permute-start.12 = (bf16[64,512]{1,0:T(8,128)(2,1)S(1)}, bf16[64,512]{1,0:T(8,128)(2,1)S(1)}, u32[]{:S(2)}, u32[]{:S(2)}) collective-permute-start(bf16[64,512]{1,0:T(8,128)(2,1)S(1)} %get-tuple-element.56), channel_id=1, source_target_pairs={{0,8},{4,12},{8,0},{12,4},{16,24},{20,28},{24,16},{28,20},{1,9},{5... | collective-permute-start | bytes 196616 | tf_op jit(solution)/shard_map/ppermute | solution.py:35
  24.4 2.7 %copy-start.1 = (bf16[512,512]{1,0:T(8,128)(2,1)S(1)}, bf16[512,512]{1,0:T(8,128)(2,1)}, u32[]{:S(2)}) copy-start(bf16[512,512]{1,0:T(8,128)(2,1)} %weight.3) | copy-start | bytes 1572868
  27.7 3.3 %collective-permute-start.14 = (bf16[64,512]{1,0:T(8,128)(2,1)S(1)}, bf16[64,512]{1,0:T(8,128)(2,1)S(1)}, u32[]{:S(2)}, u32[]{:S(2)}) collective-permute-start(bf16[64,512]{1,0:T(8,128)(2,1)S(1)} %get-tuple-element.58.first.refs_5_), channel_id=1, source_target_pairs={{0,1},{1,0},{2,3},{3,2},{4,5},{5,4},{6,7},{7,6},{8,9},{9,8},{10,11... | collective-permute-start | bytes 196616 | tf_op jit(solution)/shard_map/ppermute | solution.py:35
  27.8 4.5 %collective-permute-start.15 = (bf16[64,512]{1,0:T(8,128)(2,1)S(1)}, bf16[64,512]{1,0:T(8,128)(2,1)S(1)}, u32[]{:S(2)}, u32[]{:S(2)}) collective-permute-start(bf16[64,512]{1,0:T(8,128)(2,1)S(1)} %get-tuple-element.59.refs_6_), channel_id=1, source_target_pairs={{0,2},{1,3},{2,0},{3,1},{4,6},{5,7},{6,4},{7,5},{8,10},{9,11},{10,... | collective-permute-start | bytes 196616 | tf_op jit(solution)/shard_map/ppermute | solution.py:35
  29.4 4.0 %collective-permute-start.16 = (bf16[64,512]{1,0:T(8,128)(2,1)S(1)}, bf16[64,512]{1,0:T(8,128)(2,1)S(1)}, u32[]{:S(2)}, u32[]{:S(2)}) collective-permute-start(bf16[64,512]{1,0:T(8,128)(2,1)S(1)} %get-tuple-element.60.refs_7_), channel_id=1, source_target_pairs={{0,3},{1,2},{2,1},{3,0},{4,7},{5,6},{6,5},{7,4},{8,11},{9,10},{10,... | collective-permute-start | bytes 196616 | tf_op jit(solution)/shard_map/ppermute | solution.py:35

commit v6 on v5

--- a/solution.py
+++ b/solution.py
@@ -78,15 +78,15 @@
         out[...] = pick(hidden, one, 1, out.shape[0])
 
 
-def pick_far_kernel(rows, hidden, far, after, *refs):
-    asked, outs = refs[: len(refs) // 2], refs[len(refs) // 2 :]
+def pick_far_kernel(rows, peers, hidden, far, after, *refs):
+    asked, outs = refs[: len(peers)], refs[len(peers) :]
     for one, out in zip(asked, outs):
         out[:rows, :] = pick(far, one, 0, rows)
         if out.shape[0] > rows:
             out[rows:, :] = pick(hidden, one, 1, rows)
 
 
-def spread_kernel(per_dev, place, src, dst, tiles, out):
+def spread_kernel(per_dev, place, src, dst, tiles, after, out):
     block = tiles.shape[1]
     out[...] = jnp.zeros_like(out)
     for t in range(tiles.shape[0]):
@@ -94,7 +94,7 @@
         out[(src[0, t] // per_dev) ^ place[0], rows, :] = tiles[t]
 
 
-def load_kernel(history, after, out):
+def load_kernel(history, out):
     out[...] = history[...]
 
 
@@ -224,26 +224,17 @@
     )(place, tile_src, pull_count, pull_rows, push_rows.reshape(1, rows_dev))
     wanted = [asks[n_hist]] + [swap(asks[n_hist + k], "blk", n_blk, k) for k in range(1, n_half)]
     asked = [asks[0]] + [swap(asks[k], "hist", n_hist, k) for k in range(1, n_hist)]
-    spread = pl.pallas_call(
-        functools.partial(spread_kernel, per_dev),
-        out_shape=shape((n_blk, rows_dev, block_rows)),
-        in_specs=[smem()] * 3 + [vmem()],
-        out_specs=vmem(),
-        compiler_params=params(),
-        cost_estimate=cost(0, n_blk * rows_dev * block_rows * 2),
-        name="spread",
-    )(place, tile_src, tile_dst, tiles)
-
     history = pl.pallas_call(
         load_kernel,
         out_shape=shape(history.shape),
-        in_specs=[vmem(), anywhere],
+        in_specs=[vmem()],
         out_specs=vmem(),
         compiler_params=params(),
         cost_estimate=cost(0, held * feature * 4),
         name="load",
-    )(history, spread)
-    asked, wanted, history = lax.optimization_barrier((asked, wanted, history))
+    )(history)
+    asked, those, history = lax.optimization_barrier((asked, wanted[:3], history))
+    wanted = those + wanted[3:]
 
     fetched = pl.pallas_call(
         functools.partial(pull_kernel, n_hist, cap),
@@ -269,20 +260,37 @@
     )(hidden, *[wanted[k] for k in soon])
     early = [swap(one, "blk", n_blk, k) for one, k in zip(picked, soon)]
 
-    picked = pl.pallas_call(
-        functools.partial(pick_far_kernel, block_rows),
-        out_shape=[
-            shape((2 * block_rows if k and not one_hop(k) else block_rows, feature))
-            for k in range(n_half)
-        ],
-        in_specs=[vmem(), vmem(), anywhere] + [vmem()] * n_half,
-        out_specs=[vmem()] * n_half,
-        compiler_params=params(),
-        cost_estimate=cost(0, n_half * 4 * block_rows * feature),
-        name="pick_far",
-    )(hidden, far, arrived[1], *wanted)
+    def pick_far(peers, name):
+        return pl.pallas_call(
+            functools.partial(pick_far_kernel, block_rows, peers),
+            out_shape=[
+                shape((2 * block_rows if k and not one_hop(k) else block_rows, feature)) for k in peers
+            ],
+            in_specs=[vmem(), vmem(), anywhere] + [vmem()] * len(peers),
+            out_specs=[vmem()] * len(peers),
+            compiler_params=params(),
+            cost_estimate=cost(0, n_half * 4 * block_rows * feature),
+            name=name,
+        )(hidden, far, arrived[1], *[wanted[k] for k in peers])
+
+    single = [k for k in range(n_half) if k & (k - 1) == 0]
+    double = [k for k in range(n_half) if k & (k - 1)]
+    picked = [None] * n_half
+    for group, name in ((single, "pick_far"), (double, "pick_two_hop")):
+        for k, one in zip(group, pick_far(group, name)):
+            picked[k] = one
     mine = picked[0]
     late = [swap(picked[k], "blk", n_blk, k) for k in peers]
+
+    spread = pl.pallas_call(
+        functools.partial(spread_kernel, per_dev),
+        out_shape=shape((n_blk, rows_dev, block_rows)),
+        in_specs=[smem()] * 3 + [vmem(), anywhere],
+        out_specs=vmem(),
+        compiler_params=params(),
+        cost_estimate=cost(0, n_blk * rows_dev * block_rows * 2),
+        name="spread",
+    )(place, tile_src, tile_dst, tiles, mine)
 
     part = pl.pallas_call(
         functools.partial(partial_kernel, n_hist, n_half, cap),
@@ -324,6 +332,7 @@
     )(history, *asked, *sent)
 
     steps = 4
+    pushed[2], pushed[1], pushed[3] = lax.optimization_barrier((pushed[2], pushed[1], pushed[3]))
     new_history = pl.pallas_call(
         functools.partial(scatter_kernel, steps),
         out_shape=shape((held, feature)),

time: 34.9 us -> 33.9 us (0.971)
  waiting for transfers between devices: 7.04 us -> 5.61 us
  starting transfers between devices: 18.2 us -> 18.8 us
    ppermute x17, waiting for transfers between devices: 7.04 us -> 5.61 us  [swap(): return lax.ppermute(x, axis, [(i, i ^ k) for i in range(n)])]
    ppermute x17, starting transfers between devices: 18.2 us -> 18.8 us  [swap(): return lax.ppermute(x, axis, [(i, i ^ k) for i in range(n)])]
  transfers between devices with their start and end apart: 17 -> 17, of which waited for: 7 -> 6; matrix products, arithmetic and copies ran while one was open for 0% -> 0% of each run, Pallas kernels for 11% -> 12%
where the time goes in v6:
time: 33.9 us; the launch traced here: 33.6 us
  starting transfers between devices  18.8 us (55%)
  Pallas kernels  5.83 us (17%)
  waiting for transfers between devices  5.61 us (17%)
  local copies, waits for them, and re-layouts  2.55 us (8%)
  between operations  0.79 us (2%)
    ppermute x17, starting transfers between devices, swap(): return lax.ppermute(x, axis, [(i, i ^ k) for i in range(n)])  18.8 us
    ppermute x17, waiting for transfers between devices, swap(): return lax.ppermute(x, axis, [(i, i ^ k) for i in range(n)])  5.61 us
    unnamed x24, local copies, waits for them, and re-layouts  2.55 us
    pallas_call x1, Pallas kernels, local(): pl.pallas_call(functools.partial(scatter_kernel, steps), out_shape=shape(...  1.23 us
    pallas_call x2, Pallas kernels, final(): pl.pallas_call(functools.partial(final_kernel, n_half, chunks), out_shape...  0.99 us
    pallas_call x1, Pallas kernels, local(): pl.pallas_call(functools.partial(prepare_kernel, n_hist, cap), out_shape=...  0.98 us
    pallas_call x1, Pallas kernels, local(): pl.pallas_call(functools.partial(pull_kernel, n_hist, cap), out_shape=[sh...  0.74 us
  transfers between devices with their start and end apart: 17, of which 6 were waited for; matrix products, arithmetic and copies ran while one was open for 0% of the time, Pallas kernels for 12%

profile of v6, /device:TPU:0, one launch (start us, length us, event | category | flops | bytes accessed | tf_op | source)
XLA Modules:
  0.0 33.6 jit_solution(4455383706242183037)
XLA Ops:
  0.6 4.1 %collective-permute-start.5 = (bf16[256,512]{1,0:T(8,128)(2,1)}, bf16[256,512]{1,0:T(8,128)(2,1)S(1)}, u32[]{:S(2)}, u32[]{:S(2)}) collective-permute-start(bf16[256,512]{1,0:T(8,128)(2,1)} %hidden.7), channel_id=1, source_target_pairs={{0,16},{4,20},{8,24},{12,28},{16,0},{20,4},{24,8},{28,12},{1,17},{... | collective-permute-start | bytes 786440 | tf_op jit(solution)/shard_map/ppermute | solution.py:35
  4.7 0.0 copy-start.10
  4.7 0.0 copy-start.7
  4.7 0.1 pad_add_fusion.after.place
  4.8 0.0 copy-start.8
  4.8 0.0 copy-start.9
  4.8 0.6 %copy-done.10 = s32[1,4]{1,0:T(1,128)S(1)} copy-done((s32[1,4]{1,0:T(1,128)S(1)}, s32[1,4]{1,0:T(1,128)}, u32[]{:S(2)}) %copy-start.10) | copy-done | bytes 40
  5.4 0.0 copy-done.7
  5.4 0.0 copy-done.8
  5.5 0.0 copy-done.9
  5.5 0.3 message.1
  5.8 0.0 collective-permute-start
  5.9 1.6 %collective-permute-start.1 = (s32[1,256]{1,0:T(1,128)S(1)}, s32[1,256]{1,0:T(1,128)S(1)}, u32[]{:S(2)}, u32[]{:S(2)}) collective-permute-start(s32[1,256]{1,0:T(1,128)S(1)} %get-tuple-element.36), channel_id=1, source_target_pairs={{0,2},{1,3},{2,0},{3,1},{4,6},{5,7},{6,4},{7,5},{8,10},{9,11},{10,... | collective-permute-start | bytes 3080 | tf_op jit(solution)/shard_map/ppermute | solution.py:35
  7.4 0.3 collective-permute-start.2
  7.7 1.5 %collective-permute-start.3 = (s32[1,256]{1,0:T(1,128)S(1)}, s32[1,256]{1,0:T(1,128)S(1)}, u32[]{:S(2)}, u32[]{:S(2)}) collective-permute-start(s32[1,256]{1,0:T(1,128)S(1)} %get-tuple-element.39), channel_id=1, source_target_pairs={{0,4},{4,0},{8,12},{12,8},{16,20},{20,16},{24,28},{28,24},{1,5},{5... | collective-permute-start | bytes 3080 | tf_op jit(solution)/shard_map/ppermute | solution.py:35
  9.2 0.0 collective-permute-done.refs_1_
  9.2 1.6 %collective-permute-start.4 = (s32[1,256]{1,0:T(1,128)S(1)}, s32[1,256]{1,0:T(1,128)S(1)}, u32[]{:S(2)}, u32[]{:S(2)}) collective-permute-start(s32[1,256]{1,0:T(1,128)S(1)} %get-tuple-element.40), channel_id=1, source_target_pairs={{0,8},{4,12},{8,0},{12,4},{16,24},{20,28},{24,16},{28,20},{1,9},{5... | collective-permute-start | bytes 3080 | tf_op jit(solution)/shard_map/ppermute | solution.py:35
  10.8 1.2 %copy-done.2 = bf16[1024,512]{1,0:T(8,128)(2,1)S(1)} copy-done((bf16[1024,512]{1,0:T(8,128)(2,1)S(1)}, bf16[1024,512]{1,0:T(8,128)(2,1)}, u32[]{:S(2)}) %copy-start.2) | copy-done | bytes 1048600
  12.0 0.1 load.1.history
  12.1 0.0 collective-permute-done.1.refs_2_
  12.1 0.0 collective-permute-done.2.refs_3_
  12.1 0.0 collective-permute-done.3.refs_1_
  12.1 0.8 %collective-permute-done.4.refs_2_.refs_0_ = s32[1,256]{1,0:T(1,128)S(1)} collective-permute-done((s32[1,256]{1,0:T(1,128)S(1)}, s32[1,256]{1,0:T(1,128)S(1)}, u32[]{:S(2)}, u32[]{:S(2)}) %collective-permute-start.4) | collective-permute-done | bytes 1056 | tf_op jit(solution)/shard_map/ppermute | solution.py:35
  12.9 0.7 %pull.1 = (bf16[128,512]{1,0:T(8,128)(2,1)S(1)}, bf16[128,512]{1,0:T(8,128)(2,1)S(1)}, bf16[128,512]{1,0:T(8,128)(2,1)S(1)}, bf16[128,512]{1,0:T(8,128)(2,1)S(1)}) custom-call(bf16[1024,512]{1,0:T(8,128)(2,1)S(1)} %load.1.history, s32[1,256]{1,0:T(1,128)S(1)} %get-tuple-element.42.refs_0_, s32[1,256]{1,0:T(1,128)S(1)} %collective-permute-done.refs_1_, ...), custom_call_target="tpu_custom_call" | custom-call | flops 536870912 | bytes 2097152 | tf_op jit(solution)/shard_map/pull/pallas_call | solution.py:239
  13.6 0.1 collective-permute-start.6
  13.7 1.6 %collective-permute-start.7 = (bf16[128,512]{1,0:T(8,128)(2,1)S(1)}, bf16[128,512]{1,0:T(8,128)(2,1)S(1)}, u32[]{:S(2)}, u32[]{:S(2)}) collective-permute-start(bf16[128,512]{1,0:T(8,128)(2,1)S(1)} %get-tuple-element.52), channel_id=1, source_target_pairs={{0,2},{1,3},{2,0},{3,1},{4,6},{5,7},{6,4},{7,5},{8,10},{9,11},{10,... | collective-permute-start | bytes 393224 | tf_op jit(solution)/shard_map/ppermute | solution.py:35
  15.3 0.3 collective-permute-start.8
  15.6 1.4 %collective-permute-start.12 = (s32[1,256]{1,0:T(1,128)S(1)}, s32[1,256]{1,0:T(1,128)S(1)}, u32[]{:S(2)}, u32[]{:S(2)}) collective-permute-start(s32[1,256]{1,0:T(1,128)S(1)} %get-tuple-element.56), channel_id=1, source_target_pairs={{0,12},{4,8},{8,4},{12,0},{16,28},{20,24},{24,20},{28,16},{1,13},{... | collective-permute-start | bytes 3080 | tf_op jit(solution)/shard_map/ppermute | solution.py:35
  17.0 0.0 copy-done
  17.0 0.1 pick_own.1
  17.1 0.0 collective-permute-done.6.after.refs_1_
  17.1 0.5 %collective-permute-start.9 = (bf16[64,512]{1,0:T(8,128)(2,1)S(1)}, bf16[64,512]{1,0:T(8,128)(2,1)S(1)}, u32[]{:S(2)}, u32[]{:S(2)}) collective-permute-start(bf16[64,512]{1,0:T(8,128)(2,1)S(1)} %pick_own.1), channel_id=1, source_target_pairs={{0,8},{4,12},{8,0},{12,4},{16,24},{20,28},{24,16},{28,20},{1,9},{5... | collective-permute-start | bytes 196616 | tf_op jit(solution)/shard_map/ppermute | solution.py:35
  17.6 0.0 collective-permute-done.5.far
  17.6 0.1 pick_far.1
  17.8 0.0 copy-start.6
  17.8 1.7 %collective-permute-start.10 = (bf16[128,512]{1,0:T(8,128)(2,1)S(1)}, bf16[128,512]{1,0:T(8,128)(2,1)S(1)}, u32[]{:S(2)}, u32[]{:S(2)}) collective-permute-start(bf16[128,512]{1,0:T(8,128)(2,1)S(1)} %get-tuple-element.54), channel_id=1, source_target_pairs={{0,4},{4,0},{8,12},{12,8},{16,20},{20,16},{24,28},{28,24},{1,5},{5... | collective-permute-start | bytes 393224 | tf_op jit(solution)/shard_map/ppermute | solution.py:35
  19.4 0.6 %collective-permute-done.12.refs_0_ = s32[1,256]{1,0:T(1,128)S(1)} collective-permute-done((s32[1,256]{1,0:T(1,128)S(1)}, s32[1,256]{1,0:T(1,128)S(1)}, u32[]{:S(2)}, u32[]{:S(2)}) %collective-permute-start.12) | collective-permute-done | bytes 1056 | tf_op jit(solution)/shard_map/ppermute | solution.py:35
  20.1 0.1 pick_two_hop.1
  20.1 1.5 %collective-permute-start.13 = (bf16[128,512]{1,0:T(8,128)(2,1)S(1)}, bf16[128,512]{1,0:T(8,128)(2,1)S(1)}, u32[]{:S(2)}, u32[]{:S(2)}) collective-permute-start(bf16[128,512]{1,0:T(8,128)(2,1)S(1)} %pick_two_hop.1), channel_id=1, source_target_pairs={{0,12},{4,8},{8,4},{12,0},{16,28},{20,24},{24,20},{28,16},{1,13},{... | collective-permute-start | bytes 393224 | tf_op jit(solution)/shard_map/ppermute | solution.py:35
  21.7 0.0 collective-permute-done.9.refs_4_
  21.7 0.4 %collective-permute-start.11 = (bf16[64,512]{1,0:T(8,128)(2,1)S(1)}, bf16[64,512]{1,0:T(8,128)(2,1)S(1)}, u32[]{:S(2)}, u32[]{:S(2)}) collective-permute-start(bf16[64,512]{1,0:T(8,128)(2,1)S(1)} %get-tuple-element.55), channel_id=1, source_target_pairs={{0,8},{4,12},{8,0},{12,4},{16,24},{20,28},{24,16},{28,20},{1,9},{5... | collective-permute-start | bytes 196616 | tf_op jit(solution)/shard_map/ppermute | solution.py:35
  22.1 0.0 copy-done.6
  22.1 0.2 copy-done.11
  22.3 0.6 %spread.1 = bf16[8,256,64]{2,1,0:T(8,128)(2,1)S(1)} custom-call(s32[2]{0:T(128)S(1)} %pad_add_fusion.after.place, s32[1,4]{1,0:T(1,128)S(1)} %copy-done.8, s32[1,4]{1,0:T(1,128)S(1)} %copy-done.11, bf16[4,64,64]{2,1,0:T(8,128)(2,1)S(1)} %copy-done.6, bf16[64,512]{1,0:T(8,128)(2,1)S(1)} %get-tuple-element.50.after.mine.first), custom_call_target="tpu_custom_call" | custom-call | bytes 262144 | tf_op jit(solution)/shard_map/spread/pallas_call | solution.py:285
  23.0 0.0 collective-permute-done.7.refs_2_
  23.0 0.0 collective-permute-done.8.refs_3_
  23.0 0.3 copy-done.3
  23.3 0.1 copy-done.4
  23.4 0.0 copy-done.5
  23.4 0.6 %partial.1.part = f32[256,512]{1,0:T(8,128)S(1)} custom-call(bf16[256,256]{1,0:T(8,128)(2,1)S(1)} %copy-done.5, bf16[256,512]{1,0:T(8,128)(2,1)S(1)} %copy-done, bf16[256,512]{1,0:T(8,128)(2,1)S(1)} %copy-done.3, bf16[256,512]{1,0:T(8,128)(2,1)S(1)} %copy-done.4, bf16[8,256,64]{2,1,0:T(8,128)(2,1)S(1)} %spread.1, ...), custom_call_target="tpu_custom_call" | custom-call | flops 201326592 | bytes 1572864 | tf_op jit(solution)/shard_map/partial/pallas_call | solution.py:295
  24.0 2.1 %collective-permute-done.11.refs_1_ = bf16[64,512]{1,0:T(8,128)(2,1)S(1)} collective-permute-done((bf16[64,512]{1,0:T(8,128)(2,1)S(1)}, bf16[64,512]{1,0:T(8,128)(2,1)S(1)}, u32[]{:S(2)}, u32[]{:S(2)}) %collective-permute-start.11) | collective-permute-done | bytes 65568 | tf_op jit(solution)/shard_map/ppermute | solution.py:35
  26.1 0.0 collective-permute-done.10.refs_0_
  26.1 0.3 collective-permute-done.13.refs_2_
  26.5 0.0 copy-done.1
  26.5 0.6 %final_sent.1 = (bf16[64,512]{1,0:T(8,128)(2,1)S(1)}, bf16[64,512]{1,0:T(8,128)(2,1)S(1)}, bf16[64,512]{1,0:T(8,128)(2,1)S(1)}) custom-call(bf16[64,512]{1,0:T(8,128)(2,1)S(1)} %get-tuple-element.50.after.mine.first, f32[256,512]{1,0:T(8,128)S(1)} %partial.1.part, bf16[8,256,64]{2,1,0:T(8,128)(2,1)S(1)} %spread.1, bf16[512,512]{1,0:T(8,128)(2,1)S(1)} %copy-done.1, ...), custom_call_target="tpu_custom_call" | custom-call | flops 100663296 | bytes 1179648 | tf_op jit(solution)/shard_map/final_sent/pallas_call | solution.py:307
  27.1 1.6 %collective-permute-start.14 = (bf16[64,512]{1,0:T(8,128)(2,1)S(1)}, bf16[64,512]{1,0:T(8,128)(2,1)S(1)}, u32[]{:S(2)}, u32[]{:S(2)}) collective-permute-start(bf16[64,512]{1,0:T(8,128)(2,1)S(1)} %get-tuple-element.58.refs_6_), channel_id=1, source_target_pairs={{0,2},{1,3},{2,0},{3,1},{4,6},{5,7},{6,4},{7,5},{8,10},{9,11},{10,... | collective-permute-start | bytes 196616 | tf_op jit(solution)/shard_map/ppermute | solution.py:35
  28.7 0.0 collective-permute-start.15
  28.7 0.6 %collective-permute-start.16 = (bf16[64,512]{1,0:T(8,128)(2,1)S(1)}, bf16[64,512]{1,0:T(8,128)(2,1)S(1)}, u32[]{:S(2)}, u32[]{:S(2)}) collective-permute-start(bf16[64,512]{1,0:T(8,128)(2,1)S(1)} %get-tuple-element.59.refs_7_), channel_id=1, source_target_pairs={{0,3},{1,2},{2,1},{3,0},{4,7},{5,6},{6,5},{7,4},{8,11},{9,10},{10,... | collective-permute-start | bytes 196616 | tf_op jit(solution)/shard_map/ppermute | solution.py:35
  29.3 0.4 %final_kept.1.refs_4_.refs_0_ = bf16[64,512]{1,0:T(8,128)(2,1)S(1)} custom-call(bf16[64,512]{1,0:T(8,128)(2,1)S(1)} %get-tuple-element.57.first.refs_5_, f32[256,512]{1,0:T(8,128)S(1)} %partial.1.part, bf16[8,256,64]{2,1,0:T(8,128)(2,1)S(1)} %spread.1, bf16[512,512]{1,0:T(8,128)(2,1)S(1)} %copy-done.1, bf16[128,512]{1,0:T(8,128)(2,1)S(1)} %collective-permute-done.10.refs_0_, ...), custom_call_target="tpu_custom_call" | custom-call | flops 33554432 | bytes 393216 | tf_op jit(solution)/shard_map/final_kept/pallas_call | solution.py:307
  29.7 1.0 %prepare.1 = (bf16[1024,512]{1,0:T(8,128)(2,1)S(1)}, bf16[1024,256]{1,0:T(8,128)(2,1)S(1)}, bf16[256,512]{1,0:T(8,128)(2,1)}) custom-call(bf16[1024,512]{1,0:T(8,128)(2,1)S(1)} %load.1.history, s32[1,256]{1,0:T(1,128)S(1)} %get-tuple-element.42.refs_0_, s32[1,256]{1,0:T(1,128)S(1)} %collective-permute-done.refs_1_, ...), custom_call_target="tpu_custom_call" | custom-call | flops 2097152 | bytes 3145728 | tf_op jit(solution)/shard_map/prepare/pallas_call | solution.py:323
  30.7 0.7 %collective-permute-done.14.refs_2_ = bf16[64,512]{1,0:T(8,128)(2,1)S(1)} collective-permute-done((bf16[64,512]{1,0:T(8,128)(2,1)S(1)}, bf16[64,512]{1,0:T(8,128)(2,1)S(1)}, u32[]{:S(2)}, u32[]{:S(2)}) %collective-permute-start.14) | collective-permute-done | bytes 65568 | tf_op jit(solution)/shard_map/ppermute | solution.py:35
  31.4 0.0 collective-permute-done.15.refs_1_
  31.4 1.0 %collective-permute-done.16.refs_3_ = bf16[64,512]{1,0:T(8,128)(2,1)S(1)} collective-permute-done((bf16[64,512]{1,0:T(8,128)(2,1)S(1)}, bf16[64,512]{1,0:T(8,128)(2,1)S(1)}, u32[]{:S(2)}, u32[]{:S(2)}) %collective-permute-start.16) | collective-permute-done | bytes 65568 | tf_op jit(solution)/shard_map/ppermute | solution.py:35
  32.4 1.2 %scatter.1 = bf16[1024,512]{1,0:T(8,128)(2,1)} custom-call(bf16[1024,512]{1,0:T(8,128)(2,1)S(1)} %get-tuple-element.61.base, bf16[1024,256]{1,0:T(8,128)(2,1)S(1)} %get-tuple-element.62.hot, bf16[64,512]{1,0:T(8,128)(2,1)S(1)} %final_kept.1.refs_4_.refs_0_, bf16[64,512]{1,0:T(8,128)(2,1)S(1)} %collective-permute-done.15.refs_1_, ...), custom_call_target="tpu_custom_call" | custom-call | tf_op jit(solution)/shard_map/scatter/pallas_call | solution.py:336
  (7 shorter events, 0.0 us)
Async XLA Ops:
  0.6 17.0 %collective-permute-start.5 = (bf16[256,512]{1,0:T(8,128)(2,1)}, bf16[256,512]{1,0:T(8,128)(2,1)S(1)}, u32[]{:S(2)}, u32[]{:S(2)}) collective-permute-start(bf16[256,512]{1,0:T(8,128)(2,1)} %hidden.7), channel_id=1, source_target_pairs={{0,16},{4,20},{8,24},{12,28},{16,0},{20,4},{24,8},{28,12},{1,17},{... | collective-permute-start | bytes 786440 | tf_op jit(solution)/shard_map/ppermute | solution.py:35
  4.7 0.7 %copy-start.10 = (s32[1,4]{1,0:T(1,128)S(1)}, s32[1,4]{1,0:T(1,128)}, u32[]{:S(2)}) copy-start(s32[1,4]{1,0:T(1,128)} %count.1) | copy-start | bytes 52
  4.7 0.7 %copy-start.7 = (s32[1,4,128]{2,1,0:T(4,128)S(1)}, s32[1,4,128]{2,1,0:T(4,128)}, u32[]{:S(2)}) copy-start(s32[1,4,128]{2,1,0:T(4,128)} %rows.1) | copy-start | bytes 6148
  4.8 0.7 %copy-start.8 = (s32[1,4]{1,0:T(1,128)S(1)}, s32[1,4]{1,0:T(1,128)}, u32[]{:S(2)}) copy-start(s32[1,4]{1,0:T(1,128)} %src.3) | copy-start | bytes 52
  4.8 0.7 %copy-start.9 = (s32[256]{0:T(256)S(1)}, s32[256]{0:T(256)}, u32[]{:S(2)}) copy-start(s32[256]{0:T(256)} %param.23) | copy-start | bytes 3076
  5.8 3.4 %collective-permute-start = (s32[1,256]{1,0:T(1,128)S(1)}, s32[1,256]{1,0:T(1,128)S(1)}, u32[]{:S(2)}, u32[]{:S(2)}) collective-permute-start(s32[1,256]{1,0:T(1,128)S(1)} %get-tuple-element.35), channel_id=1, source_target_pairs={{0,1},{1,0},{2,3},{3,2},{4,5},{5,4},{6,7},{7,6},{8,9},{9,8},{10,11... | collective-permute-start | bytes 3080 | tf_op jit(solution)/shard_map/ppermute | solution.py:35
  5.9 6.2 %collective-permute-start.1 = (s32[1,256]{1,0:T(1,128)S(1)}, s32[1,256]{1,0:T(1,128)S(1)}, u32[]{:S(2)}, u32[]{:S(2)}) collective-permute-start(s32[1,256]{1,0:T(1,128)S(1)} %get-tuple-element.36), channel_id=1, source_target_pairs={{0,2},{1,3},{2,0},{3,1},{4,6},{5,7},{6,4},{7,5},{8,10},{9,11},{10,... | collective-permute-start | bytes 3080 | tf_op jit(solution)/shard_map/ppermute | solution.py:35
  7.4 4.7 %collective-permute-start.2 = (s32[1,256]{1,0:T(1,128)S(1)}, s32[1,256]{1,0:T(1,128)S(1)}, u32[]{:S(2)}, u32[]{:S(2)}) collective-permute-start(s32[1,256]{1,0:T(1,128)S(1)} %get-tuple-element.37), channel_id=1, source_target_pairs={{0,3},{1,2},{2,1},{3,0},{4,7},{5,6},{6,5},{7,4},{8,11},{9,10},{10,... | collective-permute-start | bytes 3080 | tf_op jit(solution)/shard_map/ppermute | solution.py:35
  7.7 4.4 %collective-permute-start.3 = (s32[1,256]{1,0:T(1,128)S(1)}, s32[1,256]{1,0:T(1,128)S(1)}, u32[]{:S(2)}, u32[]{:S(2)}) collective-permute-start(s32[1,256]{1,0:T(1,128)S(1)} %get-tuple-element.39), channel_id=1, source_target_pairs={{0,4},{4,0},{8,12},{12,8},{16,20},{20,16},{24,28},{28,24},{1,5},{5... | collective-permute-start | bytes 3080 | tf_op jit(solution)/shard_map/ppermute | solution.py:35
  9.2 3.7 %collective-permute-start.4 = (s32[1,256]{1,0:T(1,128)S(1)}, s32[1,256]{1,0:T(1,128)S(1)}, u32[]{:S(2)}, u32[]{:S(2)}) collective-permute-start(s32[1,256]{1,0:T(1,128)S(1)} %get-tuple-element.40), channel_id=1, source_target_pairs={{0,8},{4,12},{8,0},{12,4},{16,24},{20,28},{24,16},{28,20},{1,9},{5... | collective-permute-start | bytes 3080 | tf_op jit(solution)/shard_map/ppermute | solution.py:35
  10.8 1.2 %copy-start.2 = (bf16[1024,512]{1,0:T(8,128)(2,1)S(1)}, bf16[1024,512]{1,0:T(8,128)(2,1)}, u32[]{:S(2)}) copy-start(bf16[1024,512]{1,0:T(8,128)(2,1)} %history.1) | copy-start | bytes 3145732
  12.9 4.1 %copy-start = (bf16[256,512]{1,0:T(8,128)(2,1)S(1)}, bf16[256,512]{1,0:T(8,128)(2,1)}, u32[]{:S(2)}) copy-start(bf16[256,512]{1,0:T(8,128)(2,1)} %hidden.7) | copy-start | bytes 786436
  13.6 3.5 %collective-permute-start.6 = (bf16[128,512]{1,0:T(8,128)(2,1)S(1)}, bf16[128,512]{1,0:T(8,128)(2,1)S(1)}, u32[]{:S(2)}, u32[]{:S(2)}) collective-permute-start(bf16[128,512]{1,0:T(8,128)(2,1)S(1)} %get-tuple-element.46), channel_id=1, source_target_pairs={{0,1},{1,0},{2,3},{3,2},{4,5},{5,4},{6,7},{7,6},{8,9},{9,8},{10,11... | collective-permute-start | bytes 393224 | tf_op jit(solution)/shard_map/ppermute | solution.py:35
  13.7 9.3 %collective-permute-start.7 = (bf16[128,512]{1,0:T(8,128)(2,1)S(1)}, bf16[128,512]{1,0:T(8,128)(2,1)S(1)}, u32[]{:S(2)}, u32[]{:S(2)}) collective-permute-start(bf16[128,512]{1,0:T(8,128)(2,1)S(1)} %get-tuple-element.52), channel_id=1, source_target_pairs={{0,2},{1,3},{2,0},{3,1},{4,6},{5,7},{6,4},{7,5},{8,10},{9,11},{10,... | collective-permute-start | bytes 393224 | tf_op jit(solution)/shard_map/ppermute | solution.py:35
  15.3 7.7 %collective-permute-start.8 = (bf16[128,512]{1,0:T(8,128)(2,1)S(1)}, bf16[128,512]{1,0:T(8,128)(2,1)S(1)}, u32[]{:S(2)}, u32[]{:S(2)}) collective-permute-start(bf16[128,512]{1,0:T(8,128)(2,1)S(1)} %get-tuple-element.53), channel_id=1, source_target_pairs={{0,3},{1,2},{2,1},{3,0},{4,7},{5,6},{6,5},{7,4},{8,11},{9,10},{10,... | collective-permute-start | bytes 393224 | tf_op jit(solution)/shard_map/ppermute | solution.py:35
  15.6 4.5 %collective-permute-start.12 = (s32[1,256]{1,0:T(1,128)S(1)}, s32[1,256]{1,0:T(1,128)S(1)}, u32[]{:S(2)}, u32[]{:S(2)}) collective-permute-start(s32[1,256]{1,0:T(1,128)S(1)} %get-tuple-element.56), channel_id=1, source_target_pairs={{0,12},{4,8},{8,4},{12,0},{16,28},{20,24},{24,20},{28,16},{1,13},{... | collective-permute-start | bytes 3080 | tf_op jit(solution)/shard_map/ppermute | solution.py:35
  17.1 4.5 %collective-permute-start.9 = (bf16[64,512]{1,0:T(8,128)(2,1)S(1)}, bf16[64,512]{1,0:T(8,128)(2,1)S(1)}, u32[]{:S(2)}, u32[]{:S(2)}) collective-permute-start(bf16[64,512]{1,0:T(8,128)(2,1)S(1)} %pick_own.1), channel_id=1, source_target_pairs={{0,8},{4,12},{8,0},{12,4},{16,24},{20,28},{24,16},{28,20},{1,9},{5... | collective-permute-start | bytes 196616 | tf_op jit(solution)/shard_map/ppermute | solution.py:35
  17.8 4.4 %copy-start.6 = (bf16[4,64,64]{2,1,0:T(8,128)(2,1)S(1)}, bf16[4,64,64]{2,1,0:T(8,128)(2,1)}, u32[]{:S(2)}) copy-start(bf16[4,64,64]{2,1,0:T(8,128)(2,1)} %tiles.1) | copy-start | bytes 98308
  17.8 8.4 %collective-permute-start.10 = (bf16[128,512]{1,0:T(8,128)(2,1)S(1)}, bf16[128,512]{1,0:T(8,128)(2,1)S(1)}, u32[]{:S(2)}, u32[]{:S(2)}) collective-permute-start(bf16[128,512]{1,0:T(8,128)(2,1)S(1)} %get-tuple-element.54), channel_id=1, source_target_pairs={{0,4},{4,0},{8,12},{12,8},{16,20},{20,16},{24,28},{28,24},{1,5},{5... | collective-permute-start | bytes 393224 | tf_op jit(solution)/shard_map/ppermute | solution.py:35
  20.1 6.3 %collective-permute-start.13 = (bf16[128,512]{1,0:T(8,128)(2,1)S(1)}, bf16[128,512]{1,0:T(8,128)(2,1)S(1)}, u32[]{:S(2)}, u32[]{:S(2)}) collective-permute-start(bf16[128,512]{1,0:T(8,128)(2,1)S(1)} %pick_two_hop.1), channel_id=1, source_target_pairs={{0,12},{4,8},{8,4},{12,0},{16,28},{20,24},{24,20},{28,16},{1,13},{... | collective-permute-start | bytes 393224 | tf_op jit(solution)/shard_map/ppermute | solution.py:35
  21.7 0.7 %copy-start.11 = (s32[1,4]{1,0:T(1,128)S(1)}, s32[1,4]{1,0:T(1,128)}, u32[]{:S(2)}) copy-start(s32[1,4]{1,0:T(1,128)} %dst.1) | copy-start | bytes 52
  21.7 4.5 %collective-permute-start.11 = (bf16[64,512]{1,0:T(8,128)(2,1)S(1)}, bf16[64,512]{1,0:T(8,128)(2,1)S(1)}, u32[]{:S(2)}, u32[]{:S(2)}) collective-permute-start(bf16[64,512]{1,0:T(8,128)(2,1)S(1)} %get-tuple-element.55), channel_id=1, source_target_pairs={{0,8},{4,12},{8,0},{12,4},{16,24},{20,28},{24,16},{28,20},{1,9},{5... | collective-permute-start | bytes 196616 | tf_op jit(solution)/shard_map/ppermute | solution.py:35
  22.3 0.9 %copy-start.3 = (bf16[256,512]{1,0:T(8,128)(2,1)S(1)}, bf16[256,512]{1,0:T(8,128)(2,1)}, u32[]{:S(2)}) copy-start(bf16[256,512]{1,0:T(8,128)(2,1)} %pull_adj.1) | copy-start | bytes 786436
  22.3 1.0 %copy-start.4 = (bf16[256,512]{1,0:T(8,128)(2,1)S(1)}, bf16[256,512]{1,0:T(8,128)(2,1)}, u32[]{:S(2)}) copy-start(bf16[256,512]{1,0:T(8,128)(2,1)} %initial.1) | copy-start | bytes 786436
  22.3 1.1 %copy-start.5 = (bf16[256,256]{1,0:T(8,128)(2,1)S(1)}, bf16[256,256]{1,0:T(8,128)(2,1)}, u32[]{:S(2)}) copy-start(bf16[256,256]{1,0:T(8,128)(2,1)} %own_adj.1) | copy-start | bytes 393220
  23.4 3.1 %copy-start.1 = (bf16[512,512]{1,0:T(8,128)(2,1)S(1)}, bf16[512,512]{1,0:T(8,128)(2,1)}, u32[]{:S(2)}) copy-start(bf16[512,512]{1,0:T(8,128)(2,1)} %weight.3) | copy-start | bytes 1572868
  27.1 4.3 %collective-permute-start.14 = (bf16[64,512]{1,0:T(8,128)(2,1)S(1)}, bf16[64,512]{1,0:T(8,128)(2,1)S(1)}, u32[]{:S(2)}, u32[]{:S(2)}) collective-permute-start(bf16[64,512]{1,0:T(8,128)(2,1)S(1)} %get-tuple-element.58.refs_6_), channel_id=1, source_target_pairs={{0,2},{1,3},{2,0},{3,1},{4,6},{5,7},{6,4},{7,5},{8,10},{9,11},{10,... | collective-permute-start | bytes 196616 | tf_op jit(solution)/shard_map/ppermute | solution.py:35
  28.7 2.7 %collective-permute-start.15 = (bf16[64,512]{1,0:T(8,128)(2,1)S(1)}, bf16[64,512]{1,0:T(8,128)(2,1)S(1)}, u32[]{:S(2)}, u32[]{:S(2)}) collective-permute-start(bf16[64,512]{1,0:T(8,128)(2,1)S(1)} %get-tuple-element.57.first.refs_5_), channel_id=1, source_target_pairs={{0,1},{1,0},{2,3},{3,2},{4,5},{5,4},{6,7},{7,6},{8,9},{9,8},{10,11... | collective-permute-start | bytes 196616 | tf_op jit(solution)/shard_map/ppermute | solution.py:35
  28.7 3.7 %collective-permute-start.16 = (bf16[64,512]{1,0:T(8,128)(2,1)S(1)}, bf16[64,512]{1,0:T(8,128)(2,1)S(1)}, u32[]{:S(2)}, u32[]{:S(2)}) collective-permute-start(bf16[64,512]{1,0:T(8,128)(2,1)S(1)} %get-tuple-element.59.refs_7_), channel_id=1, source_target_pairs={{0,3},{1,2},{2,1},{3,0},{4,7},{5,6},{6,5},{7,4},{8,11},{9,10},{10,... | collective-permute-start | bytes 196616 | tf_op jit(solution)/shard_map/ppermute | solution.py:35

commit v7 on v6

--- a/solution.py
+++ b/solution.py
@@ -233,8 +233,14 @@
         cost_estimate=cost(0, held * feature * 4),
         name="load",
     )(history)
-    asked, those, history = lax.optimization_barrier((asked, wanted[:3], history))
-    wanted = those + wanted[3:]
+    ones = [k for k in range(1, n_half) if k & (k - 1) == 0]
+    first = [asked[1], wanted[1], *asked[2:], *[wanted[k] for k in ones[1:]]]
+    asked[0], wanted[0], first, history = lax.optimization_barrier(
+        (asked[0], wanted[0], first, history)
+    )
+    asked[1:], wanted[1] = [first[0], *first[2 : n_hist]], first[1]
+    for k, one in zip(ones[1:], first[n_hist:]):
+        wanted[k] = one
 
     fetched = pl.pallas_call(
         functools.partial(pull_kernel, n_hist, cap),
@@ -332,7 +338,8 @@
     )(history, *asked, *sent)
 
     steps = 4
-    pushed[2], pushed[1], pushed[3] = lax.optimization_barrier((pushed[2], pushed[1], pushed[3]))
+    outer, inner, *rest = lax.optimization_barrier((pushed[2], pushed[1], *pushed[3:]))
+    pushed = [pushed[0], inner, outer, *rest]
     new_history = pl.pallas_call(
         functools.partial(scatter_kernel, steps),
         out_shape=shape((held, feature)),

time: 33.9 us -> 33.6 us (level)
  transfers between devices with their start and end apart: 17 -> 17, of which waited for: 6 -> 7; matrix products, arithmetic and copies ran while one was open for 0% -> 0% of each run, Pallas kernels for 12% -> 12%
where the time goes in v7:
time: 33.6 us; the launch traced here: 33.4 us
  starting transfers between devices  18.5 us (55%)
  Pallas kernels  5.85 us (17%)
  waiting for transfers between devices  5.55 us (17%)
  local copies, waits for them, and re-layouts  2.55 us (8%)
  between operations  0.78 us (2%)
    ppermute x17, starting transfers between devices, swap(): return lax.ppermute(x, axis, [(i, i ^ k) for i in range(n)])  18.5 us
    ppermute x17, waiting for transfers between devices, swap(): return lax.ppermute(x, axis, [(i, i ^ k) for i in range(n)])  5.55 us
    unnamed x24, local copies, waits for them, and re-layouts  2.55 us
    pallas_call x1, Pallas kernels, local(): pl.pallas_call(functools.partial(scatter_kernel, steps), out_shape=shape(...  1.23 us
    pallas_call x2, Pallas kernels, final(): pl.pallas_call(functools.partial(final_kernel, n_half, chunks), out_shape...  1.01 us
    pallas_call x1, Pallas kernels, local(): pl.pallas_call(functools.partial(prepare_kernel, n_hist, cap), out_shape=...  0.98 us
    pallas_call x1, Pallas kernels, local(): pl.pallas_call(functools.partial(pull_kernel, n_hist, cap), out_shape=[sh...  0.74 us
  transfers between devices with their start and end apart: 17, of which 7 were waited for; matrix products, arithmetic and copies ran while one was open for 0% of the time, Pallas kernels for 12%

profile of v7, /device:TPU:0, one launch (start us, length us, event | category | flops | bytes accessed | tf_op | source)
XLA Modules:
  0.0 33.4 jit_solution(10304094957737106968)
XLA Ops:
  0.6 4.1 %collective-permute-start.5 = (bf16[256,512]{1,0:T(8,128)(2,1)}, bf16[256,512]{1,0:T(8,128)(2,1)S(1)}, u32[]{:S(2)}, u32[]{:S(2)}) collective-permute-start(bf16[256,512]{1,0:T(8,128)(2,1)} %hidden.7), channel_id=1, source_target_pairs={{0,16},{4,20},{8,24},{12,28},{16,0},{20,4},{24,8},{28,12},{1,17},{... | collective-permute-start | bytes 786440 | tf_op jit(solution)/shard_map/ppermute | solution.py:35
  4.7 0.0 copy-start.10
  4.7 0.0 copy-start.7
  4.7 0.1 pad_add_fusion.after.place
  4.8 0.0 copy-start.8
  4.8 0.0 copy-start.9
  4.8 0.6 %copy-done.10 = s32[1,4]{1,0:T(1,128)S(1)} copy-done((s32[1,4]{1,0:T(1,128)S(1)}, s32[1,4]{1,0:T(1,128)}, u32[]{:S(2)}) %copy-start.10) | copy-done | bytes 40
  5.4 0.0 copy-done.7
  5.4 0.0 copy-done.8
  5.5 0.0 copy-done.9
  5.5 0.3 message.1
  5.8 0.0 collective-permute-start
  5.9 1.6 %collective-permute-start.1 = (s32[1,256]{1,0:T(1,128)S(1)}, s32[1,256]{1,0:T(1,128)S(1)}, u32[]{:S(2)}, u32[]{:S(2)}) collective-permute-start(s32[1,256]{1,0:T(1,128)S(1)} %get-tuple-element.37), channel_id=1, source_target_pairs={{0,4},{4,0},{8,12},{12,8},{16,20},{20,16},{24,28},{28,24},{1,5},{5... | collective-permute-start | bytes 3080 | tf_op jit(solution)/shard_map/ppermute | solution.py:35
  7.4 1.6 %collective-permute-start.2 = (s32[1,256]{1,0:T(1,128)S(1)}, s32[1,256]{1,0:T(1,128)S(1)}, u32[]{:S(2)}, u32[]{:S(2)}) collective-permute-start(s32[1,256]{1,0:T(1,128)S(1)} %get-tuple-element.38), channel_id=1, source_target_pairs={{0,2},{1,3},{2,0},{3,1},{4,6},{5,7},{6,4},{7,5},{8,10},{9,11},{10,... | collective-permute-start | bytes 3080 | tf_op jit(solution)/shard_map/ppermute | solution.py:35
  9.0 0.0 collective-permute-start.3
  9.0 0.0 collective-permute-done.refs_1_
  9.0 1.6 %collective-permute-start.4 = (s32[1,256]{1,0:T(1,128)S(1)}, s32[1,256]{1,0:T(1,128)S(1)}, u32[]{:S(2)}, u32[]{:S(2)}) collective-permute-start(s32[1,256]{1,0:T(1,128)S(1)} %get-tuple-element.40), channel_id=1, source_target_pairs={{0,8},{4,12},{8,0},{12,4},{16,24},{20,28},{24,16},{28,20},{1,9},{5... | collective-permute-start | bytes 3080 | tf_op jit(solution)/shard_map/ppermute | solution.py:35
  10.6 1.2 %copy-done.2 = bf16[1024,512]{1,0:T(8,128)(2,1)S(1)} copy-done((bf16[1024,512]{1,0:T(8,128)(2,1)S(1)}, bf16[1024,512]{1,0:T(8,128)(2,1)}, u32[]{:S(2)}) %copy-start.2) | copy-done | bytes 1048600
  11.8 0.1 load.1.history
  11.8 0.0 collective-permute-done.1.refs_1_
  11.9 0.0 collective-permute-done.2.refs_2_
  11.9 0.1 collective-permute-done.3.refs_3_
  12.0 0.7 %collective-permute-done.4.refs_2_.refs_0_ = s32[1,256]{1,0:T(1,128)S(1)} collective-permute-done((s32[1,256]{1,0:T(1,128)S(1)}, s32[1,256]{1,0:T(1,128)S(1)}, u32[]{:S(2)}, u32[]{:S(2)}) %collective-permute-start.4) | collective-permute-done | bytes 1056 | tf_op jit(solution)/shard_map/ppermute | solution.py:35
  12.7 0.7 %pull.1 = (bf16[128,512]{1,0:T(8,128)(2,1)S(1)}, bf16[128,512]{1,0:T(8,128)(2,1)S(1)}, bf16[128,512]{1,0:T(8,128)(2,1)S(1)}, bf16[128,512]{1,0:T(8,128)(2,1)S(1)}) custom-call(bf16[1024,512]{1,0:T(8,128)(2,1)S(1)} %load.1.history, s32[1,256]{1,0:T(1,128)S(1)} %get-tuple-element.42.refs_0_, s32[1,256]{1,0:T(1,128)S(1)} %collective-permute-done.refs_1_, ...), custom_call_target="tpu_custom_call" | custom-call | flops 536870912 | bytes 2097152 | tf_op jit(solution)/shard_map/pull/pallas_call | solution.py:245
  13.4 0.1 collective-permute-start.6
  13.5 1.6 %collective-permute-start.7 = (bf16[128,512]{1,0:T(8,128)(2,1)S(1)}, bf16[128,512]{1,0:T(8,128)(2,1)S(1)}, u32[]{:S(2)}, u32[]{:S(2)}) collective-permute-start(bf16[128,512]{1,0:T(8,128)(2,1)S(1)} %get-tuple-element.52), channel_id=1, source_target_pairs={{0,2},{1,3},{2,0},{3,1},{4,6},{5,7},{6,4},{7,5},{8,10},{9,11},{10,... | collective-permute-start | bytes 393224 | tf_op jit(solution)/shard_map/ppermute | solution.py:35
  15.0 0.3 collective-permute-start.8
  15.3 1.4 %collective-permute-start.12 = (s32[1,256]{1,0:T(1,128)S(1)}, s32[1,256]{1,0:T(1,128)S(1)}, u32[]{:S(2)}, u32[]{:S(2)}) collective-permute-start(s32[1,256]{1,0:T(1,128)S(1)} %get-tuple-element.56), channel_id=1, source_target_pairs={{0,12},{4,8},{8,4},{12,0},{16,28},{20,24},{24,20},{28,16},{1,13},{... | collective-permute-start | bytes 3080 | tf_op jit(solution)/shard_map/ppermute | solution.py:35
  16.8 0.0 copy-done
  16.8 0.1 pick_own.1
  16.9 0.0 collective-permute-done.6.after.refs_1_
  16.9 0.5 %collective-permute-start.9 = (bf16[64,512]{1,0:T(8,128)(2,1)S(1)}, bf16[64,512]{1,0:T(8,128)(2,1)S(1)}, u32[]{:S(2)}, u32[]{:S(2)}) collective-permute-start(bf16[64,512]{1,0:T(8,128)(2,1)S(1)} %pick_own.1), channel_id=1, source_target_pairs={{0,8},{4,12},{8,0},{12,4},{16,24},{20,28},{24,16},{28,20},{1,9},{5... | collective-permute-start | bytes 196616 | tf_op jit(solution)/shard_map/ppermute | solution.py:35
  17.4 0.0 collective-permute-done.5.far
  17.4 0.1 pick_far.1
  17.5 0.0 copy-start.6
  17.5 1.7 %collective-permute-start.10 = (bf16[128,512]{1,0:T(8,128)(2,1)S(1)}, bf16[128,512]{1,0:T(8,128)(2,1)S(1)}, u32[]{:S(2)}, u32[]{:S(2)}) collective-permute-start(bf16[128,512]{1,0:T(8,128)(2,1)S(1)} %get-tuple-element.54), channel_id=1, source_target_pairs={{0,4},{4,0},{8,12},{12,8},{16,20},{20,16},{24,28},{28,24},{1,5},{5... | collective-permute-start | bytes 393224 | tf_op jit(solution)/shard_map/ppermute | solution.py:35
  19.2 0.6 %collective-permute-done.12.refs_0_ = s32[1,256]{1,0:T(1,128)S(1)} collective-permute-done((s32[1,256]{1,0:T(1,128)S(1)}, s32[1,256]{1,0:T(1,128)S(1)}, u32[]{:S(2)}, u32[]{:S(2)}) %collective-permute-start.12) | collective-permute-done | bytes 1056 | tf_op jit(solution)/shard_map/ppermute | solution.py:35
  19.8 0.1 pick_two_hop.1
  19.9 1.5 %collective-permute-start.13 = (bf16[128,512]{1,0:T(8,128)(2,1)S(1)}, bf16[128,512]{1,0:T(8,128)(2,1)S(1)}, u32[]{:S(2)}, u32[]{:S(2)}) collective-permute-start(bf16[128,512]{1,0:T(8,128)(2,1)S(1)} %pick_two_hop.1), channel_id=1, source_target_pairs={{0,12},{4,8},{8,4},{12,0},{16,28},{20,24},{24,20},{28,16},{1,13},{... | collective-permute-start | bytes 393224 | tf_op jit(solution)/shard_map/ppermute | solution.py:35
  21.4 0.0 collective-permute-done.9.refs_4_
  21.4 0.4 %collective-permute-start.11 = (bf16[64,512]{1,0:T(8,128)(2,1)S(1)}, bf16[64,512]{1,0:T(8,128)(2,1)S(1)}, u32[]{:S(2)}, u32[]{:S(2)}) collective-permute-start(bf16[64,512]{1,0:T(8,128)(2,1)S(1)} %get-tuple-element.55), channel_id=1, source_target_pairs={{0,8},{4,12},{8,0},{12,4},{16,24},{20,28},{24,16},{28,20},{1,9},{5... | collective-permute-start | bytes 196616 | tf_op jit(solution)/shard_map/ppermute | solution.py:35
  21.9 0.0 copy-done.6
  21.9 0.2 copy-done.11
  22.1 0.6 %spread.1 = bf16[8,256,64]{2,1,0:T(8,128)(2,1)S(1)} custom-call(s32[2]{0:T(128)S(1)} %pad_add_fusion.after.place, s32[1,4]{1,0:T(1,128)S(1)} %copy-done.8, s32[1,4]{1,0:T(1,128)S(1)} %copy-done.11, bf16[4,64,64]{2,1,0:T(8,128)(2,1)S(1)} %copy-done.6, bf16[64,512]{1,0:T(8,128)(2,1)S(1)} %get-tuple-element.50.after.mine.first), custom_call_target="tpu_custom_call" | custom-call | bytes 262144 | tf_op jit(solution)/shard_map/spread/pallas_call | solution.py:291
  22.7 0.0 collective-permute-done.7.refs_2_
  22.7 0.0 collective-permute-done.8.refs_3_
  22.7 0.3 copy-done.3
  23.0 0.1 copy-done.4
  23.1 0.0 copy-done.5
  23.1 0.6 %partial.1.part = f32[256,512]{1,0:T(8,128)S(1)} custom-call(bf16[256,256]{1,0:T(8,128)(2,1)S(1)} %copy-done.5, bf16[256,512]{1,0:T(8,128)(2,1)S(1)} %copy-done, bf16[256,512]{1,0:T(8,128)(2,1)S(1)} %copy-done.3, bf16[256,512]{1,0:T(8,128)(2,1)S(1)} %copy-done.4, bf16[8,256,64]{2,1,0:T(8,128)(2,1)S(1)} %spread.1, ...), custom_call_target="tpu_custom_call" | custom-call | flops 201326592 | bytes 1572864 | tf_op jit(solution)/shard_map/partial/pallas_call | solution.py:301
  23.8 2.1 %collective-permute-done.11.refs_1_ = bf16[64,512]{1,0:T(8,128)(2,1)S(1)} collective-permute-done((bf16[64,512]{1,0:T(8,128)(2,1)S(1)}, bf16[64,512]{1,0:T(8,128)(2,1)S(1)}, u32[]{:S(2)}, u32[]{:S(2)}) %collective-permute-start.11) | collective-permute-done | bytes 65568 | tf_op jit(solution)/shard_map/ppermute | solution.py:35
  25.9 0.0 collective-permute-done.10.refs_0_
  25.9 0.3 collective-permute-done.13.refs_2_
  26.2 0.0 copy-done.1
  26.2 0.6 %final_sent.1 = (bf16[64,512]{1,0:T(8,128)(2,1)S(1)}, bf16[64,512]{1,0:T(8,128)(2,1)S(1)}, bf16[64,512]{1,0:T(8,128)(2,1)S(1)}) custom-call(bf16[64,512]{1,0:T(8,128)(2,1)S(1)} %get-tuple-element.50.after.mine.first, f32[256,512]{1,0:T(8,128)S(1)} %partial.1.part, bf16[8,256,64]{2,1,0:T(8,128)(2,1)S(1)} %spread.1, bf16[512,512]{1,0:T(8,128)(2,1)S(1)} %copy-done.1, ...), custom_call_target="tpu_custom_call" | custom-call | flops 100663296 | bytes 1179648 | tf_op jit(solution)/shard_map/final_sent/pallas_call | solution.py:313
  26.8 1.5 %collective-permute-start.14 = (bf16[64,512]{1,0:T(8,128)(2,1)S(1)}, bf16[64,512]{1,0:T(8,128)(2,1)S(1)}, u32[]{:S(2)}, u32[]{:S(2)}) collective-permute-start(bf16[64,512]{1,0:T(8,128)(2,1)S(1)} %get-tuple-element.58.refs_6_), channel_id=1, source_target_pairs={{0,2},{1,3},{2,0},{3,1},{4,6},{5,7},{6,4},{7,5},{8,10},{9,11},{10,... | collective-permute-start | bytes 196616 | tf_op jit(solution)/shard_map/ppermute | solution.py:35
  28.4 0.0 collective-permute-start.15
  28.4 0.7 %collective-permute-start.16 = (bf16[64,512]{1,0:T(8,128)(2,1)S(1)}, bf16[64,512]{1,0:T(8,128)(2,1)S(1)}, u32[]{:S(2)}, u32[]{:S(2)}) collective-permute-start(bf16[64,512]{1,0:T(8,128)(2,1)S(1)} %get-tuple-element.59.refs_7_), channel_id=1, source_target_pairs={{0,3},{1,2},{2,1},{3,0},{4,7},{5,6},{6,5},{7,4},{8,11},{9,10},{10,... | collective-permute-start | bytes 196616 | tf_op jit(solution)/shard_map/ppermute | solution.py:35
  29.0 0.4 %final_kept.1.refs_4_.refs_0_ = bf16[64,512]{1,0:T(8,128)(2,1)S(1)} custom-call(bf16[64,512]{1,0:T(8,128)(2,1)S(1)} %get-tuple-element.57.first.refs_5_, f32[256,512]{1,0:T(8,128)S(1)} %partial.1.part, bf16[8,256,64]{2,1,0:T(8,128)(2,1)S(1)} %spread.1, bf16[512,512]{1,0:T(8,128)(2,1)S(1)} %copy-done.1, bf16[128,512]{1,0:T(8,128)(2,1)S(1)} %collective-permute-done.10.refs_0_, ...), custom_call_target="tpu_custom_call" | custom-call | flops 33554432 | bytes 393216 | tf_op jit(solution)/shard_map/final_kept/pallas_call | solution.py:313
  29.4 1.0 %prepare.1 = (bf16[1024,512]{1,0:T(8,128)(2,1)S(1)}, bf16[1024,256]{1,0:T(8,128)(2,1)S(1)}, bf16[256,512]{1,0:T(8,128)(2,1)}) custom-call(bf16[1024,512]{1,0:T(8,128)(2,1)S(1)} %load.1.history, s32[1,256]{1,0:T(1,128)S(1)} %get-tuple-element.42.refs_0_, s32[1,256]{1,0:T(1,128)S(1)} %collective-permute-done.refs_1_, ...), custom_call_target="tpu_custom_call" | custom-call | flops 2097152 | bytes 3145728 | tf_op jit(solution)/shard_map/prepare/pallas_call | solution.py:329
  30.4 0.7 %collective-permute-done.14.refs_2_ = bf16[64,512]{1,0:T(8,128)(2,1)S(1)} collective-permute-done((bf16[64,512]{1,0:T(8,128)(2,1)S(1)}, bf16[64,512]{1,0:T(8,128)(2,1)S(1)}, u32[]{:S(2)}, u32[]{:S(2)}) %collective-permute-start.14) | collective-permute-done | bytes 65568 | tf_op jit(solution)/shard_map/ppermute | solution.py:35
  31.2 0.0 collective-permute-done.15.refs_1_
  31.2 1.0 %collective-permute-done.16.refs_3_ = bf16[64,512]{1,0:T(8,128)(2,1)S(1)} collective-permute-done((bf16[64,512]{1,0:T(8,128)(2,1)S(1)}, bf16[64,512]{1,0:T(8,128)(2,1)S(1)}, u32[]{:S(2)}, u32[]{:S(2)}) %collective-permute-start.16) | collective-permute-done | bytes 65568 | tf_op jit(solution)/shard_map/ppermute | solution.py:35
  32.1 1.2 %scatter.1 = bf16[1024,512]{1,0:T(8,128)(2,1)} custom-call(bf16[1024,512]{1,0:T(8,128)(2,1)S(1)} %get-tuple-element.61.base, bf16[1024,256]{1,0:T(8,128)(2,1)S(1)} %get-tuple-element.62.hot, bf16[64,512]{1,0:T(8,128)(2,1)S(1)} %final_kept.1.refs_4_.refs_0_, bf16[64,512]{1,0:T(8,128)(2,1)S(1)} %collective-permute-done.15.refs_1_, ...), custom_call_target="tpu_custom_call" | custom-call | tf_op jit(solution)/shard_map/scatter/pallas_call | solution.py:343
  (7 shorter events, 0.0 us)
Async XLA Ops:
  0.6 16.8 %collective-permute-start.5 = (bf16[256,512]{1,0:T(8,128)(2,1)}, bf16[256,512]{1,0:T(8,128)(2,1)S(1)}, u32[]{:S(2)}, u32[]{:S(2)}) collective-permute-start(bf16[256,512]{1,0:T(8,128)(2,1)} %hidden.7), channel_id=1, source_target_pairs={{0,16},{4,20},{8,24},{12,28},{16,0},{20,4},{24,8},{28,12},{1,17},{... | collective-permute-start | bytes 786440 | tf_op jit(solution)/shard_map/ppermute | solution.py:35
  4.7 0.7 %copy-start.10 = (s32[1,4]{1,0:T(1,128)S(1)}, s32[1,4]{1,0:T(1,128)}, u32[]{:S(2)}) copy-start(s32[1,4]{1,0:T(1,128)} %count.1) | copy-start | bytes 52
  4.7 0.7 %copy-start.7 = (s32[1,4,128]{2,1,0:T(4,128)S(1)}, s32[1,4,128]{2,1,0:T(4,128)}, u32[]{:S(2)}) copy-start(s32[1,4,128]{2,1,0:T(4,128)} %rows.1) | copy-start | bytes 6148
  4.8 0.7 %copy-start.8 = (s32[1,4]{1,0:T(1,128)S(1)}, s32[1,4]{1,0:T(1,128)}, u32[]{:S(2)}) copy-start(s32[1,4]{1,0:T(1,128)} %src.3) | copy-start | bytes 52
  4.8 0.7 %copy-start.9 = (s32[256]{0:T(256)S(1)}, s32[256]{0:T(256)}, u32[]{:S(2)}) copy-start(s32[256]{0:T(256)} %param.23) | copy-start | bytes 3076
  5.8 3.2 %collective-permute-start = (s32[1,256]{1,0:T(1,128)S(1)}, s32[1,256]{1,0:T(1,128)S(1)}, u32[]{:S(2)}, u32[]{:S(2)}) collective-permute-start(s32[1,256]{1,0:T(1,128)S(1)} %get-tuple-element.36), channel_id=1, source_target_pairs={{0,1},{1,0},{2,3},{3,2},{4,5},{5,4},{6,7},{7,6},{8,9},{9,8},{10,11... | collective-permute-start | bytes 3080 | tf_op jit(solution)/shard_map/ppermute | solution.py:35
  5.9 6.0 %collective-permute-start.1 = (s32[1,256]{1,0:T(1,128)S(1)}, s32[1,256]{1,0:T(1,128)S(1)}, u32[]{:S(2)}, u32[]{:S(2)}) collective-permute-start(s32[1,256]{1,0:T(1,128)S(1)} %get-tuple-element.37), channel_id=1, source_target_pairs={{0,4},{4,0},{8,12},{12,8},{16,20},{20,16},{24,28},{28,24},{1,5},{5... | collective-permute-start | bytes 3080 | tf_op jit(solution)/shard_map/ppermute | solution.py:35
  7.4 4.4 %collective-permute-start.2 = (s32[1,256]{1,0:T(1,128)S(1)}, s32[1,256]{1,0:T(1,128)S(1)}, u32[]{:S(2)}, u32[]{:S(2)}) collective-permute-start(s32[1,256]{1,0:T(1,128)S(1)} %get-tuple-element.38), channel_id=1, source_target_pairs={{0,2},{1,3},{2,0},{3,1},{4,6},{5,7},{6,4},{7,5},{8,10},{9,11},{10,... | collective-permute-start | bytes 3080 | tf_op jit(solution)/shard_map/ppermute | solution.py:35
  9.0 3.0 %collective-permute-start.3 = (s32[1,256]{1,0:T(1,128)S(1)}, s32[1,256]{1,0:T(1,128)S(1)}, u32[]{:S(2)}, u32[]{:S(2)}) collective-permute-start(s32[1,256]{1,0:T(1,128)S(1)} %get-tuple-element.39), channel_id=1, source_target_pairs={{0,3},{1,2},{2,1},{3,0},{4,7},{5,6},{6,5},{7,4},{8,11},{9,10},{10,... | collective-permute-start | bytes 3080 | tf_op jit(solution)/shard_map/ppermute | solution.py:35
  9.0 3.7 %collective-permute-start.4 = (s32[1,256]{1,0:T(1,128)S(1)}, s32[1,256]{1,0:T(1,128)S(1)}, u32[]{:S(2)}, u32[]{:S(2)}) collective-permute-start(s32[1,256]{1,0:T(1,128)S(1)} %get-tuple-element.40), channel_id=1, source_target_pairs={{0,8},{4,12},{8,0},{12,4},{16,24},{20,28},{24,16},{28,20},{1,9},{5... | collective-permute-start | bytes 3080 | tf_op jit(solution)/shard_map/ppermute | solution.py:35
  10.6 1.2 %copy-start.2 = (bf16[1024,512]{1,0:T(8,128)(2,1)S(1)}, bf16[1024,512]{1,0:T(8,128)(2,1)}, u32[]{:S(2)}) copy-start(bf16[1024,512]{1,0:T(8,128)(2,1)} %history.1) | copy-start | bytes 3145732
  12.6 4.1 %copy-start = (bf16[256,512]{1,0:T(8,128)(2,1)S(1)}, bf16[256,512]{1,0:T(8,128)(2,1)}, u32[]{:S(2)}) copy-start(bf16[256,512]{1,0:T(8,128)(2,1)} %hidden.7) | copy-start | bytes 786436
  13.4 3.5 %collective-permute-start.6 = (bf16[128,512]{1,0:T(8,128)(2,1)S(1)}, bf16[128,512]{1,0:T(8,128)(2,1)S(1)}, u32[]{:S(2)}, u32[]{:S(2)}) collective-permute-start(bf16[128,512]{1,0:T(8,128)(2,1)S(1)} %get-tuple-element.46), channel_id=1, source_target_pairs={{0,1},{1,0},{2,3},{3,2},{4,5},{5,4},{6,7},{7,6},{8,9},{9,8},{10,11... | collective-permute-start | bytes 393224 | tf_op jit(solution)/shard_map/ppermute | solution.py:35
  13.5 9.2 %collective-permute-start.7 = (bf16[128,512]{1,0:T(8,128)(2,1)S(1)}, bf16[128,512]{1,0:T(8,128)(2,1)S(1)}, u32[]{:S(2)}, u32[]{:S(2)}) collective-permute-start(bf16[128,512]{1,0:T(8,128)(2,1)S(1)} %get-tuple-element.52), channel_id=1, source_target_pairs={{0,2},{1,3},{2,0},{3,1},{4,6},{5,7},{6,4},{7,5},{8,10},{9,11},{10,... | collective-permute-start | bytes 393224 | tf_op jit(solution)/shard_map/ppermute | solution.py:35
  15.0 7.7 %collective-permute-start.8 = (bf16[128,512]{1,0:T(8,128)(2,1)S(1)}, bf16[128,512]{1,0:T(8,128)(2,1)S(1)}, u32[]{:S(2)}, u32[]{:S(2)}) collective-permute-start(bf16[128,512]{1,0:T(8,128)(2,1)S(1)} %get-tuple-element.53), channel_id=1, source_target_pairs={{0,3},{1,2},{2,1},{3,0},{4,7},{5,6},{6,5},{7,4},{8,11},{9,10},{10,... | collective-permute-start | bytes 393224 | tf_op jit(solution)/shard_map/ppermute | solution.py:35
  15.3 4.5 %collective-permute-start.12 = (s32[1,256]{1,0:T(1,128)S(1)}, s32[1,256]{1,0:T(1,128)S(1)}, u32[]{:S(2)}, u32[]{:S(2)}) collective-permute-start(s32[1,256]{1,0:T(1,128)S(1)} %get-tuple-element.56), channel_id=1, source_target_pairs={{0,12},{4,8},{8,4},{12,0},{16,28},{20,24},{24,20},{28,16},{1,13},{... | collective-permute-start | bytes 3080 | tf_op jit(solution)/shard_map/ppermute | solution.py:35
  16.9 4.5 %collective-permute-start.9 = (bf16[64,512]{1,0:T(8,128)(2,1)S(1)}, bf16[64,512]{1,0:T(8,128)(2,1)S(1)}, u32[]{:S(2)}, u32[]{:S(2)}) collective-permute-start(bf16[64,512]{1,0:T(8,128)(2,1)S(1)} %pick_own.1), channel_id=1, source_target_pairs={{0,8},{4,12},{8,0},{12,4},{16,24},{20,28},{24,16},{28,20},{1,9},{5... | collective-permute-start | bytes 196616 | tf_op jit(solution)/shard_map/ppermute | solution.py:35
  17.5 4.4 %copy-start.6 = (bf16[4,64,64]{2,1,0:T(8,128)(2,1)S(1)}, bf16[4,64,64]{2,1,0:T(8,128)(2,1)}, u32[]{:S(2)}) copy-start(bf16[4,64,64]{2,1,0:T(8,128)(2,1)} %tiles.1) | copy-start | bytes 98308
  17.5 8.4 %collective-permute-start.10 = (bf16[128,512]{1,0:T(8,128)(2,1)S(1)}, bf16[128,512]{1,0:T(8,128)(2,1)S(1)}, u32[]{:S(2)}, u32[]{:S(2)}) collective-permute-start(bf16[128,512]{1,0:T(8,128)(2,1)S(1)} %get-tuple-element.54), channel_id=1, source_target_pairs={{0,4},{4,0},{8,12},{12,8},{16,20},{20,16},{24,28},{28,24},{1,5},{5... | collective-permute-start | bytes 393224 | tf_op jit(solution)/shard_map/ppermute | solution.py:35
  19.9 6.3 %collective-permute-start.13 = (bf16[128,512]{1,0:T(8,128)(2,1)S(1)}, bf16[128,512]{1,0:T(8,128)(2,1)S(1)}, u32[]{:S(2)}, u32[]{:S(2)}) collective-permute-start(bf16[128,512]{1,0:T(8,128)(2,1)S(1)} %pick_two_hop.1), channel_id=1, source_target_pairs={{0,12},{4,8},{8,4},{12,0},{16,28},{20,24},{24,20},{28,16},{1,13},{... | collective-permute-start | bytes 393224 | tf_op jit(solution)/shard_map/ppermute | solution.py:35
  21.4 0.7 %copy-start.11 = (s32[1,4]{1,0:T(1,128)S(1)}, s32[1,4]{1,0:T(1,128)}, u32[]{:S(2)}) copy-start(s32[1,4]{1,0:T(1,128)} %dst.1) | copy-start | bytes 52
  21.4 4.5 %collective-permute-start.11 = (bf16[64,512]{1,0:T(8,128)(2,1)S(1)}, bf16[64,512]{1,0:T(8,128)(2,1)S(1)}, u32[]{:S(2)}, u32[]{:S(2)}) collective-permute-start(bf16[64,512]{1,0:T(8,128)(2,1)S(1)} %get-tuple-element.55), channel_id=1, source_target_pairs={{0,8},{4,12},{8,0},{12,4},{16,24},{20,28},{24,16},{28,20},{1,9},{5... | collective-permute-start | bytes 196616 | tf_op jit(solution)/shard_map/ppermute | solution.py:35
  22.1 0.9 %copy-start.3 = (bf16[256,512]{1,0:T(8,128)(2,1)S(1)}, bf16[256,512]{1,0:T(8,128)(2,1)}, u32[]{:S(2)}) copy-start(bf16[256,512]{1,0:T(8,128)(2,1)} %pull_adj.1) | copy-start | bytes 786436
  22.1 1.0 %copy-start.4 = (bf16[256,512]{1,0:T(8,128)(2,1)S(1)}, bf16[256,512]{1,0:T(8,128)(2,1)}, u32[]{:S(2)}) copy-start(bf16[256,512]{1,0:T(8,128)(2,1)} %initial.1) | copy-start | bytes 786436
  22.1 1.1 %copy-start.5 = (bf16[256,256]{1,0:T(8,128)(2,1)S(1)}, bf16[256,256]{1,0:T(8,128)(2,1)}, u32[]{:S(2)}) copy-start(bf16[256,256]{1,0:T(8,128)(2,1)} %own_adj.1) | copy-start | bytes 393220
  23.1 3.1 %copy-start.1 = (bf16[512,512]{1,0:T(8,128)(2,1)S(1)}, bf16[512,512]{1,0:T(8,128)(2,1)}, u32[]{:S(2)}) copy-start(bf16[512,512]{1,0:T(8,128)(2,1)} %weight.3) | copy-start | bytes 1572868
  26.8 4.3 %collective-permute-start.14 = (bf16[64,512]{1,0:T(8,128)(2,1)S(1)}, bf16[64,512]{1,0:T(8,128)(2,1)S(1)}, u32[]{:S(2)}, u32[]{:S(2)}) collective-permute-start(bf16[64,512]{1,0:T(8,128)(2,1)S(1)} %get-tuple-element.58.refs_6_), channel_id=1, source_target_pairs={{0,2},{1,3},{2,0},{3,1},{4,6},{5,7},{6,4},{7,5},{8,10},{9,11},{10,... | collective-permute-start | bytes 196616 | tf_op jit(solution)/shard_map/ppermute | solution.py:35
  28.4 2.8 %collective-permute-start.15 = (bf16[64,512]{1,0:T(8,128)(2,1)S(1)}, bf16[64,512]{1,0:T(8,128)(2,1)S(1)}, u32[]{:S(2)}, u32[]{:S(2)}) collective-permute-start(bf16[64,512]{1,0:T(8,128)(2,1)S(1)} %get-tuple-element.57.first.refs_5_), channel_id=1, source_target_pairs={{0,1},{1,0},{2,3},{3,2},{4,5},{5,4},{6,7},{7,6},{8,9},{9,8},{10,11... | collective-permute-start | bytes 196616 | tf_op jit(solution)/shard_map/ppermute | solution.py:35
  28.4 3.7 %collective-permute-start.16 = (bf16[64,512]{1,0:T(8,128)(2,1)S(1)}, bf16[64,512]{1,0:T(8,128)(2,1)S(1)}, u32[]{:S(2)}, u32[]{:S(2)}) collective-permute-start(bf16[64,512]{1,0:T(8,128)(2,1)S(1)} %get-tuple-element.59.refs_7_), channel_id=1, source_target_pairs={{0,3},{1,2},{2,1},{3,0},{4,7},{5,6},{6,5},{7,4},{8,11},{9,10},{10,... | collective-permute-start | bytes 196616 | tf_op jit(solution)/shard_map/ppermute | solution.py:35

commit v8 on v7

--- a/solution.py
+++ b/solution.py
@@ -45,7 +45,8 @@
     for k in range(n_half):
         for slot, wanted in enumerate((k + n_half, k)):
             found = jnp.sum(jnp.where(name == wanted, local, 0), axis=1, keepdims=True)
-            to_half[k][:, slot * 128 : slot * 128 + 128] = jnp.broadcast_to(found, (1, 128))
+            at = k % 2 * 256 + slot * 128
+            to_half[k // 2][:, at : at + 128] = jnp.broadcast_to(found, (1, 128))
     owner = lax.broadcasted_iota(jnp.int32, count.shape, 1)
     lane = lax.broadcasted_iota(jnp.int32, (1, cap), 1)
     for k in range(n_hist):
@@ -58,8 +59,9 @@
         to_hist[k][:, cap : cap + per_owner] = pushed
 
 
-def pick(held, asked, slot, rows):
-    wanted = asked[:, slot * 128 : slot * 128 + 1]
+def pick(held, asked, k, slot, rows):
+    at = k % 2 * 256 + slot * 128
+    wanted = asked[:, at : at + 1]
     block = held[:rows, :]
     for j in range(1, held.shape[0] // rows):
         block = jnp.where(
@@ -69,21 +71,15 @@
 
 
 def one_hop(k):
-    return k > 1 and k & (k - 1) == 0
-
-
-def pick_own_kernel(hidden, *refs):
-    asked, outs = refs[: len(refs) // 2], refs[len(refs) // 2 :]
-    for one, out in zip(asked, outs):
-        out[...] = pick(hidden, one, 1, out.shape[0])
+    return False
 
 
 def pick_far_kernel(rows, peers, hidden, far, after, *refs):
     asked, outs = refs[: len(peers)], refs[len(peers) :]
-    for one, out in zip(asked, outs):
-        out[:rows, :] = pick(far, one, 0, rows)
+    for k, one, out in zip(peers, asked, outs):
+        out[:rows, :] = pick(far, one, k, 0, rows)
         if out.shape[0] > rows:
-            out[rows:, :] = pick(hidden, one, 1, rows)
+            out[rows:, :] = pick(hidden, one, k, 1, rows)
 
 
 def spread_kernel(per_dev, place, src, dst, tiles, after, out):
@@ -216,13 +212,17 @@
     asks = pl.pallas_call(
         functools.partial(message_kernel, n_hist, n_half, per_dev),
         out_shape=[shape((1, cap + 128), jnp.int32)] * n_hist
-        + [shape((1, 256), jnp.int32) for k in range(n_half)],
+        + [shape((1, 512), jnp.int32)] * (n_half // 2),
         in_specs=[anywhere] + [vmem()] * 4,
-        out_specs=[vmem()] * (n_hist + n_half),
+        out_specs=[vmem()] * (n_hist + n_half // 2),
         compiler_params=params(),
         name="message",
     )(place, tile_src, pull_count, pull_rows, push_rows.reshape(1, rows_dev))
-    wanted = [asks[n_hist]] + [swap(asks[n_hist + k], "blk", n_blk, k) for k in range(1, n_half)]
+    came = [asks[n_hist]]
+    came += [swap(asks[n_hist + k // 2], "blk", n_blk, k) for k in range(2, n_half, 2)]
+    wanted = [None] * n_half
+    wanted[0::2] = came
+    wanted[1] = swap(came[0], "blk", n_blk, 1)
     asked = [asks[0]] + [swap(asks[k], "hist", n_hist, k) for k in range(1, n_hist)]
     history = pl.pallas_call(
         load_kernel,
@@ -233,7 +233,7 @@
         cost_estimate=cost(0, held * feature * 4),
         name="load",
     )(history)
-    ones = [k for k in range(1, n_half) if k & (k - 1) == 0]
+    ones = [1, *range(2, n_half, 2)]
     first = [asked[1], wanted[1], *asked[2:], *[wanted[k] for k in ones[1:]]]
     asked[0], wanted[0], first, history = lax.optimization_barrier(
         (asked[0], wanted[0], first, history)
@@ -241,6 +241,7 @@
     asked[1:], wanted[1] = [first[0], *first[2 : n_hist]], first[1]
     for k, one in zip(ones[1:], first[n_hist:]):
         wanted[k] = one
+    wanted[3::2] = [swap(one, "blk", n_blk, 1) for one in wanted[2::2]]
 
     fetched = pl.pallas_call(
         functools.partial(pull_kernel, n_hist, cap),
@@ -255,15 +256,7 @@
 
     peers = range(1, n_half)
     soon = [k for k in peers if one_hop(k)]
-    picked = pl.pallas_call(
-        pick_own_kernel,
-        out_shape=[shape((block_rows, feature))] * len(soon),
-        in_specs=[vmem()] * (1 + len(soon)),
-        out_specs=[vmem()] * len(soon),
-        compiler_params=params(),
-        cost_estimate=cost(0, n_half * 4 * block_rows * feature),
-        name="pick_own",
-    )(hidden, *[wanted[k] for k in soon])
+    picked = []
     early = [swap(one, "blk", n_blk, k) for one, k in zip(picked, soon)]
 
     def pick_far(peers, name):
@@ -298,6 +291,7 @@
         name="spread",
     )(place, tile_src, tile_dst, tiles, mine)
 
+    late[1], late[0], late[2] = lax.optimization_barrier((late[1], late[0], late[2]))
     part = pl.pallas_call(
         functools.partial(partial_kernel, n_hist, n_half, cap),
         out_shape=shape((rows_dev, feature), jnp.float32),

time: 33.6 us -> 33.4 us (level)
  waiting for transfers between devices: 5.55 us -> 7.96 us
  starting transfers between devices: 18.5 us -> 16.7 us
  local copies, waits for them, and re-layouts: 2.55 us -> 1.95 us
    ppermute x17 -> x16, waiting for transfers between devices: 5.55 us -> 7.96 us  [swap(): return lax.ppermute(x, axis, [(i, i ^ k) for i in range(n)])]
    ppermute x17 -> x16, starting transfers between devices: 18.5 us -> 16.7 us  [swap(): return lax.ppermute(x, axis, [(i, i ^ k) for i in range(n)])]
    unnamed x24, local copies, waits for them, and re-layouts: 2.55 us -> 1.95 us
  transfers between devices with their start and end apart: 17 -> 16, of which waited for: 7 -> 9; matrix products, arithmetic and copies ran while one was open for 0% -> 0% of each run, Pallas kernels for 12% -> 12%
where the time goes in v8:
time: 33.4 us; the launch traced here: 33.2 us
  starting transfers between devices  16.7 us (50%)
  waiting for transfers between devices  7.96 us (24%)
  Pallas kernels  5.77 us (17%)
  local copies, waits for them, and re-layouts  1.95 us (6%)
  between operations  0.78 us (2%)
    ppermute x16, starting transfers between devices, swap(): return lax.ppermute(x, axis, [(i, i ^ k) for i in range(n)])  16.7 us
    ppermute x16, waiting for transfers between devices, swap(): return lax.ppermute(x, axis, [(i, i ^ k) for i in range(n)])  7.96 us
    unnamed x24, local copies, waits for them, and re-layouts  1.95 us
    pallas_call x1, Pallas kernels, local(): pl.pallas_call(functools.partial(scatter_kernel, steps), out_shape=shape(...  1.23 us
    pallas_call x2, Pallas kernels, final(): pl.pallas_call(functools.partial(final_kernel, n_half, chunks), out_shape...  1.05 us
    pallas_call x1, Pallas kernels, local(): pl.pallas_call(functools.partial(prepare_kernel, n_hist, cap), out_shape=...  0.98 us
    pallas_call x1, Pallas kernels, local(): pl.pallas_call(functools.partial(pull_kernel, n_hist, cap), out_shape=[sh...  0.75 us
  transfers between devices with their start and end apart: 16, of which 9 were waited for; matrix products, arithmetic and copies ran while one was open for 0% of the time, Pallas kernels for 12%

profile of v8, /device:TPU:0, one launch (start us, length us, event | category | flops | bytes accessed | tf_op | source)
XLA Modules:
  0.0 33.2 jit_solution(135143890374499687)
XLA Ops:
  0.6 4.1 %collective-permute-start.5 = (bf16[256,512]{1,0:T(8,128)(2,1)}, bf16[256,512]{1,0:T(8,128)(2,1)S(1)}, u32[]{:S(2)}, u32[]{:S(2)}) collective-permute-start(bf16[256,512]{1,0:T(8,128)(2,1)} %hidden.5), channel_id=1, source_target_pairs={{0,16},{4,20},{8,24},{12,28},{16,0},{20,4},{24,8},{28,12},{1,17},{... | collective-permute-start | bytes 786440 | tf_op jit(solution)/shard_map/ppermute | solution.py:35
  4.7 0.0 copy-start.10
  4.7 0.0 copy-start.7
  4.7 0.1 pad_add_fusion.after.place
  4.8 0.0 copy-start.8
  4.8 0.0 copy-start.9
  4.8 0.6 %copy-done.10 = s32[1,4]{1,0:T(1,128)S(1)} copy-done((s32[1,4]{1,0:T(1,128)S(1)}, s32[1,4]{1,0:T(1,128)}, u32[]{:S(2)}) %copy-start.10) | copy-done | bytes 40
  5.4 0.0 copy-done.7
  5.4 0.0 copy-done.8
  5.5 0.0 copy-done.9
  5.5 0.3 message.1
  5.8 0.0 collective-permute-start
  5.9 1.6 %collective-permute-start.1 = (s32[1,512]{1,0:T(1,128)S(1)}, s32[1,512]{1,0:T(1,128)S(1)}, u32[]{:S(2)}, u32[]{:S(2)}) collective-permute-start(s32[1,512]{1,0:T(1,128)S(1)} %get-tuple-element.47.refs_0_), channel_id=1, source_target_pairs={{0,4},{4,0},{8,12},{12,8},{16,20},{20,16},{24,28},{28,24},{1,5},{5... | collective-permute-start | bytes 6152 | tf_op jit(solution)/shard_map/ppermute | solution.py:35
  7.4 1.6 %collective-permute-start.4 = (s32[1,512]{1,0:T(1,128)S(1)}, s32[1,512]{1,0:T(1,128)S(1)}, u32[]{:S(2)}, u32[]{:S(2)}) collective-permute-start(s32[1,512]{1,0:T(1,128)S(1)} %get-tuple-element.40), channel_id=1, source_target_pairs={{0,8},{4,12},{8,0},{12,4},{16,24},{20,28},{24,16},{28,20},{1,9},{5... | collective-permute-start | bytes 6152 | tf_op jit(solution)/shard_map/ppermute | solution.py:35
  9.0 1.5 %collective-permute-start.2 = (s32[1,256]{1,0:T(1,128)S(1)}, s32[1,256]{1,0:T(1,128)S(1)}, u32[]{:S(2)}, u32[]{:S(2)}) collective-permute-start(s32[1,256]{1,0:T(1,128)S(1)} %get-tuple-element.38), channel_id=1, source_target_pairs={{0,2},{1,3},{2,0},{3,1},{4,6},{5,7},{6,4},{7,5},{8,10},{9,11},{10,... | collective-permute-start | bytes 3080 | tf_op jit(solution)/shard_map/ppermute | solution.py:35
  10.5 0.0 collective-permute-done.refs_1_
  10.5 0.0 collective-permute-start.3
  10.5 0.0 copy-start.2
  10.5 1.2 %copy-done.2 = bf16[1024,512]{1,0:T(8,128)(2,1)S(1)} copy-done((bf16[1024,512]{1,0:T(8,128)(2,1)S(1)}, bf16[1024,512]{1,0:T(8,128)(2,1)}, u32[]{:S(2)}) %copy-start.2) | copy-done | bytes 1048600
  11.7 0.1 load.1.history
  11.8 0.7 %collective-permute-done.2.refs_2_ = s32[1,256]{1,0:T(1,128)S(1)} collective-permute-done((s32[1,256]{1,0:T(1,128)S(1)}, s32[1,256]{1,0:T(1,128)S(1)}, u32[]{:S(2)}, u32[]{:S(2)}) %collective-permute-start.2) | collective-permute-done | bytes 1056 | tf_op jit(solution)/shard_map/ppermute | solution.py:35
  12.6 0.9 %collective-permute-done.3.refs_3_ = s32[1,256]{1,0:T(1,128)S(1)} collective-permute-done((s32[1,256]{1,0:T(1,128)S(1)}, s32[1,256]{1,0:T(1,128)S(1)}, u32[]{:S(2)}, u32[]{:S(2)}) %collective-permute-start.3) | collective-permute-done | bytes 1056 | tf_op jit(solution)/shard_map/ppermute | solution.py:35
  13.5 0.0 collective-permute-done.1.refs_1_
  13.5 0.0 collective-permute-done.4.refs_2_
  13.5 0.7 %pull.1 = (bf16[128,512]{1,0:T(8,128)(2,1)S(1)}, bf16[128,512]{1,0:T(8,128)(2,1)S(1)}, bf16[128,512]{1,0:T(8,128)(2,1)S(1)}, bf16[128,512]{1,0:T(8,128)(2,1)S(1)}) custom-call(bf16[1024,512]{1,0:T(8,128)(2,1)S(1)} %load.1.history, s32[1,256]{1,0:T(1,128)S(1)} %get-tuple-element.42.refs_0_, s32[1,256]{1,0:T(1,128)S(1)} %collective-permute-done.refs_1_, ...), custom_call_target="tpu_custom_call" | custom-call | flops 536870912 | bytes 2097152 | tf_op jit(solution)/shard_map/pull/pallas_call | solution.py:246
  14.3 0.1 collective-permute-start.6
  14.4 0.7 %collective-permute-start.7 = (bf16[128,512]{1,0:T(8,128)(2,1)S(1)}, bf16[128,512]{1,0:T(8,128)(2,1)S(1)}, u32[]{:S(2)}, u32[]{:S(2)}) collective-permute-start(bf16[128,512]{1,0:T(8,128)(2,1)S(1)} %get-tuple-element.52), channel_id=1, source_target_pairs={{0,2},{1,3},{2,0},{3,1},{4,6},{5,7},{6,4},{7,5},{8,10},{9,11},{10,... | collective-permute-start | bytes 393224 | tf_op jit(solution)/shard_map/ppermute | solution.py:35
  15.0 1.2 %collective-permute-start.8 = (bf16[128,512]{1,0:T(8,128)(2,1)S(1)}, bf16[128,512]{1,0:T(8,128)(2,1)S(1)}, u32[]{:S(2)}, u32[]{:S(2)}) collective-permute-start(bf16[128,512]{1,0:T(8,128)(2,1)S(1)} %get-tuple-element.53), channel_id=1, source_target_pairs={{0,3},{1,2},{2,1},{3,0},{4,7},{5,6},{6,5},{7,4},{8,11},{9,10},{10,... | collective-permute-start | bytes 393224 | tf_op jit(solution)/shard_map/ppermute | solution.py:35
  16.2 0.5 %collective-permute-start.11 = (s32[1,512]{1,0:T(1,128)S(1)}, s32[1,512]{1,0:T(1,128)S(1)}, u32[]{:S(2)}, u32[]{:S(2)}) collective-permute-start(s32[1,512]{1,0:T(1,128)S(1)} %collective-permute-done.4.refs_2_), channel_id=1, source_target_pairs={{0,4},{4,0},{8,12},{12,8},{16,20},{20,16},{24,28},{28,24},{1,5},{5... | collective-permute-start | bytes 6152 | tf_op jit(solution)/shard_map/ppermute | solution.py:35
  16.8 0.0 collective-permute-done.6.after.refs_1_
  16.8 0.1 collective-permute-done.5.far
  16.9 0.0 copy-done
  16.9 0.1 pick_far.1
  17.0 0.9 %collective-permute-start.9 = (bf16[128,512]{1,0:T(8,128)(2,1)S(1)}, bf16[128,512]{1,0:T(8,128)(2,1)S(1)}, u32[]{:S(2)}, u32[]{:S(2)}) collective-permute-start(bf16[128,512]{1,0:T(8,128)(2,1)S(1)} %get-tuple-element.54), channel_id=1, source_target_pairs={{0,8},{4,12},{8,0},{12,4},{16,24},{20,28},{24,16},{28,20},{1,9},{5... | collective-permute-start | bytes 393224 | tf_op jit(solution)/shard_map/ppermute | solution.py:35
  17.9 1.5 %collective-permute-start.10 = (bf16[128,512]{1,0:T(8,128)(2,1)S(1)}, bf16[128,512]{1,0:T(8,128)(2,1)S(1)}, u32[]{:S(2)}, u32[]{:S(2)}) collective-permute-start(bf16[128,512]{1,0:T(8,128)(2,1)S(1)} %get-tuple-element.55), channel_id=1, source_target_pairs={{0,4},{4,0},{8,12},{12,8},{16,20},{20,16},{24,28},{28,24},{1,5},{5... | collective-permute-start | bytes 393224 | tf_op jit(solution)/shard_map/ppermute | solution.py:35
  19.4 0.4 %collective-permute-done.11.refs_0_ = s32[1,512]{1,0:T(1,128)S(1)} collective-permute-done((s32[1,512]{1,0:T(1,128)S(1)}, s32[1,512]{1,0:T(1,128)S(1)}, u32[]{:S(2)}, u32[]{:S(2)}) %collective-permute-start.11) | collective-permute-done | bytes 2080 | tf_op jit(solution)/shard_map/ppermute | solution.py:35
  19.8 0.1 pick_two_hop.1
  19.9 0.0 copy-start.11
  19.9 0.8 %collective-permute-start.12 = (bf16[128,512]{1,0:T(8,128)(2,1)S(1)}, bf16[128,512]{1,0:T(8,128)(2,1)S(1)}, u32[]{:S(2)}, u32[]{:S(2)}) collective-permute-start(bf16[128,512]{1,0:T(8,128)(2,1)S(1)} %pick_two_hop.1), channel_id=1, source_target_pairs={{0,12},{4,8},{8,4},{12,0},{16,28},{20,24},{24,20},{28,16},{1,13},{... | collective-permute-start | bytes 393224 | tf_op jit(solution)/shard_map/ppermute | solution.py:35
  20.7 0.0 copy-done.6
  20.7 0.0 copy-done.11
  20.7 0.0 copy-start.5
  20.8 0.6 %spread.1 = bf16[8,256,64]{2,1,0:T(8,128)(2,1)S(1)} custom-call(s32[2]{0:T(128)S(1)} %pad_add_fusion.after.place, s32[1,4]{1,0:T(1,128)S(1)} %copy-done.8, s32[1,4]{1,0:T(1,128)S(1)} %copy-done.11, bf16[4,64,64]{2,1,0:T(8,128)(2,1)S(1)} %copy-done.6, bf16[64,512]{1,0:T(8,128)(2,1)S(1)} %get-tuple-element.50.after.mine.first), custom_call_target="tpu_custom_call" | custom-call | bytes 262144 | tf_op jit(solution)/shard_map/spread/pallas_call | solution.py:284
  21.4 0.0 collective-permute-done.7.refs_2_
  21.4 1.2 %collective-permute-done.8.refs_3_ = bf16[128,512]{1,0:T(8,128)(2,1)S(1)} collective-permute-done((bf16[128,512]{1,0:T(8,128)(2,1)S(1)}, bf16[128,512]{1,0:T(8,128)(2,1)S(1)}, u32[]{:S(2)}, u32[]{:S(2)}) %collective-permute-start.8) | collective-permute-done | bytes 131104 | tf_op jit(solution)/shard_map/ppermute | solution.py:35
  22.6 0.0 copy-done.3
  22.6 0.0 copy-done.4
  22.6 0.0 copy-done.5
  22.6 0.0 copy-start.1
  22.6 0.6 %partial.1.part = f32[256,512]{1,0:T(8,128)S(1)} custom-call(bf16[256,256]{1,0:T(8,128)(2,1)S(1)} %copy-done.5, bf16[256,512]{1,0:T(8,128)(2,1)S(1)} %copy-done, bf16[256,512]{1,0:T(8,128)(2,1)S(1)} %copy-done.3, bf16[256,512]{1,0:T(8,128)(2,1)S(1)} %copy-done.4, bf16[8,256,64]{2,1,0:T(8,128)(2,1)S(1)} %spread.1, ...), custom_call_target="tpu_custom_call" | custom-call | flops 201326592 | bytes 1572864 | tf_op jit(solution)/shard_map/partial/pallas_call | solution.py:295
  23.2 0.0 collective-permute-done.9.refs_1_
  23.2 1.7 %collective-permute-done.10.refs_0_ = bf16[128,512]{1,0:T(8,128)(2,1)S(1)} collective-permute-done((bf16[128,512]{1,0:T(8,128)(2,1)S(1)}, bf16[128,512]{1,0:T(8,128)(2,1)S(1)}, u32[]{:S(2)}, u32[]{:S(2)}) %collective-permute-start.10) | collective-permute-done | bytes 131104 | tf_op jit(solution)/shard_map/ppermute | solution.py:35
  24.9 1.3 %collective-permute-done.12.refs_2_ = bf16[128,512]{1,0:T(8,128)(2,1)S(1)} collective-permute-done((bf16[128,512]{1,0:T(8,128)(2,1)S(1)}, bf16[128,512]{1,0:T(8,128)(2,1)S(1)}, u32[]{:S(2)}, u32[]{:S(2)}) %collective-permute-start.12) | collective-permute-done | bytes 131104 | tf_op jit(solution)/shard_map/ppermute | solution.py:35
  26.2 0.0 copy-done.1
  26.2 0.7 %final_sent.1 = (bf16[64,512]{1,0:T(8,128)(2,1)S(1)}, bf16[64,512]{1,0:T(8,128)(2,1)S(1)}, bf16[64,512]{1,0:T(8,128)(2,1)S(1)}) custom-call(bf16[64,512]{1,0:T(8,128)(2,1)S(1)} %get-tuple-element.50.after.mine.first, f32[256,512]{1,0:T(8,128)S(1)} %partial.1.part, bf16[8,256,64]{2,1,0:T(8,128)(2,1)S(1)} %spread.1, bf16[512,512]{1,0:T(8,128)(2,1)S(1)} %copy-done.1, ...), custom_call_target="tpu_custom_call" | custom-call | flops 100663296 | bytes 1179648 | tf_op jit(solution)/shard_map/final_sent/pallas_call | solution.py:307
  26.8 1.3 %collective-permute-start.13 = (bf16[64,512]{1,0:T(8,128)(2,1)S(1)}, bf16[64,512]{1,0:T(8,128)(2,1)S(1)}, u32[]{:S(2)}, u32[]{:S(2)}) collective-permute-start(bf16[64,512]{1,0:T(8,128)(2,1)S(1)} %get-tuple-element.60.refs_6_), channel_id=1, source_target_pairs={{0,2},{1,3},{2,0},{3,1},{4,6},{5,7},{6,4},{7,5},{8,10},{9,11},{10,... | collective-permute-start | bytes 196616 | tf_op jit(solution)/shard_map/ppermute | solution.py:35
  28.1 0.0 collective-permute-start.14
  28.1 0.9 %collective-permute-start.15 = (bf16[64,512]{1,0:T(8,128)(2,1)S(1)}, bf16[64,512]{1,0:T(8,128)(2,1)S(1)}, u32[]{:S(2)}, u32[]{:S(2)}) collective-permute-start(bf16[64,512]{1,0:T(8,128)(2,1)S(1)} %get-tuple-element.61.refs_7_), channel_id=1, source_target_pairs={{0,3},{1,2},{2,1},{3,0},{4,7},{5,6},{6,5},{7,4},{8,11},{9,10},{10,... | collective-permute-start | bytes 196616 | tf_op jit(solution)/shard_map/ppermute | solution.py:35
  29.0 0.4 %final_kept.1.refs_4_.refs_0_ = bf16[64,512]{1,0:T(8,128)(2,1)S(1)} custom-call(bf16[64,512]{1,0:T(8,128)(2,1)S(1)} %get-tuple-element.59.first.refs_5_, f32[256,512]{1,0:T(8,128)S(1)} %partial.1.part, bf16[8,256,64]{2,1,0:T(8,128)(2,1)S(1)} %spread.1, bf16[512,512]{1,0:T(8,128)(2,1)S(1)} %copy-done.1, bf16[128,512]{1,0:T(8,128)(2,1)S(1)} %collective-permute-done.10.refs_0_, ...), custom_call_target="tpu_custom_call" | custom-call | flops 33554432 | bytes 393216 | tf_op jit(solution)/shard_map/final_kept/pallas_call | solution.py:307
  29.4 1.0 %prepare.1 = (bf16[1024,512]{1,0:T(8,128)(2,1)S(1)}, bf16[1024,256]{1,0:T(8,128)(2,1)S(1)}, bf16[256,512]{1,0:T(8,128)(2,1)}) custom-call(bf16[1024,512]{1,0:T(8,128)(2,1)S(1)} %load.1.history, s32[1,256]{1,0:T(1,128)S(1)} %get-tuple-element.42.refs_0_, s32[1,256]{1,0:T(1,128)S(1)} %collective-permute-done.refs_1_, ...), custom_call_target="tpu_custom_call" | custom-call | flops 2097152 | bytes 3145728 | tf_op jit(solution)/shard_map/prepare/pallas_call | solution.py:323
  30.4 0.9 %collective-permute-done.13.refs_2_ = bf16[64,512]{1,0:T(8,128)(2,1)S(1)} collective-permute-done((bf16[64,512]{1,0:T(8,128)(2,1)S(1)}, bf16[64,512]{1,0:T(8,128)(2,1)S(1)}, u32[]{:S(2)}, u32[]{:S(2)}) %collective-permute-start.13) | collective-permute-done | bytes 65568 | tf_op jit(solution)/shard_map/ppermute | solution.py:35
  31.3 0.0 collective-permute-done.14.refs_1_
  31.3 0.7 %collective-permute-done.15.refs_3_ = bf16[64,512]{1,0:T(8,128)(2,1)S(1)} collective-permute-done((bf16[64,512]{1,0:T(8,128)(2,1)S(1)}, bf16[64,512]{1,0:T(8,128)(2,1)S(1)}, u32[]{:S(2)}, u32[]{:S(2)}) %collective-permute-start.15) | collective-permute-done | bytes 65568 | tf_op jit(solution)/shard_map/ppermute | solution.py:35
  32.0 1.2 %scatter.1 = bf16[1024,512]{1,0:T(8,128)(2,1)} custom-call(bf16[1024,512]{1,0:T(8,128)(2,1)S(1)} %get-tuple-element.63.base, bf16[1024,256]{1,0:T(8,128)(2,1)S(1)} %get-tuple-element.64.hot, bf16[64,512]{1,0:T(8,128)(2,1)S(1)} %final_kept.1.refs_4_.refs_0_, bf16[64,512]{1,0:T(8,128)(2,1)S(1)} %collective-permute-done.14.refs_1_, ...), custom_call_target="tpu_custom_call" | custom-call | tf_op jit(solution)/shard_map/scatter/pallas_call | solution.py:337
  (4 shorter events, 0.0 us)
Async XLA Ops:
  0.6 16.2 %collective-permute-start.5 = (bf16[256,512]{1,0:T(8,128)(2,1)}, bf16[256,512]{1,0:T(8,128)(2,1)S(1)}, u32[]{:S(2)}, u32[]{:S(2)}) collective-permute-start(bf16[256,512]{1,0:T(8,128)(2,1)} %hidden.5), channel_id=1, source_target_pairs={{0,16},{4,20},{8,24},{12,28},{16,0},{20,4},{24,8},{28,12},{1,17},{... | collective-permute-start | bytes 786440 | tf_op jit(solution)/shard_map/ppermute | solution.py:35
  4.7 0.7 %copy-start.10 = (s32[1,4]{1,0:T(1,128)S(1)}, s32[1,4]{1,0:T(1,128)}, u32[]{:S(2)}) copy-start(s32[1,4]{1,0:T(1,128)} %count.1) | copy-start | bytes 52
  4.7 0.7 %copy-start.7 = (s32[1,4,128]{2,1,0:T(4,128)S(1)}, s32[1,4,128]{2,1,0:T(4,128)}, u32[]{:S(2)}) copy-start(s32[1,4,128]{2,1,0:T(4,128)} %rows.1) | copy-start | bytes 6148
  4.8 0.7 %copy-start.8 = (s32[1,4]{1,0:T(1,128)S(1)}, s32[1,4]{1,0:T(1,128)}, u32[]{:S(2)}) copy-start(s32[1,4]{1,0:T(1,128)} %src.3) | copy-start | bytes 52
  4.8 0.7 %copy-start.9 = (s32[256]{0:T(256)S(1)}, s32[256]{0:T(256)}, u32[]{:S(2)}) copy-start(s32[256]{0:T(256)} %param.23) | copy-start | bytes 3076
  5.8 4.7 %collective-permute-start = (s32[1,256]{1,0:T(1,128)S(1)}, s32[1,256]{1,0:T(1,128)S(1)}, u32[]{:S(2)}, u32[]{:S(2)}) collective-permute-start(s32[1,256]{1,0:T(1,128)S(1)} %get-tuple-element.37), channel_id=1, source_target_pairs={{0,1},{1,0},{2,3},{3,2},{4,5},{5,4},{6,7},{7,6},{8,9},{9,8},{10,11... | collective-permute-start | bytes 3080 | tf_op jit(solution)/shard_map/ppermute | solution.py:35
  5.9 7.7 %collective-permute-start.1 = (s32[1,512]{1,0:T(1,128)S(1)}, s32[1,512]{1,0:T(1,128)S(1)}, u32[]{:S(2)}, u32[]{:S(2)}) collective-permute-start(s32[1,512]{1,0:T(1,128)S(1)} %get-tuple-element.47.refs_0_), channel_id=1, source_target_pairs={{0,4},{4,0},{8,12},{12,8},{16,20},{20,16},{24,28},{28,24},{1,5},{5... | collective-permute-start | bytes 6152 | tf_op jit(solution)/shard_map/ppermute | solution.py:35
  7.4 6.1 %collective-permute-start.4 = (s32[1,512]{1,0:T(1,128)S(1)}, s32[1,512]{1,0:T(1,128)S(1)}, u32[]{:S(2)}, u32[]{:S(2)}) collective-permute-start(s32[1,512]{1,0:T(1,128)S(1)} %get-tuple-element.40), channel_id=1, source_target_pairs={{0,8},{4,12},{8,0},{12,4},{16,24},{20,28},{24,16},{28,20},{1,9},{5... | collective-permute-start | bytes 6152 | tf_op jit(solution)/shard_map/ppermute | solution.py:35
  9.0 3.6 %collective-permute-start.2 = (s32[1,256]{1,0:T(1,128)S(1)}, s32[1,256]{1,0:T(1,128)S(1)}, u32[]{:S(2)}, u32[]{:S(2)}) collective-permute-start(s32[1,256]{1,0:T(1,128)S(1)} %get-tuple-element.38), channel_id=1, source_target_pairs={{0,2},{1,3},{2,0},{3,1},{4,6},{5,7},{6,4},{7,5},{8,10},{9,11},{10,... | collective-permute-start | bytes 3080 | tf_op jit(solution)/shard_map/ppermute | solution.py:35
  10.5 3.0 %collective-permute-start.3 = (s32[1,256]{1,0:T(1,128)S(1)}, s32[1,256]{1,0:T(1,128)S(1)}, u32[]{:S(2)}, u32[]{:S(2)}) collective-permute-start(s32[1,256]{1,0:T(1,128)S(1)} %get-tuple-element.39), channel_id=1, source_target_pairs={{0,3},{1,2},{2,1},{3,0},{4,7},{5,6},{6,5},{7,4},{8,11},{9,10},{10,... | collective-permute-start | bytes 3080 | tf_op jit(solution)/shard_map/ppermute | solution.py:35
  10.5 1.2 %copy-start.2 = (bf16[1024,512]{1,0:T(8,128)(2,1)S(1)}, bf16[1024,512]{1,0:T(8,128)(2,1)}, u32[]{:S(2)}) copy-start(bf16[1024,512]{1,0:T(8,128)(2,1)} %history.1) | copy-start | bytes 3145732
  13.5 3.4 %copy-start = (bf16[256,512]{1,0:T(8,128)(2,1)S(1)}, bf16[256,512]{1,0:T(8,128)(2,1)}, u32[]{:S(2)}) copy-start(bf16[256,512]{1,0:T(8,128)(2,1)} %hidden.5) | copy-start | bytes 786436
  14.3 2.5 %collective-permute-start.6 = (bf16[128,512]{1,0:T(8,128)(2,1)S(1)}, bf16[128,512]{1,0:T(8,128)(2,1)S(1)}, u32[]{:S(2)}, u32[]{:S(2)}) collective-permute-start(bf16[128,512]{1,0:T(8,128)(2,1)S(1)} %get-tuple-element.46), channel_id=1, source_target_pairs={{0,1},{1,0},{2,3},{3,2},{4,5},{5,4},{6,7},{7,6},{8,9},{9,8},{10,11... | collective-permute-start | bytes 393224 | tf_op jit(solution)/shard_map/ppermute | solution.py:35
  14.4 7.0 %collective-permute-start.7 = (bf16[128,512]{1,0:T(8,128)(2,1)S(1)}, bf16[128,512]{1,0:T(8,128)(2,1)S(1)}, u32[]{:S(2)}, u32[]{:S(2)}) collective-permute-start(bf16[128,512]{1,0:T(8,128)(2,1)S(1)} %get-tuple-element.52), channel_id=1, source_target_pairs={{0,2},{1,3},{2,0},{3,1},{4,6},{5,7},{6,4},{7,5},{8,10},{9,11},{10,... | collective-permute-start | bytes 393224 | tf_op jit(solution)/shard_map/ppermute | solution.py:35
  15.0 7.6 %collective-permute-start.8 = (bf16[128,512]{1,0:T(8,128)(2,1)S(1)}, bf16[128,512]{1,0:T(8,128)(2,1)S(1)}, u32[]{:S(2)}, u32[]{:S(2)}) collective-permute-start(bf16[128,512]{1,0:T(8,128)(2,1)S(1)} %get-tuple-element.53), channel_id=1, source_target_pairs={{0,3},{1,2},{2,1},{3,0},{4,7},{5,6},{6,5},{7,4},{8,11},{9,10},{10,... | collective-permute-start | bytes 393224 | tf_op jit(solution)/shard_map/ppermute | solution.py:35
  16.2 3.6 %collective-permute-start.11 = (s32[1,512]{1,0:T(1,128)S(1)}, s32[1,512]{1,0:T(1,128)S(1)}, u32[]{:S(2)}, u32[]{:S(2)}) collective-permute-start(s32[1,512]{1,0:T(1,128)S(1)} %collective-permute-done.4.refs_2_), channel_id=1, source_target_pairs={{0,4},{4,0},{8,12},{12,8},{16,20},{20,16},{24,28},{28,24},{1,5},{5... | collective-permute-start | bytes 6152 | tf_op jit(solution)/shard_map/ppermute | solution.py:35
  17.0 6.2 %collective-permute-start.9 = (bf16[128,512]{1,0:T(8,128)(2,1)S(1)}, bf16[128,512]{1,0:T(8,128)(2,1)S(1)}, u32[]{:S(2)}, u32[]{:S(2)}) collective-permute-start(bf16[128,512]{1,0:T(8,128)(2,1)S(1)} %get-tuple-element.54), channel_id=1, source_target_pairs={{0,8},{4,12},{8,0},{12,4},{16,24},{20,28},{24,16},{28,20},{1,9},{5... | collective-permute-start | bytes 393224 | tf_op jit(solution)/shard_map/ppermute | solution.py:35
  17.9 2.8 %copy-start.6 = (bf16[4,64,64]{2,1,0:T(8,128)(2,1)S(1)}, bf16[4,64,64]{2,1,0:T(8,128)(2,1)}, u32[]{:S(2)}) copy-start(bf16[4,64,64]{2,1,0:T(8,128)(2,1)} %tiles.1) | copy-start | bytes 98308
  17.9 7.0 %collective-permute-start.10 = (bf16[128,512]{1,0:T(8,128)(2,1)S(1)}, bf16[128,512]{1,0:T(8,128)(2,1)S(1)}, u32[]{:S(2)}, u32[]{:S(2)}) collective-permute-start(bf16[128,512]{1,0:T(8,128)(2,1)S(1)} %get-tuple-element.55), channel_id=1, source_target_pairs={{0,4},{4,0},{8,12},{12,8},{16,20},{20,16},{24,28},{28,24},{1,5},{5... | collective-permute-start | bytes 393224 | tf_op jit(solution)/shard_map/ppermute | solution.py:35
  19.9 0.8 %copy-start.11 = (s32[1,4]{1,0:T(1,128)S(1)}, s32[1,4]{1,0:T(1,128)}, u32[]{:S(2)}) copy-start(s32[1,4]{1,0:T(1,128)} %dst.1) | copy-start | bytes 52
  19.9 6.3 %collective-permute-start.12 = (bf16[128,512]{1,0:T(8,128)(2,1)S(1)}, bf16[128,512]{1,0:T(8,128)(2,1)S(1)}, u32[]{:S(2)}, u32[]{:S(2)}) collective-permute-start(bf16[128,512]{1,0:T(8,128)(2,1)S(1)} %pick_two_hop.1), channel_id=1, source_target_pairs={{0,12},{4,8},{8,4},{12,0},{16,28},{20,24},{24,20},{28,16},{1,13},{... | collective-permute-start | bytes 393224 | tf_op jit(solution)/shard_map/ppermute | solution.py:35
  20.7 1.9 %copy-start.3 = (bf16[256,512]{1,0:T(8,128)(2,1)S(1)}, bf16[256,512]{1,0:T(8,128)(2,1)}, u32[]{:S(2)}) copy-start(bf16[256,512]{1,0:T(8,128)(2,1)} %pull_adj.1) | copy-start | bytes 786436
  20.7 1.9 %copy-start.4 = (bf16[256,512]{1,0:T(8,128)(2,1)S(1)}, bf16[256,512]{1,0:T(8,128)(2,1)}, u32[]{:S(2)}) copy-start(bf16[256,512]{1,0:T(8,128)(2,1)} %initial.1) | copy-start | bytes 786436
  20.7 1.9 %copy-start.5 = (bf16[256,256]{1,0:T(8,128)(2,1)S(1)}, bf16[256,256]{1,0:T(8,128)(2,1)}, u32[]{:S(2)}) copy-start(bf16[256,256]{1,0:T(8,128)(2,1)} %own_adj.1) | copy-start | bytes 393220
  22.6 3.5 %copy-start.1 = (bf16[512,512]{1,0:T(8,128)(2,1)S(1)}, bf16[512,512]{1,0:T(8,128)(2,1)}, u32[]{:S(2)}) copy-start(bf16[512,512]{1,0:T(8,128)(2,1)} %weight.3) | copy-start | bytes 1572868
  26.8 4.5 %collective-permute-start.13 = (bf16[64,512]{1,0:T(8,128)(2,1)S(1)}, bf16[64,512]{1,0:T(8,128)(2,1)S(1)}, u32[]{:S(2)}, u32[]{:S(2)}) collective-permute-start(bf16[64,512]{1,0:T(8,128)(2,1)S(1)} %get-tuple-element.60.refs_6_), channel_id=1, source_target_pairs={{0,2},{1,3},{2,0},{3,1},{4,6},{5,7},{6,4},{7,5},{8,10},{9,11},{10,... | collective-permute-start | bytes 196616 | tf_op jit(solution)/shard_map/ppermute | solution.py:35
  28.1 3.2 %collective-permute-start.14 = (bf16[64,512]{1,0:T(8,128)(2,1)S(1)}, bf16[64,512]{1,0:T(8,128)(2,1)S(1)}, u32[]{:S(2)}, u32[]{:S(2)}) collective-permute-start(bf16[64,512]{1,0:T(8,128)(2,1)S(1)} %get-tuple-element.59.first.refs_5_), channel_id=1, source_target_pairs={{0,1},{1,0},{2,3},{3,2},{4,5},{5,4},{6,7},{7,6},{8,9},{9,8},{10,11... | collective-permute-start | bytes 196616 | tf_op jit(solution)/shard_map/ppermute | solution.py:35
  28.1 3.9 %collective-permute-start.15 = (bf16[64,512]{1,0:T(8,128)(2,1)S(1)}, bf16[64,512]{1,0:T(8,128)(2,1)S(1)}, u32[]{:S(2)}, u32[]{:S(2)}) collective-permute-start(bf16[64,512]{1,0:T(8,128)(2,1)S(1)} %get-tuple-element.61.refs_7_), channel_id=1, source_target_pairs={{0,3},{1,2},{2,1},{3,0},{4,7},{5,6},{6,5},{7,4},{8,11},{9,10},{10,... | collective-permute-start | bytes 196616 | tf_op jit(solution)/shard_map/ppermute | solution.py:35
